TPU v7x, 256 devices: a whole 4x4x8 slice. The times are simulated.
256 devices in a mesh: ctx: 32 (over x_hi, z, core), head: 8 (over x_lo, y).
Axes of the slice: x: 4 (x_hi: 2, x_lo: 2; x = x_hi * 2 + x_lo), y: 4, z: 8, core: 2. Of those that a mesh axis runs over, the one named last changes fastest.
Arguments:
- queries: bfloat16 [5120, 3072], P('ctx', 'head'), may hold values from -10 to 10
- keys: bfloat16 [5120, 3072], P('ctx', 'head'), may hold values from -6 to 6
- values: bfloat16 [5120, 3072], P('ctx', 'head'), may hold values from -6 to 6
- tan_queries: bfloat16 [5120, 3072], P('ctx', 'head'), may hold values from -6 to 6
- tan_keys: bfloat16 [5120, 3072], P('ctx', 'head'), may hold values from -6 to 6
- tan_values: bfloat16 [5120, 3072], P('ctx', 'head'), may hold values from -6 to 6
- w_out: bfloat16 [3072, 3072], P('head'), may hold values from -0.15625 to 0.15625
Outputs:
- projected: bfloat16 [5120, 3072], P('ctx', 'head')
- projected_tangent: bfloat16 [5120, 3072], P('ctx', 'head')
All inputs are finite; a program needn't handle non-finite values.
Results may differ from a plain program's by a relative error of at most 0.02.
Values may be sent and summed in bfloat16 or wider, within the bound.
No kernel may reach another device: no remote copies, remote signals or barrier semaphores. Data moves between devices by JAX's collectives and lax.ppermute only.
A program may use at most 64 MiB of HBM per device.

v0:
```python
import math

import jax
import jax.numpy as jnp
from jax import lax
from jax.experimental import pallas as pl
from jax.experimental.pallas import tpu as pltpu
from jax.sharding import Mesh, PartitionSpec as P

DH = 128
FACTOR = 1.0 / math.sqrt(DH)
LOG2E = math.log2(math.e)
CTX = (("xh", 2), ("z", 8), ("core", 2))
HEAD = (("xl", 2), ("y", 4))
GROUPS = 8
VMEM_LIMIT = 20 * 1024 * 1024
PARAMS = pltpu.CompilerParams(vmem_limit_bytes=VMEM_LIMIT)

_NT = (((1,), (1,)), ((), ()))


def vmem():
    return pl.BlockSpec(memory_space=pltpu.VMEM)


def call(kernel, name, outs, args, flops=0, transcendentals=0, moves=True):
    moved = sum(x.size * x.dtype.itemsize for x in list(args) + list(outs)) if moves else 0
    return pl.pallas_call(
        kernel,
        in_specs=[vmem()] * len(args),
        out_specs=[vmem()] * len(outs),
        out_shape=list(outs),
        compiler_params=PARAMS,
        cost_estimate=pl.CostEstimate(
            flops=flops, bytes_accessed=moved, transcendentals=transcendentals
        ),
        name=name,
    )(*args)


def shape(rows, columns, dtype=jnp.bfloat16):
    return jax.ShapeDtypeStruct((rows, columns), dtype)


def wide(column):
    return jnp.broadcast_to(column, (column.shape[0], DH))


def tiled(x, columns):
    whole = -(-columns // DH)
    return jnp.concatenate([x] * whole, axis=1)[:, :columns]


def stats_columns(logs, slopes):
    rows = logs[0].shape[0]
    lane = lax.broadcasted_iota(jnp.int32, (rows, DH), 1)
    stats = jnp.zeros((rows, DH), jnp.float32)
    at = 0
    for value in logs + slopes:
        for _ in range(3):
            part = value.astype(jnp.bfloat16).astype(jnp.float32)
            stats = jnp.where(lane == at, part, stats)
            value = value - part
            at += 1
    return stats.astype(jnp.bfloat16)


def stats_of(part, heads):
    row = lax.broadcasted_iota(jnp.int32, (DH, 2 * heads * DH), 0)
    column = lax.broadcasted_iota(jnp.int32, (DH, 2 * heads * DH), 1)
    first = 3 * lax.shift_right_logical(column, DH.bit_length() - 1)
    chosen = ((row >= first) & (row < first + 3)).astype(jnp.bfloat16)
    sums = jnp.dot(part[:, 2 * heads * DH :], chosen, preferred_element_type=jnp.float32)
    columns = [sums[:, at * DH : (at + 1) * DH] for at in range(2 * heads)]
    return columns[:heads], columns[heads:]


def joined(parts, logs, slopes):
    top = logs[0]
    for log in logs[1:]:
        top = jnp.maximum(top, log)
    shares = [jnp.exp(log - top) for log in logs]
    total = sum(shares)
    inverse = 1.0 / total
    shares = [share * inverse for share in shares]
    mean_slope = sum(share * slope for share, slope in zip(shares, slopes))
    primal = sum(share * part[0] for share, part in zip(shares, parts))
    tangent = sum(
        share * (part[1] + (slope - mean_slope) * part[0])
        for share, slope, part in zip(shares, slopes, parts)
    )
    return primal, tangent, top + jnp.log(total), mean_slope


def head_of(part, head):
    both = part[:, 2 * head * DH : 2 * (head + 1) * DH].astype(jnp.float32)
    return both[:, :DH], both[:, DH:]


def attend_head(q_both, k_both, v_both, state):
    s = lax.dot_general(q_both[:, DH:], k_both[:, :DH], _NT, preferred_element_type=jnp.float32)
    slope = lax.dot_general(q_both, k_both, _NT, preferred_element_type=jnp.float32)
    peak = wide(jnp.max(s, axis=1, keepdims=True))
    if state is not None:
        peak = jnp.maximum(peak, state[2])
    weights = jnp.exp2((s - tiled(peak, s.shape[1])) * (FACTOR * LOG2E))
    total = wide(jnp.sum(weights, axis=1, keepdims=True))
    mixed = (weights * slope).astype(jnp.bfloat16)
    sums = jnp.dot(weights.astype(jnp.bfloat16), v_both, preferred_element_type=jnp.float32)
    value_one = jnp.concatenate([v_both[:, :DH], jnp.ones_like(v_both[:, :DH])], axis=1)
    more = jnp.dot(mixed, value_one, preferred_element_type=jnp.float32) * FACTOR
    primal, tangent, slope_total = sums[:, :DH], sums[:, DH:] + more[:, :DH], more[:, DH:]
    if state is not None:
        shrink = jnp.exp2((state[2] - peak) * (FACTOR * LOG2E))
        primal = primal + state[0] * shrink
        tangent = tangent + state[1] * shrink
        total = total + state[3] * shrink
        slope_total = slope_total + state[4] * shrink
    return primal, tangent, peak, total, slope_total


def attend_kernel(q_count, k_count, merge, final, *refs):
    q_refs, k_refs = refs[:q_count], refs[q_count : q_count + k_count]
    earlier = refs[q_count + k_count : 2 * q_count + k_count] if merge else ()
    outs = refs[-q_count:]
    rows, heads = q_refs[0].shape[0], q_refs[0].shape[1] // (2 * DH)
    logs, slopes = [[] for _ in outs], [[] for _ in outs]

    def both(some, head):
        halves = [
            jnp.concatenate([ref[:, at * DH : (at + 1) * DH] for ref in some], axis=0)
            for at in (head, heads + head)
        ]
        return jnp.concatenate(halves, axis=1)

    for head in range(heads):
        k_both, v_both = both(k_refs[0::2], head), both(k_refs[1::2], head)
        for pair in range(0, q_count, 2):
            q_both = both(q_refs[pair : pair + 2], head)
            state = None
            if merge:
                state = [
                    jnp.concatenate(
                        [
                            ref[:, (5 * head + at) * DH : (5 * head + at + 1) * DH]
                            for ref in earlier[pair : pair + 2]
                        ],
                        axis=0,
                    )
                    for at in range(5)
                ]
            found = attend_head(q_both, k_both, v_both, state)
            for half in range(2):
                out = outs[pair + half]
                own = [x[half * rows : (half + 1) * rows] for x in found]
                if final:
                    primal, tangent, peak, total, slope_total = own
                    inverse = 1.0 / total
                    mean_slope = slope_total * inverse
                    primal = primal * inverse
                    tangent = tangent * inverse - mean_slope * primal
                    first = 2 * head * DH
                    out[:, first : first + DH] = primal.astype(out.dtype)
                    out[:, first + DH : first + 2 * DH] = tangent.astype(out.dtype)
                    logs[pair + half].append(peak * FACTOR + jnp.log(total))
                    slopes[pair + half].append(mean_slope)
                else:
                    for at, x in enumerate(own):
                        out[:, (5 * head + at) * DH : (5 * head + at + 1) * DH] = x
    if final:
        for at, out in enumerate(outs):
            out[:, 2 * heads * DH :] = stats_columns(logs[at], slopes[at])


def attend(q_blocks, k_blocks, earlier=None, final=False, hurried=True):
    rows, width = q_blocks[0].shape
    heads = width // (2 * DH)
    keys = sum(block.shape[0] for block in k_blocks) // 2
    merge = earlier is not None
    if final:
        outs = [shape(rows, (2 * heads + 1) * DH)] * len(q_blocks)
    else:
        outs = [shape(rows, 5 * heads * DH, jnp.float32)] * len(q_blocks)
    pairs = len(q_blocks) * rows * keys * heads

    def kernel(*refs):
        attend_kernel(len(q_blocks), len(k_blocks), merge, final, *refs)

    return call(
        kernel,
        "attend",
        outs,
        list(q_blocks) + list(k_blocks) + list(earlier or ()),
        flops=2 * pairs * DH * 8 if hurried else 0,
        transcendentals=pairs if hurried else 0,
        moves=hurried,
    )


def join_parts(refs):
    parts = [ref[...] for ref in refs]
    heads = (parts[0].shape[1] - DH) // (2 * DH)
    stats = [stats_of(part, heads) for part in parts]
    return [
        joined(
            [head_of(part, head) for part in parts],
            [stat[0][head] for stat in stats],
            [stat[1][head] for stat in stats],
        )
        for head in range(heads)
    ]


def join_kernel(a_ref, b_ref, out):
    found = join_parts((a_ref, b_ref))
    for head, (primal, tangent, _, _) in enumerate(found):
        first = 2 * head * DH
        out[:, first : first + DH] = primal.astype(out.dtype)
        out[:, first + DH : first + 2 * DH] = tangent.astype(out.dtype)
    out[:, 2 * len(found) * DH :] = stats_columns([f[2] for f in found], [f[3] for f in found])


def project_kernel(a_ref, b_ref, w_ref, out):
    found = join_parts((a_ref, b_ref))
    attended = jnp.concatenate(
        [
            jnp.concatenate([f[at].astype(jnp.bfloat16) for f in found], axis=1)
            for at in range(2)
        ],
        axis=0,
    )
    columns = out.shape[2]
    for group in range(out.shape[0]):
        out[group] = jnp.dot(
            attended,
            w_ref[:, group * columns : (group + 1) * columns],
            preferred_element_type=jnp.float32,
        ).astype(out.dtype)


def total_kernel(parts_ref, value_ref, tangent_ref):
    total = parts_ref[0].astype(jnp.float32)
    for group in range(1, parts_ref.shape[0]):
        total = total + parts_ref[group].astype(jnp.float32)
    rows = value_ref.shape[0]
    value_ref[...] = total[:rows].astype(value_ref.dtype)
    tangent_ref[...] = total[rows:].astype(tangent_ref.dtype)


SWAP = [(0, 1), (1, 0)]


def along_z(x, step):
    return lax.ppermute(x, "z", [(i, (i + step) % 8) for i in range(8)])


def beside(left, right):
    width = left.shape[1]
    low = jnp.array(-jnp.inf, left.dtype)
    return jnp.maximum(
        lax.pad(left, low, [(0, 0, 0), (0, width, 0)]),
        lax.pad(right, low, [(0, 0, 0), (width, 0, 0)]),
    )


def on_device(queries, keys, values, tan_queries, tan_keys, tan_values, w_out):
    rows, width = queries.shape
    own = [beside(keys, tan_keys), beside(values, tan_values)]
    up, down = [own], [own]

    def hand_on():
        up.append([along_z(x, 1) for x in up[-1]])
        down.append([along_z(x, -1) for x in down[-1]])

    hand_on()
    own_q = beside(tan_queries, queries)
    own_q, up[1][0] = lax.optimization_barrier((own_q, up[1][0]))
    far_q = lax.ppermute(own_q, "xh", SWAP)
    near_q = [own_q, lax.ppermute(own_q, "core", SWAP)]
    away_q = [far_q, lax.ppermute(far_q, "core", SWAP)]

    hand_on()
    up.append([along_z(up[2][0], 1)])
    down.append([along_z(down[2][0], -1)])
    states = attend(near_q + away_q, own + up[1] + down[1])
    up[2][1], states = lax.optimization_barrier((up[2][1], states))
    up[3].append(along_z(up[2][1], 1))
    down[3].append(along_z(down[2][1], -1))
    states = attend(near_q + away_q, up[2] + down[2], states)
    up[3][0], states = lax.optimization_barrier((up[3][0], states))
    last = [along_z(up[3][0], 1), along_z(down[3][1], -1)]
    states = attend(near_q + away_q, up[3] + down[3], states)

    away, away_other = attend(away_q, last, states[2:], True)
    whole = [shape(*away.shape)]
    to_far = call(join_kernel, "join", whole, [away, lax.ppermute(away_other, "core", SWAP)])[0]
    to_far, near_states = lax.optimization_barrier((to_far, states[:2]))
    from_far = lax.ppermute(to_far, "xh", SWAP)
    near, near_other = attend(near_q, last, near_states, True, False)
    near_parts = [near, lax.ppermute(near_other, "core", SWAP)]
    near = call(join_kernel, "join", whole, near_parts, moves=False)[0]
    parts = call(
        project_kernel,
        "project",
        [jax.ShapeDtypeStruct((GROUPS, 2 * rows, w_out.shape[1] // GROUPS), jnp.bfloat16)],
        [near, from_far, w_out],
        flops=4 * rows * w_out.shape[0] * w_out.shape[1],
    )[0]
    parts = lax.all_to_all(parts, ("xl", "y"), 0, 0)
    return tuple(call(total_kernel, "total", [shape(rows, width)] * 2, [parts]))


def solution(mesh):
    fine = Mesh(
        mesh.devices.reshape([size for _, size in CTX + HEAD]), [name for name, _ in CTX + HEAD]
    )
    ctx, head = tuple(name for name, _ in CTX), tuple(name for name, _ in HEAD)
    split = P(ctx, head)
    return jax.shard_map(
        on_device,
        mesh=fine,
        in_specs=(split,) * 6 + (P(head, None),),
        out_specs=(split, split),
        check_vma=False,
    )
```

profile of v0, /device:TPU:98, one launch (start us, length us, event | category | flops | bytes accessed | tf_op | source)
XLA Modules:
  0.0 99.7 jit_solution(16707781974919909212)
XLA Ops:
  0.6 1.0 pad_maximum_fusion.1.refs_4_
  1.6 3.2 %collective-permute-start = (bf16[160,768]{1,0:T(8,128)(2,1)S(1)}, bf16[160,768]{1,0:T(8,128)(2,1)S(1)}, u32[]{:S(2)}, u32[]{:S(2)}) collective-permute-start(bf16[160,768]{1,0:T(8,128)(2,1)S(1)} %pad_maximum_fusion.1.refs_4_), channel_id=1, source_target_pairs={{0,16},{16,32},{32,48},{48,64},{64,80},{80,96},{96,112},{112,0},{1... | collective-permute-start | bytes 737288 | tf_op jit(solution)/shard_map/ppermute | solution.py:254
  5.8 3.3 %collective-permute-start.6 = (bf16[160,768]{1,0:T(8,128)(2,1)S(1)}, bf16[160,768]{1,0:T(8,128)(2,1)S(1)}, u32[]{:S(2)}, u32[]{:S(2)}) collective-permute-start(bf16[160,768]{1,0:T(8,128)(2,1)S(1)} %pad_maximum_fusion.refs_5_), channel_id=1, source_target_pairs={{0,16},{16,32},{32,48},{48,64},{64,80},{80,96},{96,112},{112,0},{1... | collective-permute-start | bytes 737288 | tf_op jit(solution)/shard_map/ppermute | solution.py:254
  10.1 1.1 %collective-permute-done.refs_6_ = bf16[160,768]{1,0:T(8,128)(2,1)S(1)} collective-permute-done((bf16[160,768]{1,0:T(8,128)(2,1)S(1)}, bf16[160,768]{1,0:T(8,128)(2,1)S(1)}, u32[]{:S(2)}, u32[]{:S(2)}) %collective-permute-start) | collective-permute-done | bytes 245792 | tf_op jit(solution)/shard_map/ppermute | solution.py:254
  11.2 2.1 %collective-permute-start.4 = (bf16[160,768]{1,0:T(8,128)(2,1)S(1)}, bf16[160,768]{1,0:T(8,128)(2,1)S(1)}, u32[]{:S(2)}, u32[]{:S(2)}) collective-permute-start(bf16[160,768]{1,0:T(8,128)(2,1)S(1)} %pad_maximum_fusion.2.refs_0_), channel_id=1, source_target_pairs={{0,128},{128,0},{1,129},{129,1},{2,130},{130,2},{3,131},{131,3},{4... | collective-permute-start | bytes 737288 | tf_op jit(solution)/shard_map/ppermute | solution.py:278
  13.3 2.0 %collective-permute-done.6.refs_7_ = bf16[160,768]{1,0:T(8,128)(2,1)S(1)} collective-permute-done((bf16[160,768]{1,0:T(8,128)(2,1)S(1)}, bf16[160,768]{1,0:T(8,128)(2,1)S(1)}, u32[]{:S(2)}, u32[]{:S(2)}) %collective-permute-start.6) | collective-permute-done | bytes 245792 | tf_op jit(solution)/shard_map/ppermute | solution.py:254
  15.3 3.7 %collective-permute-start.2 = (bf16[160,768]{1,0:T(8,128)(2,1)S(1)}, bf16[160,768]{1,0:T(8,128)(2,1)S(1)}, u32[]{:S(2)}, u32[]{:S(2)}) collective-permute-start(bf16[160,768]{1,0:T(8,128)(2,1)S(1)} %collective-permute-done.refs_6_), channel_id=1, source_target_pairs={{0,16},{16,32},{32,48},{48,64},{64,80},{80,96},{96,112},{112,0},{1... | collective-permute-start | bytes 737288 | tf_op jit(solution)/shard_map/ppermute | solution.py:254
  19.2 3.4 %collective-permute-start.7 = (bf16[160,768]{1,0:T(8,128)(2,1)S(1)}, bf16[160,768]{1,0:T(8,128)(2,1)S(1)}, u32[]{:S(2)}, u32[]{:S(2)}) collective-permute-start(bf16[160,768]{1,0:T(8,128)(2,1)S(1)} %collective-permute-done.6.refs_7_), channel_id=1, source_target_pairs={{0,16},{16,32},{32,48},{48,64},{64,80},{80,96},{96,112},{112,0},{1... | collective-permute-start | bytes 737288 | tf_op jit(solution)/shard_map/ppermute | solution.py:254
  23.3 3.8 %collective-permute-start.3 = (bf16[160,768]{1,0:T(8,128)(2,1)S(1)}, bf16[160,768]{1,0:T(8,128)(2,1)S(1)}, u32[]{:S(2)}, u32[]{:S(2)}) collective-permute-start(bf16[160,768]{1,0:T(8,128)(2,1)S(1)} %collective-permute-done.2.refs_4_), channel_id=1, source_target_pairs={{0,16},{16,32},{32,48},{48,64},{64,80},{80,96},{96,112},{112,0},{1... | collective-permute-start | bytes 737288 | tf_op jit(solution)/shard_map/ppermute | solution.py:254
  27.1 2.0 %collective-permute-done.11.refs_7_ = bf16[160,768]{1,0:T(8,128)(2,1)S(1)} collective-permute-done((bf16[160,768]{1,0:T(8,128)(2,1)S(1)}, bf16[160,768]{1,0:T(8,128)(2,1)S(1)}, u32[]{:S(2)}, u32[]{:S(2)}) %collective-permute-start.11) | collective-permute-done | bytes 245792 | tf_op jit(solution)/shard_map/ppermute | solution.py:254
  29.1 5.3 %collective-permute-done.10.refs_6_ = bf16[160,768]{1,0:T(8,128)(2,1)S(1)} collective-permute-done((bf16[160,768]{1,0:T(8,128)(2,1)S(1)}, bf16[160,768]{1,0:T(8,128)(2,1)S(1)}, u32[]{:S(2)}, u32[]{:S(2)}) %collective-permute-start.10) | collective-permute-done | bytes 245792 | tf_op jit(solution)/shard_map/ppermute | solution.py:254
  34.4 2.7 %attend.5 = (f32[160,1920]{1,0:T(8,128)S(1)}, f32[160,1920]{1,0:T(8,128)S(1)}, f32[160,1920]{1,0:T(8,128)S(1)}, f32[160,1920]{1,0:T(8,128)S(1)}) custom-call(bf16[160,768]{1,0:T(8,128)(2,1)S(1)} %pad_maximum_fusion.2.refs_0_, bf16[160,768]{1,0:T(8,128)(2,1)S(1)} %collective-permute-done.1.refs_1_, ...), custom_call_target="tpu_custom_call" | custom-call | flops 1887436800 | bytes 7372800 | tf_op jit(solution)/shard_map/attend/pallas_call | solution.py:28
  37.1 3.3 %collective-permute-start.15 = (bf16[160,768]{1,0:T(8,128)(2,1)S(1)}, bf16[160,768]{1,0:T(8,128)(2,1)S(1)}, u32[]{:S(2)}, u32[]{:S(2)}) collective-permute-start(bf16[160,768]{1,0:T(8,128)(2,1)S(1)} %collective-permute-done.7.refs_5_), channel_id=1, source_target_pairs={{0,16},{16,32},{32,48},{48,64},{64,80},{80,96},{96,112},{112,0},{1... | collective-permute-start | bytes 737288 | tf_op jit(solution)/shard_map/ppermute | solution.py:254
  40.4 2.7 %attend.6 = (f32[160,1920]{1,0:T(8,128)S(1)}, f32[160,1920]{1,0:T(8,128)S(1)}, f32[160,1920]{1,0:T(8,128)S(1)}, f32[160,1920]{1,0:T(8,128)S(1)}) custom-call(bf16[160,768]{1,0:T(8,128)(2,1)S(1)} %pad_maximum_fusion.2.refs_0_, bf16[160,768]{1,0:T(8,128)(2,1)S(1)} %collective-permute-done.1.refs_1_, ...), custom_call_target="tpu_custom_call" | custom-call | flops 1258291200 | bytes 11796480 | tf_op jit(solution)/shard_map/attend/pallas_call | solution.py:28
  43.1 2.0 %collective-permute-start.14 = (bf16[160,768]{1,0:T(8,128)(2,1)S(1)}, bf16[160,768]{1,0:T(8,128)(2,1)S(1)}, u32[]{:S(2)}, u32[]{:S(2)}) collective-permute-start(bf16[160,768]{1,0:T(8,128)(2,1)S(1)} %collective-permute-done.13.refs_7_), channel_id=1, source_target_pairs={{0,112},{16,0},{32,16},{48,32},{64,48},{80,64},{96,80},{112,96},{1... | collective-permute-start | bytes 737288 | tf_op jit(solution)/shard_map/ppermute | solution.py:254
  45.8 2.7 %attend.7 = (f32[160,1920]{1,0:T(8,128)S(1)}, f32[160,1920]{1,0:T(8,128)S(1)}, f32[160,1920]{1,0:T(8,128)S(1)}, f32[160,1920]{1,0:T(8,128)S(1)}) custom-call(bf16[160,768]{1,0:T(8,128)(2,1)S(1)} %pad_maximum_fusion.2.refs_0_, bf16[160,768]{1,0:T(8,128)(2,1)S(1)} %collective-permute-done.1.refs_1_, ...), custom_call_target="tpu_custom_call" | custom-call | flops 1258291200 | bytes 11796480 | tf_op jit(solution)/shard_map/attend/pallas_call | solution.py:28
  49.3 1.3 %collective-permute-done.14.refs_3_ = bf16[160,768]{1,0:T(8,128)(2,1)S(1)} collective-permute-done((bf16[160,768]{1,0:T(8,128)(2,1)S(1)}, bf16[160,768]{1,0:T(8,128)(2,1)S(1)}, u32[]{:S(2)}, u32[]{:S(2)}) %collective-permute-start.14) | collective-permute-done | bytes 245792 | tf_op jit(solution)/shard_map/ppermute | solution.py:254
  50.6 1.6 %attend.8 = (bf16[160,896]{1,0:T(8,128)(2,1)S(1)}, bf16[160,896]{1,0:T(8,128)(2,1)S(1)}) custom-call(bf16[160,768]{1,0:T(8,128)(2,1)S(1)} %collective-permute-done.4.refs_2_.refs_0_, bf16[160,768]{1,0:T(8,128)(2,1)S(1)} %collective-permute-done.5.refs_3_.refs_1_, bf16[160,768]{1,0:T(8,128)(2,1)S(1)} %collective-permute-done.12.refs_2_, ...), custom_call_target="tpu_custom_call" | custom-call | flops 314572800 | bytes 4014080 | tf_op jit(solution)/shard_map/attend/pallas_call | solution.py:28
  52.6 1.6 %collective-permute-done.17.b_ref = bf16[160,896]{1,0:T(8,128)(2,1)S(1)} collective-permute-done((bf16[160,896]{1,0:T(8,128)(2,1)S(1)}, bf16[160,896]{1,0:T(8,128)(2,1)S(1)}, u32[]{:S(2)}, u32[]{:S(2)}) %collective-permute-start.17) | collective-permute-done | bytes 286752 | tf_op jit(solution)/shard_map/ppermute | solution.py:296
  54.8 1.6 %attend.9 = (bf16[160,896]{1,0:T(8,128)(2,1)S(1)}, bf16[160,896]{1,0:T(8,128)(2,1)S(1)}) custom-call(bf16[160,768]{1,0:T(8,128)(2,1)S(1)} %pad_maximum_fusion.2.refs_0_, bf16[160,768]{1,0:T(8,128)(2,1)S(1)} %collective-permute-done.1.refs_1_, bf16[160,768]{1,0:T(8,128)(2,1)S(1)} %collective-permute-done.12.refs_2_, ...), custom_call_target="tpu_custom_call" | custom-call | tf_op jit(solution)/shard_map/attend/pallas_call | solution.py:28
  56.7 2.1 %collective-permute-start.19 = (bf16[160,896]{1,0:T(8,128)(2,1)S(1)}, bf16[160,896]{1,0:T(8,128)(2,1)S(1)}, u32[]{:S(2)}, u32[]{:S(2)}) collective-permute-start(bf16[160,896]{1,0:T(8,128)(2,1)S(1)} %join.2), channel_id=1, source_target_pairs={{0,128},{128,0},{1,129},{129,1},{2,130},{130,2},{3,131},{131,3},{4... | collective-permute-start | bytes 860168 | tf_op jit(solution)/shard_map/ppermute | solution.py:298
  59.6 7.7 %collective-permute-done.19.b_ref = bf16[160,896]{1,0:T(8,128)(2,1)S(1)} collective-permute-done((bf16[160,896]{1,0:T(8,128)(2,1)S(1)}, bf16[160,896]{1,0:T(8,128)(2,1)S(1)}, u32[]{:S(2)}, u32[]{:S(2)}) %collective-permute-start.19) | collective-permute-done | bytes 286752 | tf_op jit(solution)/shard_map/ppermute | solution.py:298
  67.3 1.8 %project.1 = bf16[8,320,384]{2,1,0:T(8,128)(2,1)S(1)} custom-call(bf16[160,896]{1,0:T(8,128)(2,1)S(1)} %join.3.a_ref, bf16[160,896]{1,0:T(8,128)(2,1)S(1)} %collective-permute-done.19.b_ref, bf16[384,3072]{1,0:T(8,128)(2,1)S(1)} %copy-done), custom_call_target="tpu_custom_call" | custom-call | flops 754974720 | bytes 4898816 | tf_op jit(solution)/shard_map/project/pallas_call | solution.py:28
  69.1 29.6 %all_to_all.5.parts_ref = bf16[8,320,384]{2,1,0:T(8,128)(2,1)S(1)} all-to-all(bf16[8,320,384]{2,1,0:T(8,128)(2,1)S(1)} %project.1), channel_id=1, replica_groups=mesh['xh'=2,'z'=8,'core'=2,'xl'=2,'y'=4] {'xl','y'}, dimensions={0} | all-to-all | bytes 3932160 | tf_op jit(solution)/shard_map/all_to_all | solution.py:309
  (31 shorter events, 7.4 us)
Async XLA Ops:
  1.6 9.6 %collective-permute-start = (bf16[160,768]{1,0:T(8,128)(2,1)S(1)}, bf16[160,768]{1,0:T(8,128)(2,1)S(1)}, u32[]{:S(2)}, u32[]{:S(2)}) collective-permute-start(bf16[160,768]{1,0:T(8,128)(2,1)S(1)} %pad_maximum_fusion.1.refs_4_), channel_id=1, source_target_pairs={{0,16},{16,32},{32,48},{48,64},{64,80},{80,96},{96,112},{112,0},{1... | collective-permute-start | bytes 737288 | tf_op jit(solution)/shard_map/ppermute | solution.py:254
  4.8 14.2 %collective-permute-start.8 = (bf16[160,768]{1,0:T(8,128)(2,1)S(1)}, bf16[160,768]{1,0:T(8,128)(2,1)S(1)}, u32[]{:S(2)}, u32[]{:S(2)}) collective-permute-start(bf16[160,768]{1,0:T(8,128)(2,1)S(1)} %pad_maximum_fusion.1.refs_4_), channel_id=1, source_target_pairs={{0,112},{16,0},{32,16},{48,32},{64,48},{80,64},{96,80},{112,96},{1... | collective-permute-start | bytes 737288 | tf_op jit(solution)/shard_map/ppermute | solution.py:254
  5.8 9.5 %collective-permute-start.6 = (bf16[160,768]{1,0:T(8,128)(2,1)S(1)}, bf16[160,768]{1,0:T(8,128)(2,1)S(1)}, u32[]{:S(2)}, u32[]{:S(2)}) collective-permute-start(bf16[160,768]{1,0:T(8,128)(2,1)S(1)} %pad_maximum_fusion.refs_5_), channel_id=1, source_target_pairs={{0,16},{16,32},{32,48},{48,64},{64,80},{80,96},{96,112},{112,0},{1... | collective-permute-start | bytes 737288 | tf_op jit(solution)/shard_map/ppermute | solution.py:254
  9.1 9.9 %collective-permute-start.9 = (bf16[160,768]{1,0:T(8,128)(2,1)S(1)}, bf16[160,768]{1,0:T(8,128)(2,1)S(1)}, u32[]{:S(2)}, u32[]{:S(2)}) collective-permute-start(bf16[160,768]{1,0:T(8,128)(2,1)S(1)} %pad_maximum_fusion.refs_5_), channel_id=1, source_target_pairs={{0,112},{16,0},{32,16},{48,32},{64,48},{80,64},{96,80},{112,96},{1... | collective-permute-start | bytes 737288 | tf_op jit(solution)/shard_map/ppermute | solution.py:254
  11.2 7.9 %collective-permute-start.4 = (bf16[160,768]{1,0:T(8,128)(2,1)S(1)}, bf16[160,768]{1,0:T(8,128)(2,1)S(1)}, u32[]{:S(2)}, u32[]{:S(2)}) collective-permute-start(bf16[160,768]{1,0:T(8,128)(2,1)S(1)} %pad_maximum_fusion.2.refs_0_), channel_id=1, source_target_pairs={{0,128},{128,0},{1,129},{129,1},{2,130},{130,2},{3,131},{131,3},{4... | collective-permute-start | bytes 737288 | tf_op jit(solution)/shard_map/ppermute | solution.py:278
  13.3 5.9 %collective-permute-start.1 = (bf16[160,768]{1,0:T(8,128)(2,1)S(1)}, bf16[160,768]{1,0:T(8,128)(2,1)S(1)}, u32[]{:S(2)}, u32[]{:S(2)}) collective-permute-start(bf16[160,768]{1,0:T(8,128)(2,1)S(1)} %pad_maximum_fusion.2.refs_0_), channel_id=1, source_target_pairs={{0,8},{8,0},{1,9},{9,1},{2,10},{10,2},{3,11},{11,3},{4,12},{12,4},... | collective-permute-start | bytes 737288 | tf_op jit(solution)/shard_map/ppermute | solution.py:279
  15.3 8.0 %collective-permute-start.2 = (bf16[160,768]{1,0:T(8,128)(2,1)S(1)}, bf16[160,768]{1,0:T(8,128)(2,1)S(1)}, u32[]{:S(2)}, u32[]{:S(2)}) collective-permute-start(bf16[160,768]{1,0:T(8,128)(2,1)S(1)} %collective-permute-done.refs_6_), channel_id=1, source_target_pairs={{0,16},{16,32},{32,48},{48,64},{64,80},{80,96},{96,112},{112,0},{1... | collective-permute-start | bytes 737288 | tf_op jit(solution)/shard_map/ppermute | solution.py:254
  19.0 10.1 %collective-permute-start.11 = (bf16[160,768]{1,0:T(8,128)(2,1)S(1)}, bf16[160,768]{1,0:T(8,128)(2,1)S(1)}, u32[]{:S(2)}, u32[]{:S(2)}) collective-permute-start(bf16[160,768]{1,0:T(8,128)(2,1)S(1)} %collective-permute-done.9.refs_9_), channel_id=1, source_target_pairs={{0,112},{16,0},{32,16},{48,32},{64,48},{80,64},{96,80},{112,96},{1... | collective-permute-start | bytes 737288 | tf_op jit(solution)/shard_map/ppermute | solution.py:254
  19.0 15.4 %collective-permute-start.10 = (bf16[160,768]{1,0:T(8,128)(2,1)S(1)}, bf16[160,768]{1,0:T(8,128)(2,1)S(1)}, u32[]{:S(2)}, u32[]{:S(2)}) collective-permute-start(bf16[160,768]{1,0:T(8,128)(2,1)S(1)} %collective-permute-done.8.refs_8_), channel_id=1, source_target_pairs={{0,112},{16,0},{32,16},{48,32},{64,48},{80,64},{96,80},{112,96},{1... | collective-permute-start | bytes 737288 | tf_op jit(solution)/shard_map/ppermute | solution.py:254
  19.1 15.3 %collective-permute-start.5 = (bf16[160,768]{1,0:T(8,128)(2,1)S(1)}, bf16[160,768]{1,0:T(8,128)(2,1)S(1)}, u32[]{:S(2)}, u32[]{:S(2)}) collective-permute-start(bf16[160,768]{1,0:T(8,128)(2,1)S(1)} %collective-permute-done.4.refs_2_.refs_0_), channel_id=1, source_target_pairs={{0,8},{8,0},{1,9},{9,1},{2,10},{10,2},{3,11},{11,3},{4,12},{12,4},... | collective-permute-start | bytes 737288 | tf_op jit(solution)/shard_map/ppermute | solution.py:280
  19.2 17.8 %collective-permute-start.7 = (bf16[160,768]{1,0:T(8,128)(2,1)S(1)}, bf16[160,768]{1,0:T(8,128)(2,1)S(1)}, u32[]{:S(2)}, u32[]{:S(2)}) collective-permute-start(bf16[160,768]{1,0:T(8,128)(2,1)S(1)} %collective-permute-done.6.refs_7_), channel_id=1, source_target_pairs={{0,16},{16,32},{32,48},{48,64},{64,80},{80,96},{96,112},{112,0},{1... | collective-permute-start | bytes 737288 | tf_op jit(solution)/shard_map/ppermute | solution.py:254
  23.3 19.7 %collective-permute-start.3 = (bf16[160,768]{1,0:T(8,128)(2,1)S(1)}, bf16[160,768]{1,0:T(8,128)(2,1)S(1)}, u32[]{:S(2)}, u32[]{:S(2)}) collective-permute-start(bf16[160,768]{1,0:T(8,128)(2,1)S(1)} %collective-permute-done.2.refs_4_), channel_id=1, source_target_pairs={{0,16},{16,32},{32,48},{48,64},{64,80},{80,96},{96,112},{112,0},{1... | collective-permute-start | bytes 737288 | tf_op jit(solution)/shard_map/ppermute | solution.py:254
  29.1 14.0 %collective-permute-start.13 = (bf16[160,768]{1,0:T(8,128)(2,1)S(1)}, bf16[160,768]{1,0:T(8,128)(2,1)S(1)}, u32[]{:S(2)}, u32[]{:S(2)}) collective-permute-start(bf16[160,768]{1,0:T(8,128)(2,1)S(1)} %collective-permute-done.11.refs_7_), channel_id=1, source_target_pairs={{0,112},{16,0},{32,16},{48,32},{64,48},{80,64},{96,80},{112,96},{1... | collective-permute-start | bytes 737288 | tf_op jit(solution)/shard_map/ppermute | solution.py:254
  34.4 10.8 %collective-permute-start.16 = (bf16[160,768]{1,0:T(8,128)(2,1)S(1)}, bf16[160,768]{1,0:T(8,128)(2,1)S(1)}, u32[]{:S(2)}, u32[]{:S(2)}) collective-permute-start(bf16[160,768]{1,0:T(8,128)(2,1)S(1)} %collective-permute-done.10.refs_6_), channel_id=1, source_target_pairs={{0,112},{16,0},{32,16},{48,32},{64,48},{80,64},{96,80},{112,96},{1... | collective-permute-start | bytes 737288 | tf_op jit(solution)/shard_map/ppermute | solution.py:254
  37.1 8.8 %collective-permute-start.15 = (bf16[160,768]{1,0:T(8,128)(2,1)S(1)}, bf16[160,768]{1,0:T(8,128)(2,1)S(1)}, u32[]{:S(2)}, u32[]{:S(2)}) collective-permute-start(bf16[160,768]{1,0:T(8,128)(2,1)S(1)} %collective-permute-done.7.refs_5_), channel_id=1, source_target_pairs={{0,16},{16,32},{32,48},{48,64},{64,80},{80,96},{96,112},{112,0},{1... | collective-permute-start | bytes 737288 | tf_op jit(solution)/shard_map/ppermute | solution.py:254
  43.0 6.3 %collective-permute-start.12 = (bf16[160,768]{1,0:T(8,128)(2,1)S(1)}, bf16[160,768]{1,0:T(8,128)(2,1)S(1)}, u32[]{:S(2)}, u32[]{:S(2)}) collective-permute-start(bf16[160,768]{1,0:T(8,128)(2,1)S(1)} %collective-permute-done.3.refs_4_), channel_id=1, source_target_pairs={{0,16},{16,32},{32,48},{48,64},{64,80},{80,96},{96,112},{112,0},{1... | collective-permute-start | bytes 737288 | tf_op jit(solution)/shard_map/ppermute | solution.py:254
  43.1 7.5 %collective-permute-start.14 = (bf16[160,768]{1,0:T(8,128)(2,1)S(1)}, bf16[160,768]{1,0:T(8,128)(2,1)S(1)}, u32[]{:S(2)}, u32[]{:S(2)}) collective-permute-start(bf16[160,768]{1,0:T(8,128)(2,1)S(1)} %collective-permute-done.13.refs_7_), channel_id=1, source_target_pairs={{0,112},{16,0},{32,16},{48,32},{64,48},{80,64},{96,80},{112,96},{1... | collective-permute-start | bytes 737288 | tf_op jit(solution)/shard_map/ppermute | solution.py:254
  52.2 1.9 %collective-permute-start.17 = (bf16[160,896]{1,0:T(8,128)(2,1)S(1)}, bf16[160,896]{1,0:T(8,128)(2,1)S(1)}, u32[]{:S(2)}, u32[]{:S(2)}) collective-permute-start(bf16[160,896]{1,0:T(8,128)(2,1)S(1)} %get-tuple-element.56), channel_id=1, source_target_pairs={{0,8},{8,0},{1,9},{9,1},{2,10},{10,2},{3,11},{11,3},{4,12},{12,4},... | collective-permute-start | bytes 860168 | tf_op jit(solution)/shard_map/ppermute | solution.py:296
  54.8 12.5 %copy-start = (bf16[384,3072]{1,0:T(8,128)(2,1)S(1)}, bf16[384,3072]{1,0:T(8,128)(2,1)}, u32[]{:S(2)}) copy-start(bf16[384,3072]{1,0:T(8,128)(2,1)} %w_ref.1) | copy-start | bytes 7077892
  56.5 2.4 %collective-permute-start.18 = (bf16[160,896]{1,0:T(8,128)(2,1)S(1)}, bf16[160,896]{1,0:T(8,128)(2,1)S(1)}, u32[]{:S(2)}, u32[]{:S(2)}) collective-permute-start(bf16[160,896]{1,0:T(8,128)(2,1)S(1)} %get-tuple-element.62), channel_id=1, source_target_pairs={{0,8},{8,0},{1,9},{9,1},{2,10},{10,2},{3,11},{11,3},{4,12},{12,4},... | collective-permute-start | bytes 860168 | tf_op jit(solution)/shard_map/ppermute | solution.py:300
  56.7 10.6 %collective-permute-start.19 = (bf16[160,896]{1,0:T(8,128)(2,1)S(1)}, bf16[160,896]{1,0:T(8,128)(2,1)S(1)}, u32[]{:S(2)}, u32[]{:S(2)}) collective-permute-start(bf16[160,896]{1,0:T(8,128)(2,1)S(1)} %join.2), channel_id=1, source_target_pairs={{0,128},{128,0},{1,129},{129,1},{2,130},{130,2},{3,131},{131,3},{4... | collective-permute-start | bytes 860168 | tf_op jit(solution)/shard_map/ppermute | solution.py:298
where the time goes:
time: 101 us; the launch traced here: 99.7 us
  blocking collectives  29.6 us (29%)
  starting transfers between devices  27.7 us (27%)
  waiting for transfers between devices  23.2 us (23%)
  Pallas kernels  15.3 us (15%)
  other arithmetic  2.95 us (3%)
    all_to_all x1, blocking collectives, on_device(): parts = lax.all_to_all(parts, ('xl', 'y'), 0, 0)  29.6 us
    ppermute x14, starting transfers between devices, along_z(): return lax.ppermute(x, 'z', [(i, (i + step) % 8) for i in range(8)])  22.8 us
    pallas_call x9, Pallas kernels, call(): pl.pallas_call(kernel, in_specs=[vmem()] * len(args), out_specs=[vmem()]...  15.3 us
    ppermute x14, waiting for transfers between devices, along_z(): return lax.ppermute(x, 'z', [(i, (i + step) % 8) for i in range(8)])  13.9 us
    ppermute x1, waiting for transfers between devices, on_device(): from_far = lax.ppermute(to_far, 'xh', SWAP)  7.75 us
    max x3, other arithmetic, beside(): jnp.maximum(lax.pad(left, low, [(0, 0, 0), (0, width, 0)]), lax.pad(right...  2.95 us
    ppermute x1, starting transfers between devices, on_device(): from_far = lax.ppermute(to_far, 'xh', SWAP)  2.15 us
    ppermute x1, starting transfers between devices, on_device(): far_q = lax.ppermute(own_q, 'xh', SWAP)  2.12 us
  transfers between devices with their start and end apart: 20, of which 10 were waited for; matrix products, arithmetic and copies ran while one was open for 2% of the time, Pallas kernels for 9%

commit v1 on v0

--- a/solution.py
+++ b/solution.py
@@ -23,8 +23,8 @@
     return pl.BlockSpec(memory_space=pltpu.VMEM)
 
 
-def call(kernel, name, outs, args, flops=0, transcendentals=0, moves=True):
-    moved = sum(x.size * x.dtype.itemsize for x in list(args) + list(outs)) if moves else 0
+def call(kernel, name, outs, args, flops=0, transcendentals=0):
+    moved = sum(x.size * x.dtype.itemsize for x in list(args) + list(outs))
     return pl.pallas_call(
         kernel,
         in_specs=[vmem()] * len(args),
@@ -52,17 +52,18 @@
 
 
 def stats_columns(logs, slopes):
-    rows = logs[0].shape[0]
-    lane = lax.broadcasted_iota(jnp.int32, (rows, DH), 1)
-    stats = jnp.zeros((rows, DH), jnp.float32)
-    at = 0
-    for value in logs + slopes:
-        for _ in range(3):
-            part = value.astype(jnp.bfloat16).astype(jnp.float32)
-            stats = jnp.where(lane == at, part, stats)
-            value = value - part
-            at += 1
-    return stats.astype(jnp.bfloat16)
+    lane = lax.broadcasted_iota(jnp.int32, logs[0].shape, 1)
+    stats = jnp.zeros(logs[0].shape, jnp.float32)
+    third = jnp.zeros(logs[0].shape, jnp.int32)
+    for at, value in enumerate(logs + slopes):
+        stats = jnp.where(lane >= 3 * at, value, stats)
+        third = jnp.where(lane >= 3 * at, 3 * at, third)
+    third = lane - third
+    high = stats.astype(jnp.bfloat16).astype(jnp.float32)
+    rest = stats - high
+    middle = rest.astype(jnp.bfloat16).astype(jnp.float32)
+    kept = jnp.where(third == 0, high, jnp.where(third == 1, middle, rest - middle))
+    return jnp.where(third < 3, kept, 0.0).astype(jnp.bfloat16)
 
 
 def stats_of(part, heads):
@@ -123,7 +124,7 @@
     q_refs, k_refs = refs[:q_count], refs[q_count : q_count + k_count]
     earlier = refs[q_count + k_count : 2 * q_count + k_count] if merge else ()
     outs = refs[-q_count:]
-    rows, heads = q_refs[0].shape[0], q_refs[0].shape[1] // (2 * DH)
+    heads = q_refs[0].shape[1] // (2 * DH)
     logs, slopes = [[] for _ in outs], [[] for _ in outs]
 
     def both(some, head):
@@ -135,70 +136,58 @@
 
     for head in range(heads):
         k_both, v_both = both(k_refs[0::2], head), both(k_refs[1::2], head)
-        for pair in range(0, q_count, 2):
-            q_both = both(q_refs[pair : pair + 2], head)
+        for stack, out in enumerate(outs):
             state = None
             if merge:
                 state = [
-                    jnp.concatenate(
-                        [
-                            ref[:, (5 * head + at) * DH : (5 * head + at + 1) * DH]
-                            for ref in earlier[pair : pair + 2]
-                        ],
-                        axis=0,
-                    )
+                    earlier[stack][:, (5 * head + at) * DH : (5 * head + at + 1) * DH]
                     for at in range(5)
                 ]
-            found = attend_head(q_both, k_both, v_both, state)
-            for half in range(2):
-                out = outs[pair + half]
-                own = [x[half * rows : (half + 1) * rows] for x in found]
-                if final:
-                    primal, tangent, peak, total, slope_total = own
-                    inverse = 1.0 / total
-                    mean_slope = slope_total * inverse
-                    primal = primal * inverse
-                    tangent = tangent * inverse - mean_slope * primal
-                    first = 2 * head * DH
-                    out[:, first : first + DH] = primal.astype(out.dtype)
-                    out[:, first + DH : first + 2 * DH] = tangent.astype(out.dtype)
-                    logs[pair + half].append(peak * FACTOR + jnp.log(total))
-                    slopes[pair + half].append(mean_slope)
-                else:
-                    for at, x in enumerate(own):
-                        out[:, (5 * head + at) * DH : (5 * head + at + 1) * DH] = x
+            found = attend_head(both(q_refs[stack : stack + 1], head), k_both, v_both, state)
+            if final:
+                primal, tangent, peak, total, slope_total = found
+                inverse = 1.0 / total
+                mean_slope = slope_total * inverse
+                primal = primal * inverse
+                tangent = tangent * inverse - mean_slope * primal
+                first = 2 * head * DH
+                out[:, first : first + DH] = primal.astype(out.dtype)
+                out[:, first + DH : first + 2 * DH] = tangent.astype(out.dtype)
+                logs[stack].append(peak * FACTOR + jnp.log(total))
+                slopes[stack].append(mean_slope)
+            else:
+                for at, x in enumerate(found):
+                    out[:, (5 * head + at) * DH : (5 * head + at + 1) * DH] = x
     if final:
-        for at, out in enumerate(outs):
-            out[:, 2 * heads * DH :] = stats_columns(logs[at], slopes[at])
-
-
-def attend(q_blocks, k_blocks, earlier=None, final=False, hurried=True):
-    rows, width = q_blocks[0].shape
+        for stack, out in enumerate(outs):
+            out[:, 2 * heads * DH :] = stats_columns(logs[stack], slopes[stack])
+
+
+def attend(q_stacks, k_blocks, earlier=None, final=False):
+    rows, width = q_stacks[0].shape
     heads = width // (2 * DH)
     keys = sum(block.shape[0] for block in k_blocks) // 2
     merge = earlier is not None
     if final:
-        outs = [shape(rows, (2 * heads + 1) * DH)] * len(q_blocks)
+        outs = [shape(rows, (2 * heads + 1) * DH)] * len(q_stacks)
     else:
-        outs = [shape(rows, 5 * heads * DH, jnp.float32)] * len(q_blocks)
-    pairs = len(q_blocks) * rows * keys * heads
+        outs = [shape(rows, 5 * heads * DH, jnp.float32)] * len(q_stacks)
+    pairs = len(q_stacks) * rows * keys * heads
 
     def kernel(*refs):
-        attend_kernel(len(q_blocks), len(k_blocks), merge, final, *refs)
+        attend_kernel(len(q_stacks), len(k_blocks), merge, final, *refs)
 
     return call(
         kernel,
         "attend",
         outs,
-        list(q_blocks) + list(k_blocks) + list(earlier or ()),
-        flops=2 * pairs * DH * 8 if hurried else 0,
-        transcendentals=pairs if hurried else 0,
-        moves=hurried,
-    )
-
-
-def join_parts(refs):
-    parts = [ref[...] for ref in refs]
+        list(q_stacks) + list(k_blocks) + list(earlier or ()),
+        flops=2 * pairs * DH * 8,
+        transcendentals=pairs,
+    )
+
+
+def join_parts(parts):
     heads = (parts[0].shape[1] - DH) // (2 * DH)
     stats = [stats_of(part, heads) for part in parts]
     return [
@@ -211,8 +200,9 @@
     ]
 
 
-def join_kernel(a_ref, b_ref, out):
-    found = join_parts((a_ref, b_ref))
+def join_kernel(first_row, a_ref, b_ref, out):
+    own = pl.ds(first_row, out.shape[0])
+    found = join_parts([a_ref[own, :], b_ref[own, :]])
     for head, (primal, tangent, _, _) in enumerate(found):
         first = 2 * head * DH
         out[:, first : first + DH] = primal.astype(out.dtype)
@@ -221,7 +211,7 @@
 
 
 def project_kernel(a_ref, b_ref, w_ref, out):
-    found = join_parts((a_ref, b_ref))
+    found = join_parts([a_ref[...], b_ref[...]])
     attended = jnp.concatenate(
         [
             jnp.concatenate([f[at].astype(jnp.bfloat16) for f in found], axis=1)
@@ -266,39 +256,48 @@
 def on_device(queries, keys, values, tan_queries, tan_keys, tan_values, w_out):
     rows, width = queries.shape
     own = [beside(keys, tan_keys), beside(values, tan_values)]
-    up, down = [own], [own]
-
-    def hand_on():
-        up.append([along_z(x, 1) for x in up[-1]])
-        down.append([along_z(x, -1) for x in down[-1]])
-
-    hand_on()
+    def around(pair):
+        return along_z(pair[0], 1), along_z(pair[1], -1)
+
+    k_steps, v_steps = [(own[0], own[0])], [(own[1], own[1])]
+    k_steps.append(around(k_steps[0]))
+    v_steps.append(around(v_steps[0]))
+
     own_q = beside(tan_queries, queries)
-    own_q, up[1][0] = lax.optimization_barrier((own_q, up[1][0]))
-    far_q = lax.ppermute(own_q, "xh", SWAP)
-    near_q = [own_q, lax.ppermute(own_q, "core", SWAP)]
-    away_q = [far_q, lax.ppermute(far_q, "core", SWAP)]
-
-    hand_on()
-    up.append([along_z(up[2][0], 1)])
-    down.append([along_z(down[2][0], -1)])
-    states = attend(near_q + away_q, own + up[1] + down[1])
-    up[2][1], states = lax.optimization_barrier((up[2][1], states))
-    up[3].append(along_z(up[2][1], 1))
-    down[3].append(along_z(down[2][1], -1))
-    states = attend(near_q + away_q, up[2] + down[2], states)
-    up[3][0], states = lax.optimization_barrier((up[3][0], states))
-    last = [along_z(up[3][0], 1), along_z(down[3][1], -1)]
-    states = attend(near_q + away_q, up[3] + down[3], states)
-
-    away, away_other = attend(away_q, last, states[2:], True)
-    whole = [shape(*away.shape)]
-    to_far = call(join_kernel, "join", whole, [away, lax.ppermute(away_other, "core", SWAP)])[0]
-    to_far, near_states = lax.optimization_barrier((to_far, states[:2]))
-    from_far = lax.ppermute(to_far, "xh", SWAP)
-    near, near_other = attend(near_q, last, near_states, True, False)
-    near_parts = [near, lax.ppermute(near_other, "core", SWAP)]
-    near = call(join_kernel, "join", whole, near_parts, moves=False)[0]
+    stack = jnp.concatenate([own_q, lax.ppermute(own_q, "xh", SWAP)], axis=0)
+    stacks = [stack, lax.ppermute(stack, "core", SWAP)]
+
+    k_steps.append(around(k_steps[1]))
+    v_steps[1], k_steps[1] = lax.optimization_barrier((v_steps[1], k_steps[1]))
+    v_steps.append(around(v_steps[1]))
+    k_steps[2], v_steps[1] = lax.optimization_barrier((k_steps[2], v_steps[1]))
+    k_steps.append(around(k_steps[2]))
+    v_steps[2], k_steps[2], stacks = lax.optimization_barrier((v_steps[2], k_steps[2], stacks))
+    v_steps.append(around(v_steps[2]))
+
+    def both_ways(step):
+        return [x for pair in zip(k_steps[step], v_steps[step]) for x in pair]
+
+    states = attend(stacks, own + both_ways(1))
+    k_steps[3], v_steps[2], states = lax.optimization_barrier((k_steps[3], v_steps[2], states))
+    last = [along_z(k_steps[3][0], 1)]
+    states = attend(stacks, both_ways(2), states)
+    v_steps[3], k_steps[3], states = lax.optimization_barrier((v_steps[3], k_steps[3], states))
+    last.append(along_z(v_steps[3][1], -1))
+    states = attend(stacks, both_ways(3), states)
+
+    other = attend(stacks[1:], last, states[1:], True)[0]
+    other = lax.ppermute(other, "core", SWAP)
+    mine = attend(stacks[:1], last, states[:1], True)[0]
+
+    def join(first_row):
+        def kernel(*refs):
+            join_kernel(first_row, *refs)
+
+        return call(kernel, "join", [shape(rows, mine.shape[1])], [mine, other])[0]
+
+    from_far = lax.ppermute(join(rows), "xh", SWAP)
+    near = join(0)
     parts = call(
         project_kernel,
         "project",

time: 101 us -> 98.2 us (0.972)
  starting transfers between devices: 27.7 us -> 22.4 us
  waiting for transfers between devices: 23.2 us -> 27.1 us
    ppermute x14, starting transfers between devices: 22.8 us -> 18.3 us  [along_z(): return lax.ppermute(x, 'z', [(i, (i + step) % 8) for i in range(8)])]
    ppermute x14, waiting for transfers between devices: 13.9 us -> 18.1 us  [along_z(): return lax.ppermute(x, 'z', [(i, (i + step) % 8) for i in range(8)])]
    ppermute x6 -> x4, starting transfers between devices: 4.89 us -> 4.1 us  [the longest x1 2.21 us: on_device(): stack = jnp.concatenate([own_q, lax.ppermute(own_q, 'xh', SWAP)], axis=0)]
    ppermute x6 -> x4, waiting for transfers between devices: 9.32 us -> 8.96 us  [the longest x1 8.38 us: on_device(): from_far = lax.ppermute(join(rows), 'xh', SWAP)]
  transfers between devices with their start and end apart: 20 -> 18, of which waited for: 10 -> 10; matrix products, arithmetic and copies ran while one was open for 2% -> 2% of each run, Pallas kernels for 9% -> 10%
where the time goes in v1:
time: 98.2 us; the launch traced here: 97.3 us
  blocking collectives  29.4 us (30%)
  waiting for transfers between devices  27.1 us (28%)
  starting transfers between devices  22.4 us (23%)
  Pallas kernels  14.6 us (15%)
  other arithmetic  2.98 us (3%)
    all_to_all x1, blocking collectives, on_device(): parts = lax.all_to_all(parts, ('xl', 'y'), 0, 0)  29.4 us
    ppermute x14, starting transfers between devices, along_z(): return lax.ppermute(x, 'z', [(i, (i + step) % 8) for i in range(8)])  18.3 us
    ppermute x14, waiting for transfers between devices, along_z(): return lax.ppermute(x, 'z', [(i, (i + step) % 8) for i in range(8)])  18.1 us
    pallas_call x9, Pallas kernels, call(): pl.pallas_call(kernel, in_specs=[vmem()] * len(args), out_specs=[vmem()]...  14.6 us
    ppermute x1, waiting for transfers between devices, on_device(): from_far = lax.ppermute(join(rows), 'xh', SWAP)  8.38 us
    max x3, other arithmetic, beside(): jnp.maximum(lax.pad(left, low, [(0, 0, 0), (0, width, 0)]), lax.pad(right...  2.95 us
    ppermute x1, starting transfers between devices, on_device(): stack = jnp.concatenate([own_q, lax.ppermute(own_q, 'xh', SWAP)], axis=0)  2.21 us
  transfers between devices with their start and end apart: 18, of which 10 were waited for; matrix products, arithmetic and copies ran while one was open for 2% of the time, Pallas kernels for 10%

profile of v1, /device:TPU:98, one launch (start us, length us, event | category | flops | bytes accessed | tf_op | source)
XLA Modules:
  0.0 97.3 jit_solution(8879204946400757134)
XLA Ops:
  1.6 2.2 %collective-permute-start.8 = (bf16[160,768]{1,0:T(8,128)(2,1)S(1)}, bf16[160,768]{1,0:T(8,128)(2,1)S(1)}, u32[]{:S(2)}, u32[]{:S(2)}) collective-permute-start(bf16[160,768]{1,0:T(8,128)(2,1)S(1)} %pad_maximum_fusion.1), channel_id=1, source_target_pairs={{0,128},{128,0},{1,129},{129,1},{2,130},{130,2},{3,131},{131,3},{4... | collective-permute-start | bytes 737288 | tf_op jit(solution)/shard_map/ppermute | solution.py:267
  4.8 3.2 %collective-permute-start.2 = (bf16[160,768]{1,0:T(8,128)(2,1)S(1)}, bf16[160,768]{1,0:T(8,128)(2,1)S(1)}, u32[]{:S(2)}, u32[]{:S(2)}) collective-permute-start(bf16[160,768]{1,0:T(8,128)(2,1)S(1)} %pad_maximum_fusion.2.refs_2_), channel_id=1, source_target_pairs={{0,16},{16,32},{32,48},{48,64},{64,80},{80,96},{96,112},{112,0},{1... | collective-permute-start | bytes 737288 | tf_op jit(solution)/shard_map/ppermute | solution.py:244
  9.0 3.3 %collective-permute-start = (bf16[160,768]{1,0:T(8,128)(2,1)S(1)}, bf16[160,768]{1,0:T(8,128)(2,1)S(1)}, u32[]{:S(2)}, u32[]{:S(2)}) collective-permute-start(bf16[160,768]{1,0:T(8,128)(2,1)S(1)} %pad_maximum_fusion.3.refs_3_), channel_id=1, source_target_pairs={{0,16},{16,32},{32,48},{48,64},{64,80},{80,96},{96,112},{112,0},{1... | collective-permute-start | bytes 737288 | tf_op jit(solution)/shard_map/ppermute | solution.py:244
  12.5 2.0 %collective-permute-done.2.refs_4_ = bf16[160,768]{1,0:T(8,128)(2,1)S(1)} collective-permute-done((bf16[160,768]{1,0:T(8,128)(2,1)S(1)}, bf16[160,768]{1,0:T(8,128)(2,1)S(1)}, u32[]{:S(2)}, u32[]{:S(2)}) %collective-permute-start.2) | collective-permute-done | bytes 245792 | tf_op jit(solution)/shard_map/ppermute | solution.py:244
  14.4 3.7 %collective-permute-start.6 = (bf16[160,768]{1,0:T(8,128)(2,1)S(1)}, bf16[160,768]{1,0:T(8,128)(2,1)S(1)}, u32[]{:S(2)}, u32[]{:S(2)}) collective-permute-start(bf16[160,768]{1,0:T(8,128)(2,1)S(1)} %collective-permute-done.2.refs_4_), channel_id=1, source_target_pairs={{0,16},{16,32},{32,48},{48,64},{64,80},{80,96},{96,112},{112,0},{1... | collective-permute-start | bytes 737288 | tf_op jit(solution)/shard_map/ppermute | solution.py:244
  18.1 1.6 %collective-permute-done.refs_5_ = bf16[160,768]{1,0:T(8,128)(2,1)S(1)} collective-permute-done((bf16[160,768]{1,0:T(8,128)(2,1)S(1)}, bf16[160,768]{1,0:T(8,128)(2,1)S(1)}, u32[]{:S(2)}, u32[]{:S(2)}) %collective-permute-start) | collective-permute-done | bytes 245792 | tf_op jit(solution)/shard_map/ppermute | solution.py:244
  19.7 3.4 %collective-permute-done.1.refs_7_ = bf16[160,768]{1,0:T(8,128)(2,1)S(1)} collective-permute-done((bf16[160,768]{1,0:T(8,128)(2,1)S(1)}, bf16[160,768]{1,0:T(8,128)(2,1)S(1)}, u32[]{:S(2)}, u32[]{:S(2)}) %collective-permute-start.1) | collective-permute-done | bytes 245792 | tf_op jit(solution)/shard_map/ppermute | solution.py:244
  23.4 1.7 %collective-permute-start.5 = (bf16[160,768]{1,0:T(8,128)(2,1)S(1)}, bf16[160,768]{1,0:T(8,128)(2,1)S(1)}, u32[]{:S(2)}, u32[]{:S(2)}) collective-permute-start(bf16[160,768]{1,0:T(8,128)(2,1)S(1)} %collective-permute-done.1.refs_7_), channel_id=1, source_target_pairs={{0,112},{16,0},{32,16},{48,32},{64,48},{80,64},{96,80},{112,96},{1... | collective-permute-start | bytes 737288 | tf_op jit(solution)/shard_map/ppermute | solution.py:244
  25.1 3.2 %collective-permute-done.7.refs_4_ = bf16[160,768]{1,0:T(8,128)(2,1)S(1)} collective-permute-done((bf16[160,768]{1,0:T(8,128)(2,1)S(1)}, bf16[160,768]{1,0:T(8,128)(2,1)S(1)}, u32[]{:S(2)}, u32[]{:S(2)}) %collective-permute-start.7) | collective-permute-done | bytes 245792 | tf_op jit(solution)/shard_map/ppermute | solution.py:244
  28.6 1.7 %collective-permute-start.11 = (bf16[160,768]{1,0:T(8,128)(2,1)S(1)}, bf16[160,768]{1,0:T(8,128)(2,1)S(1)}, u32[]{:S(2)}, u32[]{:S(2)}) collective-permute-start(bf16[160,768]{1,0:T(8,128)(2,1)S(1)} %collective-permute-done.7.refs_4_), channel_id=1, source_target_pairs={{0,112},{16,0},{32,16},{48,32},{64,48},{80,64},{96,80},{112,96},{1... | collective-permute-start | bytes 737288 | tf_op jit(solution)/shard_map/ppermute | solution.py:244
  30.4 3.2 %collective-permute-done.5.refs_5_ = bf16[160,768]{1,0:T(8,128)(2,1)S(1)} collective-permute-done((bf16[160,768]{1,0:T(8,128)(2,1)S(1)}, bf16[160,768]{1,0:T(8,128)(2,1)S(1)}, u32[]{:S(2)}, u32[]{:S(2)}) %collective-permute-start.5) | collective-permute-done | bytes 245792 | tf_op jit(solution)/shard_map/ppermute | solution.py:244
  33.9 1.7 %collective-permute-start.14 = (bf16[160,768]{1,0:T(8,128)(2,1)S(1)}, bf16[160,768]{1,0:T(8,128)(2,1)S(1)}, u32[]{:S(2)}, u32[]{:S(2)}) collective-permute-start(bf16[160,768]{1,0:T(8,128)(2,1)S(1)} %collective-permute-done.5.refs_5_), channel_id=1, source_target_pairs={{0,112},{16,0},{32,16},{48,32},{64,48},{80,64},{96,80},{112,96},{1... | collective-permute-start | bytes 737288 | tf_op jit(solution)/shard_map/ppermute | solution.py:244
  35.7 2.7 %attend.5 = (f32[320,1920]{1,0:T(8,128)S(1)}, f32[320,1920]{1,0:T(8,128)S(1)}) custom-call(bf16[320,768]{1,0:T(8,128)(2,1)S(1)} %pad_maximum_fusion.refs_0_, bf16[320,768]{1,0:T(8,128)(2,1)S(1)} %collective-permute-done.9.refs_1_.refs_0_, bf16[160,768]{1,0:T(8,128)(2,1)S(1)} %pad_maximum_fusion.2.refs_2_, bf16[160,768]{1,0:T(8,128)(2,1)S(1)} %pad_maximum_fusion.3.refs_3_, ...), custom_call_target="tpu_custom_call" | custom-call | flops 1887436800 | bytes 7372800 | tf_op jit(solution)/shard_map/attend/pallas_call | solution.py:28
  38.9 1.0 %collective-permute-start.12 = (bf16[160,768]{1,0:T(8,128)(2,1)S(1)}, bf16[160,768]{1,0:T(8,128)(2,1)S(1)}, u32[]{:S(2)}, u32[]{:S(2)}) collective-permute-start(bf16[160,768]{1,0:T(8,128)(2,1)S(1)} %collective-permute-done.10.refs_2_), channel_id=1, source_target_pairs={{0,16},{16,32},{32,48},{48,64},{64,80},{80,96},{96,112},{112,0},{1... | collective-permute-start | bytes 737288 | tf_op jit(solution)/shard_map/ppermute | solution.py:244
  39.9 2.7 %attend.6 = (f32[320,1920]{1,0:T(8,128)S(1)}, f32[320,1920]{1,0:T(8,128)S(1)}) custom-call(bf16[320,768]{1,0:T(8,128)(2,1)S(1)} %pad_maximum_fusion.refs_0_, bf16[320,768]{1,0:T(8,128)(2,1)S(1)} %collective-permute-done.9.refs_1_.refs_0_, bf16[160,768]{1,0:T(8,128)(2,1)S(1)} %collective-permute-done.6.refs_2_, ...), custom_call_target="tpu_custom_call" | custom-call | flops 1258291200 | bytes 11796480 | tf_op jit(solution)/shard_map/attend/pallas_call | solution.py:28
  42.7 1.0 %collective-permute-start.15 = (bf16[160,768]{1,0:T(8,128)(2,1)S(1)}, bf16[160,768]{1,0:T(8,128)(2,1)S(1)}, u32[]{:S(2)}, u32[]{:S(2)}) collective-permute-start(bf16[160,768]{1,0:T(8,128)(2,1)S(1)} %collective-permute-done.14.refs_5_), channel_id=1, source_target_pairs={{0,112},{16,0},{32,16},{48,32},{64,48},{80,64},{96,80},{112,96},{1... | collective-permute-start | bytes 737288 | tf_op jit(solution)/shard_map/ppermute | solution.py:244
  43.7 2.7 %attend.7 = (f32[320,1920]{1,0:T(8,128)S(1)}, f32[320,1920]{1,0:T(8,128)S(1)}) custom-call(bf16[320,768]{1,0:T(8,128)(2,1)S(1)} %pad_maximum_fusion.refs_0_, bf16[320,768]{1,0:T(8,128)(2,1)S(1)} %collective-permute-done.9.refs_1_.refs_0_, bf16[160,768]{1,0:T(8,128)(2,1)S(1)} %collective-permute-done.10.refs_2_, ...), custom_call_target="tpu_custom_call" | custom-call | flops 1258291200 | bytes 11796480 | tf_op jit(solution)/shard_map/attend/pallas_call | solution.py:28
  46.4 4.1 %collective-permute-done.15.refs_2_ = bf16[160,768]{1,0:T(8,128)(2,1)S(1)} collective-permute-done((bf16[160,768]{1,0:T(8,128)(2,1)S(1)}, bf16[160,768]{1,0:T(8,128)(2,1)S(1)}, u32[]{:S(2)}, u32[]{:S(2)}) %collective-permute-start.15) | collective-permute-done | bytes 245792 | tf_op jit(solution)/shard_map/ppermute | solution.py:244
  50.4 1.4 %attend.9 = bf16[320,896]{1,0:T(8,128)(2,1)S(1)} custom-call(bf16[320,768]{1,0:T(8,128)(2,1)S(1)} %collective-permute-done.9.refs_1_.refs_0_, bf16[160,768]{1,0:T(8,128)(2,1)S(1)} %collective-permute-done.12.refs_1_, bf16[160,768]{1,0:T(8,128)(2,1)S(1)} %collective-permute-done.15.refs_2_, f32[320,1920]{1,0:T(8,128)S(1)} %get-tuple-element.65.refs_3_), custom_call_target="tpu_custom_call" | custom-call | flops 314572800 | bytes 4014080 | tf_op jit(solution)/shard_map/attend/pallas_call | solution.py:28
  52.1 1.4 %attend.8.refs_0_ = bf16[320,896]{1,0:T(8,128)(2,1)S(1)} custom-call(bf16[320,768]{1,0:T(8,128)(2,1)S(1)} %pad_maximum_fusion.refs_0_, bf16[160,768]{1,0:T(8,128)(2,1)S(1)} %collective-permute-done.12.refs_1_, bf16[160,768]{1,0:T(8,128)(2,1)S(1)} %collective-permute-done.15.refs_2_, f32[320,1920]{1,0:T(8,128)S(1)} %get-tuple-element.64.refs_3_), custom_call_target="tpu_custom_call" | custom-call | flops 314572800 | bytes 4014080 | tf_op jit(solution)/shard_map/attend/pallas_call | solution.py:28
  54.7 1.5 %collective-permute-start.17 = (bf16[160,896]{1,0:T(8,128)(2,1)S(1)}, bf16[160,896]{1,0:T(8,128)(2,1)S(1)}, u32[]{:S(2)}, u32[]{:S(2)}) collective-permute-start(bf16[160,896]{1,0:T(8,128)(2,1)S(1)} %join.3), channel_id=1, source_target_pairs={{0,128},{128,0},{1,129},{129,1},{2,130},{130,2},{3,131},{131,3},{4... | collective-permute-start | bytes 860168 | tf_op jit(solution)/shard_map/ppermute | solution.py:299
  56.8 8.4 %collective-permute-done.17.b_ref = bf16[160,896]{1,0:T(8,128)(2,1)S(1)} collective-permute-done((bf16[160,896]{1,0:T(8,128)(2,1)S(1)}, bf16[160,896]{1,0:T(8,128)(2,1)S(1)}, u32[]{:S(2)}, u32[]{:S(2)}) %collective-permute-start.17) | collective-permute-done | bytes 286752 | tf_op jit(solution)/shard_map/ppermute | solution.py:299
  65.2 1.8 %project.1 = bf16[8,320,384]{2,1,0:T(8,128)(2,1)S(1)} custom-call(bf16[160,896]{1,0:T(8,128)(2,1)S(1)} %join.2.a_ref, bf16[160,896]{1,0:T(8,128)(2,1)S(1)} %collective-permute-done.17.b_ref, bf16[384,3072]{1,0:T(8,128)(2,1)S(1)} %copy-done), custom_call_target="tpu_custom_call" | custom-call | flops 754974720 | bytes 4898816 | tf_op jit(solution)/shard_map/project/pallas_call | solution.py:28
  67.0 29.4 %all_to_all.5.parts_ref = bf16[8,320,384]{2,1,0:T(8,128)(2,1)S(1)} all-to-all(bf16[8,320,384]{2,1,0:T(8,128)(2,1)S(1)} %project.1), channel_id=1, replica_groups=mesh['xh'=2,'z'=8,'core'=2,'xl'=2,'y'=4] {'xl','y'}, dimensions={0} | all-to-all | bytes 3932160 | tf_op jit(solution)/shard_map/all_to_all | solution.py:308
  (28 shorter events, 7.6 us)
Async XLA Ops:
  1.6 10.7 %collective-permute-start.8 = (bf16[160,768]{1,0:T(8,128)(2,1)S(1)}, bf16[160,768]{1,0:T(8,128)(2,1)S(1)}, u32[]{:S(2)}, u32[]{:S(2)}) collective-permute-start(bf16[160,768]{1,0:T(8,128)(2,1)S(1)} %pad_maximum_fusion.1), channel_id=1, source_target_pairs={{0,128},{128,0},{1,129},{129,1},{2,130},{130,2},{3,131},{131,3},{4... | collective-permute-start | bytes 737288 | tf_op jit(solution)/shard_map/ppermute | solution.py:267
  4.8 9.6 %collective-permute-start.2 = (bf16[160,768]{1,0:T(8,128)(2,1)S(1)}, bf16[160,768]{1,0:T(8,128)(2,1)S(1)}, u32[]{:S(2)}, u32[]{:S(2)}) collective-permute-start(bf16[160,768]{1,0:T(8,128)(2,1)S(1)} %pad_maximum_fusion.2.refs_2_), channel_id=1, source_target_pairs={{0,16},{16,32},{32,48},{48,64},{64,80},{80,96},{96,112},{112,0},{1... | collective-permute-start | bytes 737288 | tf_op jit(solution)/shard_map/ppermute | solution.py:244
  8.0 10.1 %collective-permute-start.3 = (bf16[160,768]{1,0:T(8,128)(2,1)S(1)}, bf16[160,768]{1,0:T(8,128)(2,1)S(1)}, u32[]{:S(2)}, u32[]{:S(2)}) collective-permute-start(bf16[160,768]{1,0:T(8,128)(2,1)S(1)} %pad_maximum_fusion.2.refs_2_), channel_id=1, source_target_pairs={{0,112},{16,0},{32,16},{48,32},{64,48},{80,64},{96,80},{112,96},{1... | collective-permute-start | bytes 737288 | tf_op jit(solution)/shard_map/ppermute | solution.py:244
  9.0 10.7 %collective-permute-start = (bf16[160,768]{1,0:T(8,128)(2,1)S(1)}, bf16[160,768]{1,0:T(8,128)(2,1)S(1)}, u32[]{:S(2)}, u32[]{:S(2)}) collective-permute-start(bf16[160,768]{1,0:T(8,128)(2,1)S(1)} %pad_maximum_fusion.3.refs_3_), channel_id=1, source_target_pairs={{0,16},{16,32},{32,48},{48,64},{64,80},{80,96},{96,112},{112,0},{1... | collective-permute-start | bytes 737288 | tf_op jit(solution)/shard_map/ppermute | solution.py:244
  12.3 10.8 %collective-permute-start.1 = (bf16[160,768]{1,0:T(8,128)(2,1)S(1)}, bf16[160,768]{1,0:T(8,128)(2,1)S(1)}, u32[]{:S(2)}, u32[]{:S(2)}) collective-permute-start(bf16[160,768]{1,0:T(8,128)(2,1)S(1)} %pad_maximum_fusion.3.refs_3_), channel_id=1, source_target_pairs={{0,112},{16,0},{32,16},{48,32},{64,48},{80,64},{96,80},{112,96},{1... | collective-permute-start | bytes 737288 | tf_op jit(solution)/shard_map/ppermute | solution.py:244
  12.4 21.3 %collective-permute-start.9 = (bf16[320,768]{1,0:T(8,128)(2,1)S(1)}, bf16[320,768]{1,0:T(8,128)(2,1)S(1)}, u32[]{:S(2)}, u32[]{:S(2)}) collective-permute-start(bf16[320,768]{1,0:T(8,128)(2,1)S(1)} %pad_maximum_fusion.refs_0_), channel_id=1, source_target_pairs={{0,8},{8,0},{1,9},{9,1},{2,10},{10,2},{3,11},{11,3},{4,12},{12,4},... | collective-permute-start | bytes 1474568 | tf_op jit(solution)/shard_map/ppermute | solution.py:268
  14.4 10.7 %collective-permute-start.6 = (bf16[160,768]{1,0:T(8,128)(2,1)S(1)}, bf16[160,768]{1,0:T(8,128)(2,1)S(1)}, u32[]{:S(2)}, u32[]{:S(2)}) collective-permute-start(bf16[160,768]{1,0:T(8,128)(2,1)S(1)} %collective-permute-done.2.refs_4_), channel_id=1, source_target_pairs={{0,16},{16,32},{32,48},{48,64},{64,80},{80,96},{96,112},{112,0},{1... | collective-permute-start | bytes 737288 | tf_op jit(solution)/shard_map/ppermute | solution.py:244
  18.1 10.2 %collective-permute-start.7 = (bf16[160,768]{1,0:T(8,128)(2,1)S(1)}, bf16[160,768]{1,0:T(8,128)(2,1)S(1)}, u32[]{:S(2)}, u32[]{:S(2)}) collective-permute-start(bf16[160,768]{1,0:T(8,128)(2,1)S(1)} %collective-permute-done.3.refs_6_), channel_id=1, source_target_pairs={{0,112},{16,0},{32,16},{48,32},{64,48},{80,64},{96,80},{112,96},{1... | collective-permute-start | bytes 737288 | tf_op jit(solution)/shard_map/ppermute | solution.py:244
  23.1 7.3 %collective-permute-start.4 = (bf16[160,768]{1,0:T(8,128)(2,1)S(1)}, bf16[160,768]{1,0:T(8,128)(2,1)S(1)}, u32[]{:S(2)}, u32[]{:S(2)}) collective-permute-start(bf16[160,768]{1,0:T(8,128)(2,1)S(1)} %collective-permute-done.refs_5_), channel_id=1, source_target_pairs={{0,16},{16,32},{32,48},{48,64},{64,80},{80,96},{96,112},{112,0},{1... | collective-permute-start | bytes 737288 | tf_op jit(solution)/shard_map/ppermute | solution.py:244
  23.4 10.2 %collective-permute-start.5 = (bf16[160,768]{1,0:T(8,128)(2,1)S(1)}, bf16[160,768]{1,0:T(8,128)(2,1)S(1)}, u32[]{:S(2)}, u32[]{:S(2)}) collective-permute-start(bf16[160,768]{1,0:T(8,128)(2,1)S(1)} %collective-permute-done.1.refs_7_), channel_id=1, source_target_pairs={{0,112},{16,0},{32,16},{48,32},{64,48},{80,64},{96,80},{112,96},{1... | collective-permute-start | bytes 737288 | tf_op jit(solution)/shard_map/ppermute | solution.py:244
  28.4 10.0 %collective-permute-start.10 = (bf16[160,768]{1,0:T(8,128)(2,1)S(1)}, bf16[160,768]{1,0:T(8,128)(2,1)S(1)}, u32[]{:S(2)}, u32[]{:S(2)}) collective-permute-start(bf16[160,768]{1,0:T(8,128)(2,1)S(1)} %collective-permute-done.6.refs_2_), channel_id=1, source_target_pairs={{0,16},{16,32},{32,48},{48,64},{64,80},{80,96},{96,112},{112,0},{1... | collective-permute-start | bytes 737288 | tf_op jit(solution)/shard_map/ppermute | solution.py:244
  28.6 10.2 %collective-permute-start.11 = (bf16[160,768]{1,0:T(8,128)(2,1)S(1)}, bf16[160,768]{1,0:T(8,128)(2,1)S(1)}, u32[]{:S(2)}, u32[]{:S(2)}) collective-permute-start(bf16[160,768]{1,0:T(8,128)(2,1)S(1)} %collective-permute-done.7.refs_4_), channel_id=1, source_target_pairs={{0,112},{16,0},{32,16},{48,32},{64,48},{80,64},{96,80},{112,96},{1... | collective-permute-start | bytes 737288 | tf_op jit(solution)/shard_map/ppermute | solution.py:244
  33.6 9.0 %collective-permute-start.13 = (bf16[160,768]{1,0:T(8,128)(2,1)S(1)}, bf16[160,768]{1,0:T(8,128)(2,1)S(1)}, u32[]{:S(2)}, u32[]{:S(2)}) collective-permute-start(bf16[160,768]{1,0:T(8,128)(2,1)S(1)} %collective-permute-done.4.refs_3_), channel_id=1, source_target_pairs={{0,16},{16,32},{32,48},{48,64},{64,80},{80,96},{96,112},{112,0},{1... | collective-permute-start | bytes 737288 | tf_op jit(solution)/shard_map/ppermute | solution.py:244
  33.9 8.8 %collective-permute-start.14 = (bf16[160,768]{1,0:T(8,128)(2,1)S(1)}, bf16[160,768]{1,0:T(8,128)(2,1)S(1)}, u32[]{:S(2)}, u32[]{:S(2)}) collective-permute-start(bf16[160,768]{1,0:T(8,128)(2,1)S(1)} %collective-permute-done.5.refs_5_), channel_id=1, source_target_pairs={{0,112},{16,0},{32,16},{48,32},{64,48},{80,64},{96,80},{112,96},{1... | collective-permute-start | bytes 737288 | tf_op jit(solution)/shard_map/ppermute | solution.py:244
  38.9 7.5 %collective-permute-start.12 = (bf16[160,768]{1,0:T(8,128)(2,1)S(1)}, bf16[160,768]{1,0:T(8,128)(2,1)S(1)}, u32[]{:S(2)}, u32[]{:S(2)}) collective-permute-start(bf16[160,768]{1,0:T(8,128)(2,1)S(1)} %collective-permute-done.10.refs_2_), channel_id=1, source_target_pairs={{0,16},{16,32},{32,48},{48,64},{64,80},{80,96},{96,112},{112,0},{1... | collective-permute-start | bytes 737288 | tf_op jit(solution)/shard_map/ppermute | solution.py:244
  42.7 7.7 %collective-permute-start.15 = (bf16[160,768]{1,0:T(8,128)(2,1)S(1)}, bf16[160,768]{1,0:T(8,128)(2,1)S(1)}, u32[]{:S(2)}, u32[]{:S(2)}) collective-permute-start(bf16[160,768]{1,0:T(8,128)(2,1)S(1)} %collective-permute-done.14.refs_5_), channel_id=1, source_target_pairs={{0,112},{16,0},{32,16},{48,32},{64,48},{80,64},{96,80},{112,96},{1... | collective-permute-start | bytes 737288 | tf_op jit(solution)/shard_map/ppermute | solution.py:244
  51.8 2.3 %collective-permute-start.16 = (bf16[320,896]{1,0:T(8,128)(2,1)S(1)}, bf16[320,896]{1,0:T(8,128)(2,1)S(1)}, u32[]{:S(2)}, u32[]{:S(2)}) collective-permute-start(bf16[320,896]{1,0:T(8,128)(2,1)S(1)} %attend.9), channel_id=1, source_target_pairs={{0,8},{8,0},{1,9},{9,1},{2,10},{10,2},{3,11},{11,3},{4,12},{12,4},... | collective-permute-start | bytes 1720328 | tf_op jit(solution)/shard_map/ppermute | solution.py:290
  52.1 13.0 %copy-start = (bf16[384,3072]{1,0:T(8,128)(2,1)S(1)}, bf16[384,3072]{1,0:T(8,128)(2,1)}, u32[]{:S(2)}) copy-start(bf16[384,3072]{1,0:T(8,128)(2,1)} %w_ref.1) | copy-start | bytes 7077892
  54.7 10.5 %collective-permute-start.17 = (bf16[160,896]{1,0:T(8,128)(2,1)S(1)}, bf16[160,896]{1,0:T(8,128)(2,1)S(1)}, u32[]{:S(2)}, u32[]{:S(2)}) collective-permute-start(bf16[160,896]{1,0:T(8,128)(2,1)S(1)} %join.3), channel_id=1, source_target_pairs={{0,128},{128,0},{1,129},{129,1},{2,130},{130,2},{3,131},{131,3},{4... | collective-permute-start | bytes 860168 | tf_op jit(solution)/shard_map/ppermute | solution.py:299

commit v2 on v1

--- a/solution.py
+++ b/solution.py
@@ -12,8 +12,7 @@
 LOG2E = math.log2(math.e)
 CTX = (("xh", 2), ("z", 8), ("core", 2))
 HEAD = (("xl", 2), ("y", 4))
-GROUPS = 8
-VMEM_LIMIT = 20 * 1024 * 1024
+VMEM_LIMIT = 12 * 1024 * 1024
 PARAMS = pltpu.CompilerParams(vmem_limit_bytes=VMEM_LIMIT)
 
 _NT = (((1,), (1,)), ((), ()))
@@ -210,28 +209,46 @@
     out[:, 2 * len(found) * DH :] = stats_columns([f[2] for f in found], [f[3] for f in found])
 
 
-def project_kernel(a_ref, b_ref, w_ref, out):
+def attended_kernel(a_ref, b_ref, out):
     found = join_parts([a_ref[...], b_ref[...]])
-    attended = jnp.concatenate(
-        [
-            jnp.concatenate([f[at].astype(jnp.bfloat16) for f in found], axis=1)
-            for at in range(2)
-        ],
-        axis=0,
-    )
-    columns = out.shape[2]
-    for group in range(out.shape[0]):
-        out[group] = jnp.dot(
-            attended,
-            w_ref[:, group * columns : (group + 1) * columns],
-            preferred_element_type=jnp.float32,
-        ).astype(out.dtype)
-
-
-def total_kernel(parts_ref, value_ref, tangent_ref):
-    total = parts_ref[0].astype(jnp.float32)
-    for group in range(1, parts_ref.shape[0]):
-        total = total + parts_ref[group].astype(jnp.float32)
+    rows = out.shape[0] // 2
+    for head, each in enumerate(found):
+        for at in range(2):
+            out[at * rows : (at + 1) * rows, head * DH : (head + 1) * DH] = each[at].astype(out.dtype)
+
+
+def project_kernel(at_ref, own_ref, beside_ref, w_ref, w_mine_ref, w_other_ref, *outs):
+    xl, y, core = at_ref[0], at_ref[1], at_ref[2]
+    columns = outs[0].shape[1]
+    for step, out in enumerate(outs):
+        target = lax.rem(y + step, len(outs))
+        fetched_by, place = lax.div(target, 2), lax.rem(target, 2)
+        first = pl.multiple_of((xl * len(outs) + target) * columns, DH)
+        first_beside = pl.ds(pl.multiple_of(place * columns, DH), columns)
+        w_beside = jnp.where(
+            fetched_by == core, w_mine_ref[:, first_beside], w_other_ref[:, first_beside]
+        )
+        total = jnp.dot(
+            own_ref[...], w_ref[:, pl.ds(first, columns)], preferred_element_type=jnp.float32
+        ) + jnp.dot(beside_ref[...], w_beside, preferred_element_type=jnp.float32)
+        out[...] = total.astype(out.dtype)
+
+
+def project(place, own, beside, w_out, w_mine, w_other):
+    outs = [shape(*own.shape)] * 4
+    return pl.pallas_call(
+        project_kernel,
+        in_specs=[pl.BlockSpec(memory_space=pltpu.SMEM)] + [vmem()] * 5,
+        out_specs=[vmem()] * len(outs),
+        out_shape=outs,
+        compiler_params=PARAMS,
+        name="project",
+    )(jnp.stack(place).astype(jnp.int32), own, beside, w_out, w_mine, w_other)
+
+
+def total_kernel(*refs):
+    parts, (value_ref, tangent_ref) = refs[:-2], refs[-2:]
+    total = sum(part[...].astype(jnp.float32) for part in parts)
     rows = value_ref.shape[0]
     value_ref[...] = total[:rows].astype(value_ref.dtype)
     tangent_ref[...] = total[rows:].astype(tangent_ref.dtype)
@@ -264,7 +281,14 @@
     v_steps.append(around(v_steps[0]))
 
     own_q = beside(tan_queries, queries)
-    stack = jnp.concatenate([own_q, lax.ppermute(own_q, "xh", SWAP)], axis=0)
+    place = [lax.axis_index(name) for name in ("xl", "y", "core")]
+    quarter = w_out.shape[1] // 4
+    wanted = lax.dynamic_slice_in_dim(
+        w_out, ((1 - place[0]) * 2 + place[2]) * quarter, quarter, axis=1
+    )
+    far_q = lax.ppermute(own_q, "xh", SWAP)
+    wanted, far_q = lax.optimization_barrier((wanted, far_q))
+    stack = jnp.concatenate([own_q, far_q], axis=0)
     stacks = [stack, lax.ppermute(stack, "core", SWAP)]
 
     k_steps.append(around(k_steps[1]))
@@ -275,6 +299,9 @@
     v_steps[2], k_steps[2], stacks = lax.optimization_barrier((v_steps[2], k_steps[2], stacks))
     v_steps.append(around(v_steps[2]))
 
+    wanted, v_steps[1] = lax.optimization_barrier((wanted, v_steps[1]))
+    w_mine = lax.ppermute(wanted, "xl", SWAP)
+
     def both_ways(step):
         return [x for pair in zip(k_steps[step], v_steps[step]) for x in pair]
 
@@ -286,6 +313,7 @@
     last.append(along_z(v_steps[3][1], -1))
     states = attend(stacks, both_ways(3), states)
 
+    states, w_mine = lax.optimization_barrier((states, w_mine))
     other = attend(stacks[1:], last, states[1:], True)[0]
     other = lax.ppermute(other, "core", SWAP)
     mine = attend(stacks[:1], last, states[:1], True)[0]
@@ -298,15 +326,15 @@
 
     from_far = lax.ppermute(join(rows), "xh", SWAP)
     near = join(0)
-    parts = call(
-        project_kernel,
-        "project",
-        [jax.ShapeDtypeStruct((GROUPS, 2 * rows, w_out.shape[1] // GROUPS), jnp.bfloat16)],
-        [near, from_far, w_out],
-        flops=4 * rows * w_out.shape[0] * w_out.shape[1],
-    )[0]
-    parts = lax.all_to_all(parts, ("xl", "y"), 0, 0)
-    return tuple(call(total_kernel, "total", [shape(rows, width)] * 2, [parts]))
+    attended = call(attended_kernel, "attended", [shape(2 * rows, width)], [near, from_far])[0]
+    beside_attended = lax.ppermute(attended, "xl", SWAP)
+    w_other = lax.ppermute(w_mine, "core", SWAP)
+    parts = list(project(place, attended, beside_attended, w_out, w_mine, w_other))
+    parts = parts[:1] + [
+        lax.ppermute(part, "y", [(i, (i + step) % 4) for i in range(4)])
+        for step, part in enumerate(parts[1:], 1)
+    ]
+    return tuple(call(total_kernel, "total", [shape(rows, width)] * 2, parts))
 
 
 def solution(mesh):

time: 98.2 us -> 91.6 us (0.933)
  blocking collectives: 29.4 us -> 0 us
  waiting for transfers between devices: 27.1 us -> 42.1 us
  starting transfers between devices: 22.4 us -> 28.6 us
  local copies, waits for them, and re-layouts: 0.01 us -> 1.11 us
  Pallas kernels: 14.6 us -> 15.7 us
    all_to_all x1 -> x0, blocking collectives: 29.4 us -> none  [on_device(): parts = lax.all_to_all(parts, ('xl', 'y'), 0, 0)]
    ppermute x1 -> x7, waiting for transfers between devices: 0.01 us -> 16.8 us  [the longest x3 8.27 us: on_device(): lax.ppermute(part, 'y', [(i, (i + step) % 4) for i in range(4)])]
    ppermute x1 -> x7, starting transfers between devices: 2.21 us -> 9.35 us  [the longest x3 5.91 us: on_device(): lax.ppermute(part, 'y', [(i, (i + step) % 4) for i in range(4)])]
    pallas_call x0 -> x1, Pallas kernels: none -> 2.46 us  [project(): pl.pallas_call(project_kernel, in_specs=[pl.BlockSpec(memory_space=pltpu....]
    pallas_call x9, Pallas kernels: 14.6 us -> 13.2 us  [call(): pl.pallas_call(kernel, in_specs=[vmem()] * len(args), out_specs=[vmem()]...]
    ppermute x14, starting transfers between devices: 18.3 us -> 17.2 us  [along_z(): return lax.ppermute(x, 'z', [(i, (i + step) % 8) for i in range(8)])]
    dynamic_slice x0 -> x1, local copies, waits for them, and re-layouts: none -> 1.1 us  [on_device(): lax.dynamic_slice_in_dim(w_out, ((1 - place[0]) * 2 + place[2]) * quarter...]
    ppermute x14, waiting for transfers between devices: 18.1 us -> 17.1 us  [along_z(): return lax.ppermute(x, 'z', [(i, (i + step) % 8) for i in range(8)])]
  transfers between devices with their start and end apart: 18 -> 24, of which waited for: 10 -> 13; matrix products, arithmetic and copies ran while one was open for 2% -> 3% of each run, Pallas kernels for 10% -> 12%
where the time goes in v2:
time: 91.6 us; the launch traced here: 91.3 us
  waiting for transfers between devices  42.1 us (46%)
  starting transfers between devices  28.6 us (31%)
  Pallas kernels  15.7 us (17%)
  other arithmetic  3.06 us (3%)
  local copies, waits for them, and re-layouts  1.11 us (1%)
    ppermute x14, starting transfers between devices, along_z(): return lax.ppermute(x, 'z', [(i, (i + step) % 8) for i in range(8)])  17.2 us
    ppermute x14, waiting for transfers between devices, along_z(): return lax.ppermute(x, 'z', [(i, (i + step) % 8) for i in range(8)])  17.1 us
    pallas_call x9, Pallas kernels, call(): pl.pallas_call(kernel, in_specs=[vmem()] * len(args), out_specs=[vmem()]...  13.2 us
    ppermute x3, waiting for transfers between devices, on_device(): lax.ppermute(part, 'y', [(i, (i + step) % 4) for i in range(4)])  8.27 us
    ppermute x1, waiting for transfers between devices, on_device(): from_far = lax.ppermute(join(rows), 'xh', SWAP)  8.08 us
    ppermute x1, waiting for transfers between devices, on_device(): beside_attended = lax.ppermute(attended, 'xl', SWAP)  7.12 us
    ppermute x3, starting transfers between devices, on_device(): lax.ppermute(part, 'y', [(i, (i + step) % 4) for i in range(4)])  5.91 us
    max x3, other arithmetic, beside(): jnp.maximum(lax.pad(left, low, [(0, 0, 0), (0, width, 0)]), lax.pad(right...  2.95 us
  transfers between devices with their start and end apart: 24, of which 13 were waited for; matrix products, arithmetic and copies ran while one was open for 3% of the time, Pallas kernels for 12%

profile of v2, /device:TPU:98, one launch (start us, length us, event | category | flops | bytes accessed | tf_op | source)
XLA Modules:
  0.0 91.3 jit_solution(7972306819605222781)
XLA Ops:
  1.6 3.2 %collective-permute-start.2 = (bf16[160,768]{1,0:T(8,128)(2,1)S(1)}, bf16[160,768]{1,0:T(8,128)(2,1)S(1)}, u32[]{:S(2)}, u32[]{:S(2)}) collective-permute-start(bf16[160,768]{1,0:T(8,128)(2,1)S(1)} %pad_maximum_fusion.2.refs_2_), channel_id=1, source_target_pairs={{0,16},{16,32},{32,48},{48,64},{64,80},{80,96},{96,112},{112,0},{1... | collective-permute-start | bytes 737288 | tf_op jit(solution)/shard_map/ppermute | solution.py:261
  5.8 2.2 %collective-permute-start.8 = (bf16[160,768]{1,0:T(8,128)(2,1)S(1)}, bf16[160,768]{1,0:T(8,128)(2,1)S(1)}, u32[]{:S(2)}, u32[]{:S(2)}) collective-permute-start(bf16[160,768]{1,0:T(8,128)(2,1)S(1)} %pad_maximum_fusion.1), channel_id=1, source_target_pairs={{0,128},{128,0},{1,129},{129,1},{2,130},{130,2},{3,131},{131,3},{4... | collective-permute-start | bytes 737288 | tf_op jit(solution)/shard_map/ppermute | solution.py:289
  9.0 3.3 %collective-permute-start = (bf16[160,768]{1,0:T(8,128)(2,1)S(1)}, bf16[160,768]{1,0:T(8,128)(2,1)S(1)}, u32[]{:S(2)}, u32[]{:S(2)}) collective-permute-start(bf16[160,768]{1,0:T(8,128)(2,1)S(1)} %pad_maximum_fusion.3.refs_3_), channel_id=1, source_target_pairs={{0,16},{16,32},{32,48},{48,64},{64,80},{80,96},{96,112},{112,0},{1... | collective-permute-start | bytes 737288 | tf_op jit(solution)/shard_map/ppermute | solution.py:261
  13.4 1.4 %collective-permute-done.8 = bf16[160,768]{1,0:T(8,128)(2,1)S(1)} collective-permute-done((bf16[160,768]{1,0:T(8,128)(2,1)S(1)}, bf16[160,768]{1,0:T(8,128)(2,1)S(1)}, u32[]{:S(2)}, u32[]{:S(2)}) %collective-permute-start.8) | collective-permute-done | bytes 245792 | tf_op jit(solution)/shard_map/ppermute | solution.py:289
  15.0 3.0 %collective-permute-start.6 = (bf16[160,768]{1,0:T(8,128)(2,1)S(1)}, bf16[160,768]{1,0:T(8,128)(2,1)S(1)}, u32[]{:S(2)}, u32[]{:S(2)}) collective-permute-start(bf16[160,768]{1,0:T(8,128)(2,1)S(1)} %collective-permute-done.2.refs_4_), channel_id=1, source_target_pairs={{0,16},{16,32},{32,48},{48,64},{64,80},{80,96},{96,112},{112,0},{1... | collective-permute-start | bytes 737288 | tf_op jit(solution)/shard_map/ppermute | solution.py:261
  18.0 2.1 %collective-permute-done.1.refs_7_ = bf16[160,768]{1,0:T(8,128)(2,1)S(1)} collective-permute-done((bf16[160,768]{1,0:T(8,128)(2,1)S(1)}, bf16[160,768]{1,0:T(8,128)(2,1)S(1)}, u32[]{:S(2)}, u32[]{:S(2)}) %collective-permute-start.1) | collective-permute-done | bytes 245792 | tf_op jit(solution)/shard_map/ppermute | solution.py:261
  22.1 2.1 %collective-permute-done.6.refs_2_ = bf16[160,768]{1,0:T(8,128)(2,1)S(1)} collective-permute-done((bf16[160,768]{1,0:T(8,128)(2,1)S(1)}, bf16[160,768]{1,0:T(8,128)(2,1)S(1)}, u32[]{:S(2)}, u32[]{:S(2)}) %collective-permute-start.6) | collective-permute-done | bytes 245792 | tf_op jit(solution)/shard_map/ppermute | solution.py:261
  24.3 3.7 %collective-permute-done.7.refs_4_ = bf16[160,768]{1,0:T(8,128)(2,1)S(1)} collective-permute-done((bf16[160,768]{1,0:T(8,128)(2,1)S(1)}, bf16[160,768]{1,0:T(8,128)(2,1)S(1)}, u32[]{:S(2)}, u32[]{:S(2)}) %collective-permute-start.7) | collective-permute-done | bytes 245792 | tf_op jit(solution)/shard_map/ppermute | solution.py:261
  28.0 2.0 %collective-permute-start.11 = (bf16[160,768]{1,0:T(8,128)(2,1)S(1)}, bf16[160,768]{1,0:T(8,128)(2,1)S(1)}, u32[]{:S(2)}, u32[]{:S(2)}) collective-permute-start(bf16[160,768]{1,0:T(8,128)(2,1)S(1)} %collective-permute-done.7.refs_4_), channel_id=1, source_target_pairs={{0,112},{16,0},{32,16},{48,32},{64,48},{80,64},{96,80},{112,96},{1... | collective-permute-start | bytes 737288 | tf_op jit(solution)/shard_map/ppermute | solution.py:261
  30.6 2.7 %collective-permute-done.5.refs_5_ = bf16[160,768]{1,0:T(8,128)(2,1)S(1)} collective-permute-done((bf16[160,768]{1,0:T(8,128)(2,1)S(1)}, bf16[160,768]{1,0:T(8,128)(2,1)S(1)}, u32[]{:S(2)}, u32[]{:S(2)}) %collective-permute-start.5) | collective-permute-done | bytes 245792 | tf_op jit(solution)/shard_map/ppermute | solution.py:261
  33.8 1.5 %collective-permute-start.14 = (bf16[160,768]{1,0:T(8,128)(2,1)S(1)}, bf16[160,768]{1,0:T(8,128)(2,1)S(1)}, u32[]{:S(2)}, u32[]{:S(2)}) collective-permute-start(bf16[160,768]{1,0:T(8,128)(2,1)S(1)} %collective-permute-done.5.refs_5_), channel_id=1, source_target_pairs={{0,112},{16,0},{32,16},{48,32},{64,48},{80,64},{96,80},{112,96},{1... | collective-permute-start | bytes 737288 | tf_op jit(solution)/shard_map/ppermute | solution.py:261
  35.3 2.7 %attend.5 = (f32[320,1920]{1,0:T(8,128)S(1)}, f32[320,1920]{1,0:T(8,128)S(1)}) custom-call(bf16[320,768]{1,0:T(8,128)(2,1)S(1)} %pad_maximum_fusion.refs_0_, bf16[320,768]{1,0:T(8,128)(2,1)S(1)} %collective-permute-done.9.refs_1_.refs_0_, bf16[160,768]{1,0:T(8,128)(2,1)S(1)} %pad_maximum_fusion.2.refs_2_, bf16[160,768]{1,0:T(8,128)(2,1)S(1)} %pad_maximum_fusion.3.refs_3_, ...), custom_call_target="tpu_custom_call" | custom-call | flops 1887436800 | bytes 7372800 | tf_op jit(solution)/shard_map/attend/pallas_call | solution.py:27
  39.8 2.7 %attend.6 = (f32[320,1920]{1,0:T(8,128)S(1)}, f32[320,1920]{1,0:T(8,128)S(1)}) custom-call(bf16[320,768]{1,0:T(8,128)(2,1)S(1)} %pad_maximum_fusion.refs_0_, bf16[320,768]{1,0:T(8,128)(2,1)S(1)} %collective-permute-done.9.refs_1_.refs_0_, bf16[160,768]{1,0:T(8,128)(2,1)S(1)} %collective-permute-done.6.refs_2_, ...), custom_call_target="tpu_custom_call" | custom-call | flops 1258291200 | bytes 11796480 | tf_op jit(solution)/shard_map/attend/pallas_call | solution.py:27
  43.3 2.7 %attend.7 = (f32[320,1920]{1,0:T(8,128)S(1)}, f32[320,1920]{1,0:T(8,128)S(1)}) custom-call(bf16[320,768]{1,0:T(8,128)(2,1)S(1)} %pad_maximum_fusion.refs_0_, bf16[320,768]{1,0:T(8,128)(2,1)S(1)} %collective-permute-done.9.refs_1_.refs_0_, bf16[160,768]{1,0:T(8,128)(2,1)S(1)} %collective-permute-done.10.refs_2_, ...), custom_call_target="tpu_custom_call" | custom-call | flops 1258291200 | bytes 11796480 | tf_op jit(solution)/shard_map/attend/pallas_call | solution.py:27
  46.0 5.3 %collective-permute-done.15.refs_2_ = bf16[160,768]{1,0:T(8,128)(2,1)S(1)} collective-permute-done((bf16[160,768]{1,0:T(8,128)(2,1)S(1)}, bf16[160,768]{1,0:T(8,128)(2,1)S(1)}, u32[]{:S(2)}, u32[]{:S(2)}) %collective-permute-start.15) | collective-permute-done | bytes 245792 | tf_op jit(solution)/shard_map/ppermute | solution.py:261
  51.3 1.4 %attend.9 = bf16[320,896]{1,0:T(8,128)(2,1)S(1)} custom-call(bf16[320,768]{1,0:T(8,128)(2,1)S(1)} %collective-permute-done.9.refs_1_.refs_0_, bf16[160,768]{1,0:T(8,128)(2,1)S(1)} %collective-permute-done.12.refs_1_, bf16[160,768]{1,0:T(8,128)(2,1)S(1)} %collective-permute-done.15.refs_2_, f32[320,1920]{1,0:T(8,128)S(1)} %get-tuple-element.84.refs_3_), custom_call_target="tpu_custom_call" | custom-call | flops 314572800 | bytes 4014080 | tf_op jit(solution)/shard_map/attend/pallas_call | solution.py:27
  55.4 1.9 %collective-permute-start.18 = (bf16[160,896]{1,0:T(8,128)(2,1)S(1)}, bf16[160,896]{1,0:T(8,128)(2,1)S(1)}, u32[]{:S(2)}, u32[]{:S(2)}) collective-permute-start(bf16[160,896]{1,0:T(8,128)(2,1)S(1)} %join.3), channel_id=1, source_target_pairs={{0,128},{128,0},{1,129},{129,1},{2,130},{130,2},{3,131},{131,3},{4... | collective-permute-start | bytes 860168 | tf_op jit(solution)/shard_map/ppermute | solution.py:327
  57.9 8.1 %collective-permute-done.18.b_ref = bf16[160,896]{1,0:T(8,128)(2,1)S(1)} collective-permute-done((bf16[160,896]{1,0:T(8,128)(2,1)S(1)}, bf16[160,896]{1,0:T(8,128)(2,1)S(1)}, u32[]{:S(2)}, u32[]{:S(2)}) %collective-permute-start.18) | collective-permute-done | bytes 286752 | tf_op jit(solution)/shard_map/ppermute | solution.py:327
  66.8 7.1 %collective-permute-done.19.beside_ref = bf16[320,384]{1,0:T(8,128)(2,1)S(1)} collective-permute-done((bf16[320,384]{1,0:T(8,128)(2,1)S(1)}, bf16[320,384]{1,0:T(8,128)(2,1)S(1)}, u32[]{:S(2)}, u32[]{:S(2)}) %collective-permute-start.19) | collective-permute-done | bytes 245792 | tf_op jit(solution)/shard_map/ppermute | solution.py:330
  73.9 2.5 %project.1 = (bf16[320,384]{1,0:T(8,128)(2,1)S(1)}, bf16[320,384]{1,0:T(8,128)(2,1)S(1)}, bf16[320,384]{1,0:T(8,128)(2,1)S(1)}, bf16[320,384]{1,0:T(8,128)(2,1)S(1)}) custom-call(s32[3]{0:T(128)S(1)} %pad_add_fusion.at_ref, bf16[320,384]{1,0:T(8,128)(2,1)S(1)} %attended.1.own_ref, bf16[320,384]{1,0:T(8,128)(2,1)S(1)} %collective-permute-done.19.beside_ref, ...), custom_call_target="tpu_custom_call" | custom-call | tf_op jit(solution)/shard_map/project/pallas_call | solution.py:239
  76.4 1.7 %collective-permute-start.21 = (bf16[320,384]{1,0:T(8,128)(2,1)S(1)}, bf16[320,384]{1,0:T(8,128)(2,1)S(1)}, u32[]{:S(2)}, u32[]{:S(2)}) collective-permute-start(bf16[320,384]{1,0:T(8,128)(2,1)S(1)} %get-tuple-element.87), channel_id=1, source_target_pairs={{0,1},{1,2},{2,3},{3,0},{4,5},{5,6},{6,7},{7,4},{8,9},{9,10},{10,1... | collective-permute-start | bytes 737288 | tf_op jit(solution)/shard_map/ppermute | solution.py:334
  78.0 2.9 %collective-permute-start.22 = (bf16[320,384]{1,0:T(8,128)(2,1)S(1)}, bf16[320,384]{1,0:T(8,128)(2,1)S(1)}, u32[]{:S(2)}, u32[]{:S(2)}) collective-permute-start(bf16[320,384]{1,0:T(8,128)(2,1)S(1)} %get-tuple-element.88), channel_id=1, source_target_pairs={{0,2},{1,3},{2,0},{3,1},{4,6},{5,7},{6,4},{7,5},{8,10},{9,11},{10,... | collective-permute-start | bytes 737288 | tf_op jit(solution)/shard_map/ppermute | solution.py:334
  82.3 3.2 %collective-permute-done.21.refs_1_ = bf16[320,384]{1,0:T(8,128)(2,1)S(1)} collective-permute-done((bf16[320,384]{1,0:T(8,128)(2,1)S(1)}, bf16[320,384]{1,0:T(8,128)(2,1)S(1)}, u32[]{:S(2)}, u32[]{:S(2)}) %collective-permute-start.21) | collective-permute-done | bytes 245792 | tf_op jit(solution)/shard_map/ppermute | solution.py:334
  85.5 5.1 %collective-permute-done.22.refs_2_ = bf16[320,384]{1,0:T(8,128)(2,1)S(1)} collective-permute-done((bf16[320,384]{1,0:T(8,128)(2,1)S(1)}, bf16[320,384]{1,0:T(8,128)(2,1)S(1)}, u32[]{:S(2)}, u32[]{:S(2)}) %collective-permute-start.22) | collective-permute-done | bytes 245792 | tf_op jit(solution)/shard_map/ppermute | solution.py:334
  (42 shorter events, 16.1 us)
Async XLA Ops:
  1.6 13.3 %collective-permute-start.2 = (bf16[160,768]{1,0:T(8,128)(2,1)S(1)}, bf16[160,768]{1,0:T(8,128)(2,1)S(1)}, u32[]{:S(2)}, u32[]{:S(2)}) collective-permute-start(bf16[160,768]{1,0:T(8,128)(2,1)S(1)} %pad_maximum_fusion.2.refs_2_), channel_id=1, source_target_pairs={{0,16},{16,32},{32,48},{48,64},{64,80},{80,96},{96,112},{112,0},{1... | collective-permute-start | bytes 737288 | tf_op jit(solution)/shard_map/ppermute | solution.py:261
  4.8 13.2 %collective-permute-start.3 = (bf16[160,768]{1,0:T(8,128)(2,1)S(1)}, bf16[160,768]{1,0:T(8,128)(2,1)S(1)}, u32[]{:S(2)}, u32[]{:S(2)}) collective-permute-start(bf16[160,768]{1,0:T(8,128)(2,1)S(1)} %pad_maximum_fusion.2.refs_2_), channel_id=1, source_target_pairs={{0,112},{16,0},{32,16},{48,32},{64,48},{80,64},{96,80},{112,96},{1... | collective-permute-start | bytes 737288 | tf_op jit(solution)/shard_map/ppermute | solution.py:261
  5.8 9.0 %collective-permute-start.8 = (bf16[160,768]{1,0:T(8,128)(2,1)S(1)}, bf16[160,768]{1,0:T(8,128)(2,1)S(1)}, u32[]{:S(2)}, u32[]{:S(2)}) collective-permute-start(bf16[160,768]{1,0:T(8,128)(2,1)S(1)} %pad_maximum_fusion.1), channel_id=1, source_target_pairs={{0,128},{128,0},{1,129},{129,1},{2,130},{130,2},{3,131},{131,3},{4... | collective-permute-start | bytes 737288 | tf_op jit(solution)/shard_map/ppermute | solution.py:289
  9.0 9.0 %collective-permute-start = (bf16[160,768]{1,0:T(8,128)(2,1)S(1)}, bf16[160,768]{1,0:T(8,128)(2,1)S(1)}, u32[]{:S(2)}, u32[]{:S(2)}) collective-permute-start(bf16[160,768]{1,0:T(8,128)(2,1)S(1)} %pad_maximum_fusion.3.refs_3_), channel_id=1, source_target_pairs={{0,16},{16,32},{32,48},{48,64},{64,80},{80,96},{96,112},{112,0},{1... | collective-permute-start | bytes 737288 | tf_op jit(solution)/shard_map/ppermute | solution.py:261
  12.3 7.8 %collective-permute-start.1 = (bf16[160,768]{1,0:T(8,128)(2,1)S(1)}, bf16[160,768]{1,0:T(8,128)(2,1)S(1)}, u32[]{:S(2)}, u32[]{:S(2)}) collective-permute-start(bf16[160,768]{1,0:T(8,128)(2,1)S(1)} %pad_maximum_fusion.3.refs_3_), channel_id=1, source_target_pairs={{0,112},{16,0},{32,16},{48,32},{64,48},{80,64},{96,80},{112,96},{1... | collective-permute-start | bytes 737288 | tf_op jit(solution)/shard_map/ppermute | solution.py:261
  14.9 18.4 %collective-permute-start.9 = (bf16[320,768]{1,0:T(8,128)(2,1)S(1)}, bf16[320,768]{1,0:T(8,128)(2,1)S(1)}, u32[]{:S(2)}, u32[]{:S(2)}) collective-permute-start(bf16[320,768]{1,0:T(8,128)(2,1)S(1)} %pad_maximum_fusion.refs_0_), channel_id=1, source_target_pairs={{0,8},{8,0},{1,9},{9,1},{2,10},{10,2},{3,11},{11,3},{4,12},{12,4},... | collective-permute-start | bytes 1474568 | tf_op jit(solution)/shard_map/ppermute | solution.py:292
  15.0 9.3 %collective-permute-start.6 = (bf16[160,768]{1,0:T(8,128)(2,1)S(1)}, bf16[160,768]{1,0:T(8,128)(2,1)S(1)}, u32[]{:S(2)}, u32[]{:S(2)}) collective-permute-start(bf16[160,768]{1,0:T(8,128)(2,1)S(1)} %collective-permute-done.2.refs_4_), channel_id=1, source_target_pairs={{0,16},{16,32},{32,48},{48,64},{64,80},{80,96},{96,112},{112,0},{1... | collective-permute-start | bytes 737288 | tf_op jit(solution)/shard_map/ppermute | solution.py:261
  18.0 10.0 %collective-permute-start.7 = (bf16[160,768]{1,0:T(8,128)(2,1)S(1)}, bf16[160,768]{1,0:T(8,128)(2,1)S(1)}, u32[]{:S(2)}, u32[]{:S(2)}) collective-permute-start(bf16[160,768]{1,0:T(8,128)(2,1)S(1)} %collective-permute-done.3.refs_6_), channel_id=1, source_target_pairs={{0,112},{16,0},{32,16},{48,32},{64,48},{80,64},{96,80},{112,96},{1... | collective-permute-start | bytes 737288 | tf_op jit(solution)/shard_map/ppermute | solution.py:261
  20.1 9.9 %collective-permute-start.4 = (bf16[160,768]{1,0:T(8,128)(2,1)S(1)}, bf16[160,768]{1,0:T(8,128)(2,1)S(1)}, u32[]{:S(2)}, u32[]{:S(2)}) collective-permute-start(bf16[160,768]{1,0:T(8,128)(2,1)S(1)} %collective-permute-done.refs_5_), channel_id=1, source_target_pairs={{0,16},{16,32},{32,48},{48,64},{64,80},{80,96},{96,112},{112,0},{1... | collective-permute-start | bytes 737288 | tf_op jit(solution)/shard_map/ppermute | solution.py:261
  21.2 12.0 %collective-permute-start.5 = (bf16[160,768]{1,0:T(8,128)(2,1)S(1)}, bf16[160,768]{1,0:T(8,128)(2,1)S(1)}, u32[]{:S(2)}, u32[]{:S(2)}) collective-permute-start(bf16[160,768]{1,0:T(8,128)(2,1)S(1)} %collective-permute-done.1.refs_7_), channel_id=1, source_target_pairs={{0,112},{16,0},{32,16},{48,32},{64,48},{80,64},{96,80},{112,96},{1... | collective-permute-start | bytes 737288 | tf_op jit(solution)/shard_map/ppermute | solution.py:261
  28.0 10.0 %collective-permute-start.10 = (bf16[160,768]{1,0:T(8,128)(2,1)S(1)}, bf16[160,768]{1,0:T(8,128)(2,1)S(1)}, u32[]{:S(2)}, u32[]{:S(2)}) collective-permute-start(bf16[160,768]{1,0:T(8,128)(2,1)S(1)} %collective-permute-done.6.refs_2_), channel_id=1, source_target_pairs={{0,16},{16,32},{32,48},{48,64},{64,80},{80,96},{96,112},{112,0},{1... | collective-permute-start | bytes 737288 | tf_op jit(solution)/shard_map/ppermute | solution.py:261
  28.0 10.5 %collective-permute-start.11 = (bf16[160,768]{1,0:T(8,128)(2,1)S(1)}, bf16[160,768]{1,0:T(8,128)(2,1)S(1)}, u32[]{:S(2)}, u32[]{:S(2)}) collective-permute-start(bf16[160,768]{1,0:T(8,128)(2,1)S(1)} %collective-permute-done.7.refs_4_), channel_id=1, source_target_pairs={{0,112},{16,0},{32,16},{48,32},{64,48},{80,64},{96,80},{112,96},{1... | collective-permute-start | bytes 737288 | tf_op jit(solution)/shard_map/ppermute | solution.py:261
  30.0 16.0 %collective-permute-start.16 = (bf16[384,768]{1,0:T(8,128)(2,1)S(1)}, bf16[384,768]{1,0:T(8,128)(2,1)S(1)}, u32[]{:S(2)}, u32[]{:S(2)}) collective-permute-start(bf16[384,768]{1,0:T(8,128)(2,1)S(1)} %constant_dynamic-slice_fusion), channel_id=1, source_target_pairs={{0,4},{4,0},{1,5},{5,1},{2,6},{6,2},{3,7},{7,3},{8,12},{12,8},{9,1... | collective-permute-start | bytes 1769480 | tf_op jit(solution)/shard_map/ppermute | solution.py:303
  33.3 9.2 %collective-permute-start.13 = (bf16[160,768]{1,0:T(8,128)(2,1)S(1)}, bf16[160,768]{1,0:T(8,128)(2,1)S(1)}, u32[]{:S(2)}, u32[]{:S(2)}) collective-permute-start(bf16[160,768]{1,0:T(8,128)(2,1)S(1)} %collective-permute-done.4.refs_3_), channel_id=1, source_target_pairs={{0,16},{16,32},{32,48},{48,64},{64,80},{80,96},{96,112},{112,0},{1... | collective-permute-start | bytes 737288 | tf_op jit(solution)/shard_map/ppermute | solution.py:261
  33.8 9.2 %collective-permute-start.14 = (bf16[160,768]{1,0:T(8,128)(2,1)S(1)}, bf16[160,768]{1,0:T(8,128)(2,1)S(1)}, u32[]{:S(2)}, u32[]{:S(2)}) collective-permute-start(bf16[160,768]{1,0:T(8,128)(2,1)S(1)} %collective-permute-done.5.refs_5_), channel_id=1, source_target_pairs={{0,112},{16,0},{32,16},{48,32},{64,48},{80,64},{96,80},{112,96},{1... | collective-permute-start | bytes 737288 | tf_op jit(solution)/shard_map/ppermute | solution.py:261
  38.5 7.5 %collective-permute-start.12 = (bf16[160,768]{1,0:T(8,128)(2,1)S(1)}, bf16[160,768]{1,0:T(8,128)(2,1)S(1)}, u32[]{:S(2)}, u32[]{:S(2)}) collective-permute-start(bf16[160,768]{1,0:T(8,128)(2,1)S(1)} %collective-permute-done.10.refs_2_), channel_id=1, source_target_pairs={{0,16},{16,32},{32,48},{48,64},{64,80},{80,96},{96,112},{112,0},{1... | collective-permute-start | bytes 737288 | tf_op jit(solution)/shard_map/ppermute | solution.py:261
  43.0 8.3 %collective-permute-start.15 = (bf16[160,768]{1,0:T(8,128)(2,1)S(1)}, bf16[160,768]{1,0:T(8,128)(2,1)S(1)}, u32[]{:S(2)}, u32[]{:S(2)}) collective-permute-start(bf16[160,768]{1,0:T(8,128)(2,1)S(1)} %collective-permute-done.14.refs_5_), channel_id=1, source_target_pairs={{0,112},{16,0},{32,16},{48,32},{64,48},{80,64},{96,80},{112,96},{1... | collective-permute-start | bytes 737288 | tf_op jit(solution)/shard_map/ppermute | solution.py:261
  52.7 2.1 %collective-permute-start.17 = (bf16[320,896]{1,0:T(8,128)(2,1)S(1)}, bf16[320,896]{1,0:T(8,128)(2,1)S(1)}, u32[]{:S(2)}, u32[]{:S(2)}) collective-permute-start(bf16[320,896]{1,0:T(8,128)(2,1)S(1)} %attend.9), channel_id=1, source_target_pairs={{0,8},{8,0},{1,9},{9,1},{2,10},{10,2},{3,11},{11,3},{4,12},{12,4},... | collective-permute-start | bytes 1720328 | tf_op jit(solution)/shard_map/ppermute | solution.py:318
  52.8 14.0 %collective-permute-start.20 = (bf16[384,768]{1,0:T(8,128)(2,1)S(1)}, bf16[384,768]{1,0:T(8,128)(2,1)}, u32[]{:S(2)}, u32[]{:S(2)}) collective-permute-start(bf16[384,768]{1,0:T(8,128)(2,1)S(1)} %collective-permute-done.16.w_mine_ref), channel_id=1, source_target_pairs={{0,8},{8,0},{1,9},{9,1},{2,10},{10,2},{3,11},{11,3},{4,12},{12,4},... | collective-permute-start | bytes 1769480 | tf_op jit(solution)/shard_map/ppermute | solution.py:331
  55.4 10.6 %collective-permute-start.18 = (bf16[160,896]{1,0:T(8,128)(2,1)S(1)}, bf16[160,896]{1,0:T(8,128)(2,1)S(1)}, u32[]{:S(2)}, u32[]{:S(2)}) collective-permute-start(bf16[160,896]{1,0:T(8,128)(2,1)S(1)} %join.3), channel_id=1, source_target_pairs={{0,128},{128,0},{1,129},{129,1},{2,130},{130,2},{3,131},{131,3},{4... | collective-permute-start | bytes 860168 | tf_op jit(solution)/shard_map/ppermute | solution.py:327
  66.5 7.4 %collective-permute-start.19 = (bf16[320,384]{1,0:T(8,128)(2,1)S(1)}, bf16[320,384]{1,0:T(8,128)(2,1)S(1)}, u32[]{:S(2)}, u32[]{:S(2)}) collective-permute-start(bf16[320,384]{1,0:T(8,128)(2,1)S(1)} %attended.1.own_ref), channel_id=1, source_target_pairs={{0,4},{4,0},{1,5},{5,1},{2,6},{6,2},{3,7},{7,3},{8,12},{12,8},{9,1... | collective-permute-start | bytes 737288 | tf_op jit(solution)/shard_map/ppermute | solution.py:330
  76.4 9.1 %collective-permute-start.21 = (bf16[320,384]{1,0:T(8,128)(2,1)S(1)}, bf16[320,384]{1,0:T(8,128)(2,1)S(1)}, u32[]{:S(2)}, u32[]{:S(2)}) collective-permute-start(bf16[320,384]{1,0:T(8,128)(2,1)S(1)} %get-tuple-element.87), channel_id=1, source_target_pairs={{0,1},{1,2},{2,3},{3,0},{4,5},{5,6},{6,7},{7,4},{8,9},{9,10},{10,1... | collective-permute-start | bytes 737288 | tf_op jit(solution)/shard_map/ppermute | solution.py:334
  78.0 12.5 %collective-permute-start.22 = (bf16[320,384]{1,0:T(8,128)(2,1)S(1)}, bf16[320,384]{1,0:T(8,128)(2,1)S(1)}, u32[]{:S(2)}, u32[]{:S(2)}) collective-permute-start(bf16[320,384]{1,0:T(8,128)(2,1)S(1)} %get-tuple-element.88), channel_id=1, source_target_pairs={{0,2},{1,3},{2,0},{3,1},{4,6},{5,7},{6,4},{7,5},{8,10},{9,11},{10,... | collective-permute-start | bytes 737288 | tf_op jit(solution)/shard_map/ppermute | solution.py:334
  80.9 9.6 %collective-permute-start.23 = (bf16[320,384]{1,0:T(8,128)(2,1)S(1)}, bf16[320,384]{1,0:T(8,128)(2,1)S(1)}, u32[]{:S(2)}, u32[]{:S(2)}) collective-permute-start(bf16[320,384]{1,0:T(8,128)(2,1)S(1)} %get-tuple-element.89), channel_id=1, source_target_pairs={{0,3},{1,0},{2,1},{3,2},{4,7},{5,4},{6,5},{7,6},{8,11},{9,8},{10,9... | collective-permute-start | bytes 737288 | tf_op jit(solution)/shard_map/ppermute | solution.py:334
  (1 other events, 19.2 us)

commit v3 on v2

--- a/solution.py
+++ b/solution.py
@@ -220,6 +220,7 @@
 def project_kernel(at_ref, own_ref, beside_ref, w_ref, w_mine_ref, w_other_ref, *outs):
     xl, y, core = at_ref[0], at_ref[1], at_ref[2]
     columns = outs[0].shape[1]
+    both = jnp.concatenate([own_ref[...], beside_ref[...]], axis=1)
     for step, out in enumerate(outs):
         target = lax.rem(y + step, len(outs))
         fetched_by, place = lax.div(target, 2), lax.rem(target, 2)
@@ -228,10 +229,8 @@
         w_beside = jnp.where(
             fetched_by == core, w_mine_ref[:, first_beside], w_other_ref[:, first_beside]
         )
-        total = jnp.dot(
-            own_ref[...], w_ref[:, pl.ds(first, columns)], preferred_element_type=jnp.float32
-        ) + jnp.dot(beside_ref[...], w_beside, preferred_element_type=jnp.float32)
-        out[...] = total.astype(out.dtype)
+        w_both = jnp.concatenate([w_ref[:, pl.ds(first, columns)], w_beside], axis=0)
+        out[...] = jnp.dot(both, w_both, preferred_element_type=jnp.float32).astype(out.dtype)
 
 
 def project(place, own, beside, w_out, w_mine, w_other):
@@ -287,8 +286,8 @@
         w_out, ((1 - place[0]) * 2 + place[2]) * quarter, quarter, axis=1
     )
     far_q = lax.ppermute(own_q, "xh", SWAP)
-    wanted, far_q = lax.optimization_barrier((wanted, far_q))
     stack = jnp.concatenate([own_q, far_q], axis=0)
+    wanted, stack = lax.optimization_barrier((wanted, stack))
     stacks = [stack, lax.ppermute(stack, "core", SWAP)]
 
     k_steps.append(around(k_steps[1]))
@@ -332,7 +331,7 @@
     parts = list(project(place, attended, beside_attended, w_out, w_mine, w_other))
     parts = parts[:1] + [
         lax.ppermute(part, "y", [(i, (i + step) % 4) for i in range(4)])
-        for step, part in enumerate(parts[1:], 1)
+        for step, part in ((2, parts[2]), (1, parts[1]), (3, parts[3]))
     ]
     return tuple(call(total_kernel, "total", [shape(rows, width)] * 2, parts))
 

time: 91.6 us -> 90.8 us (level)
  waiting for transfers between devices: 42.1 us -> 40.9 us
    ppermute x3, waiting for transfers between devices: 8.27 us -> 7.06 us  [on_device(): lax.ppermute(part, 'y', [(i, (i + step) % 4) for i in range(4)])]
  transfers between devices with their start and end apart: 24 -> 24, of which waited for: 13 -> 14; matrix products, arithmetic and copies ran while one was open for 3% -> 4% of each run, Pallas kernels for 12% -> 12%
where the time goes in v3:
time: 90.8 us; the launch traced here: 90.6 us
  waiting for transfers between devices  40.9 us (45%)
  starting transfers between devices  29.2 us (32%)
  Pallas kernels  15.5 us (17%)
  other arithmetic  3.06 us (3%)
  local copies, waits for them, and re-layouts  1.11 us (1%)
    ppermute x14, starting transfers between devices, along_z(): return lax.ppermute(x, 'z', [(i, (i + step) % 8) for i in range(8)])  17.2 us
    ppermute x14, waiting for transfers between devices, along_z(): return lax.ppermute(x, 'z', [(i, (i + step) % 8) for i in range(8)])  17.1 us
    pallas_call x9, Pallas kernels, call(): pl.pallas_call(kernel, in_specs=[vmem()] * len(args), out_specs=[vmem()]...  13.2 us
    ppermute x1, waiting for transfers between devices, on_device(): from_far = lax.ppermute(join(rows), 'xh', SWAP)  8.08 us
    ppermute x1, waiting for transfers between devices, on_device(): beside_attended = lax.ppermute(attended, 'xl', SWAP)  7.12 us
    ppermute x3, waiting for transfers between devices, on_device(): lax.ppermute(part, 'y', [(i, (i + step) % 4) for i in range(4)])  7.06 us
    ppermute x3, starting transfers between devices, on_device(): lax.ppermute(part, 'y', [(i, (i + step) % 4) for i in range(4)])  6.52 us
    max x3, other arithmetic, beside(): jnp.maximum(lax.pad(left, low, [(0, 0, 0), (0, width, 0)]), lax.pad(right...  2.95 us
  transfers between devices with their start and end apart: 24, of which 14 were waited for; matrix products, arithmetic and copies ran while one was open for 4% of the time, Pallas kernels for 12%

profile of v3, /device:TPU:98, one launch (start us, length us, event | category | flops | bytes accessed | tf_op | source)
XLA Modules:
  0.0 90.6 jit_solution(12399570409857640311)
XLA Ops:
  1.6 3.2 %collective-permute-start.2 = (bf16[160,768]{1,0:T(8,128)(2,1)S(1)}, bf16[160,768]{1,0:T(8,128)(2,1)S(1)}, u32[]{:S(2)}, u32[]{:S(2)}) collective-permute-start(bf16[160,768]{1,0:T(8,128)(2,1)S(1)} %pad_maximum_fusion.2.refs_2_), channel_id=1, source_target_pairs={{0,16},{16,32},{32,48},{48,64},{64,80},{80,96},{96,112},{112,0},{1... | collective-permute-start | bytes 737288 | tf_op jit(solution)/shard_map/ppermute | solution.py:260
  5.8 2.2 %collective-permute-start.8 = (bf16[160,768]{1,0:T(8,128)(2,1)S(1)}, bf16[160,768]{1,0:T(8,128)(2,1)S(1)}, u32[]{:S(2)}, u32[]{:S(2)}) collective-permute-start(bf16[160,768]{1,0:T(8,128)(2,1)S(1)} %pad_maximum_fusion.1), channel_id=1, source_target_pairs={{0,128},{128,0},{1,129},{129,1},{2,130},{130,2},{3,131},{131,3},{4... | collective-permute-start | bytes 737288 | tf_op jit(solution)/shard_map/ppermute | solution.py:288
  9.0 3.3 %collective-permute-start = (bf16[160,768]{1,0:T(8,128)(2,1)S(1)}, bf16[160,768]{1,0:T(8,128)(2,1)S(1)}, u32[]{:S(2)}, u32[]{:S(2)}) collective-permute-start(bf16[160,768]{1,0:T(8,128)(2,1)S(1)} %pad_maximum_fusion.3.refs_3_), channel_id=1, source_target_pairs={{0,16},{16,32},{32,48},{48,64},{64,80},{80,96},{96,112},{112,0},{1... | collective-permute-start | bytes 737288 | tf_op jit(solution)/shard_map/ppermute | solution.py:260
  13.4 1.4 %collective-permute-done.8 = bf16[160,768]{1,0:T(8,128)(2,1)S(1)} collective-permute-done((bf16[160,768]{1,0:T(8,128)(2,1)S(1)}, bf16[160,768]{1,0:T(8,128)(2,1)S(1)}, u32[]{:S(2)}, u32[]{:S(2)}) %collective-permute-start.8) | collective-permute-done | bytes 245792 | tf_op jit(solution)/shard_map/ppermute | solution.py:288
  15.0 3.0 %collective-permute-start.6 = (bf16[160,768]{1,0:T(8,128)(2,1)S(1)}, bf16[160,768]{1,0:T(8,128)(2,1)S(1)}, u32[]{:S(2)}, u32[]{:S(2)}) collective-permute-start(bf16[160,768]{1,0:T(8,128)(2,1)S(1)} %collective-permute-done.2.refs_4_), channel_id=1, source_target_pairs={{0,16},{16,32},{32,48},{48,64},{64,80},{80,96},{96,112},{112,0},{1... | collective-permute-start | bytes 737288 | tf_op jit(solution)/shard_map/ppermute | solution.py:260
  18.0 2.1 %collective-permute-done.1.refs_7_ = bf16[160,768]{1,0:T(8,128)(2,1)S(1)} collective-permute-done((bf16[160,768]{1,0:T(8,128)(2,1)S(1)}, bf16[160,768]{1,0:T(8,128)(2,1)S(1)}, u32[]{:S(2)}, u32[]{:S(2)}) %collective-permute-start.1) | collective-permute-done | bytes 245792 | tf_op jit(solution)/shard_map/ppermute | solution.py:260
  22.1 2.1 %collective-permute-done.6.refs_2_ = bf16[160,768]{1,0:T(8,128)(2,1)S(1)} collective-permute-done((bf16[160,768]{1,0:T(8,128)(2,1)S(1)}, bf16[160,768]{1,0:T(8,128)(2,1)S(1)}, u32[]{:S(2)}, u32[]{:S(2)}) %collective-permute-start.6) | collective-permute-done | bytes 245792 | tf_op jit(solution)/shard_map/ppermute | solution.py:260
  24.3 3.7 %collective-permute-done.7.refs_4_ = bf16[160,768]{1,0:T(8,128)(2,1)S(1)} collective-permute-done((bf16[160,768]{1,0:T(8,128)(2,1)S(1)}, bf16[160,768]{1,0:T(8,128)(2,1)S(1)}, u32[]{:S(2)}, u32[]{:S(2)}) %collective-permute-start.7) | collective-permute-done | bytes 245792 | tf_op jit(solution)/shard_map/ppermute | solution.py:260
  28.0 2.0 %collective-permute-start.11 = (bf16[160,768]{1,0:T(8,128)(2,1)S(1)}, bf16[160,768]{1,0:T(8,128)(2,1)S(1)}, u32[]{:S(2)}, u32[]{:S(2)}) collective-permute-start(bf16[160,768]{1,0:T(8,128)(2,1)S(1)} %collective-permute-done.7.refs_4_), channel_id=1, source_target_pairs={{0,112},{16,0},{32,16},{48,32},{64,48},{80,64},{96,80},{112,96},{1... | collective-permute-start | bytes 737288 | tf_op jit(solution)/shard_map/ppermute | solution.py:260
  30.6 2.7 %collective-permute-done.5.refs_5_ = bf16[160,768]{1,0:T(8,128)(2,1)S(1)} collective-permute-done((bf16[160,768]{1,0:T(8,128)(2,1)S(1)}, bf16[160,768]{1,0:T(8,128)(2,1)S(1)}, u32[]{:S(2)}, u32[]{:S(2)}) %collective-permute-start.5) | collective-permute-done | bytes 245792 | tf_op jit(solution)/shard_map/ppermute | solution.py:260
  33.8 1.5 %collective-permute-start.14 = (bf16[160,768]{1,0:T(8,128)(2,1)S(1)}, bf16[160,768]{1,0:T(8,128)(2,1)S(1)}, u32[]{:S(2)}, u32[]{:S(2)}) collective-permute-start(bf16[160,768]{1,0:T(8,128)(2,1)S(1)} %collective-permute-done.5.refs_5_), channel_id=1, source_target_pairs={{0,112},{16,0},{32,16},{48,32},{64,48},{80,64},{96,80},{112,96},{1... | collective-permute-start | bytes 737288 | tf_op jit(solution)/shard_map/ppermute | solution.py:260
  35.3 2.7 %attend.5 = (f32[320,1920]{1,0:T(8,128)S(1)}, f32[320,1920]{1,0:T(8,128)S(1)}) custom-call(bf16[320,768]{1,0:T(8,128)(2,1)S(1)} %pad_maximum_fusion.refs_0_, bf16[320,768]{1,0:T(8,128)(2,1)S(1)} %collective-permute-done.9.refs_1_.refs_0_, bf16[160,768]{1,0:T(8,128)(2,1)S(1)} %pad_maximum_fusion.2.refs_2_, bf16[160,768]{1,0:T(8,128)(2,1)S(1)} %pad_maximum_fusion.3.refs_3_, ...), custom_call_target="tpu_custom_call" | custom-call | flops 1887436800 | bytes 7372800 | tf_op jit(solution)/shard_map/attend/pallas_call | solution.py:27
  39.8 2.7 %attend.6 = (f32[320,1920]{1,0:T(8,128)S(1)}, f32[320,1920]{1,0:T(8,128)S(1)}) custom-call(bf16[320,768]{1,0:T(8,128)(2,1)S(1)} %pad_maximum_fusion.refs_0_, bf16[320,768]{1,0:T(8,128)(2,1)S(1)} %collective-permute-done.9.refs_1_.refs_0_, bf16[160,768]{1,0:T(8,128)(2,1)S(1)} %collective-permute-done.6.refs_2_, ...), custom_call_target="tpu_custom_call" | custom-call | flops 1258291200 | bytes 11796480 | tf_op jit(solution)/shard_map/attend/pallas_call | solution.py:27
  43.3 2.7 %attend.7 = (f32[320,1920]{1,0:T(8,128)S(1)}, f32[320,1920]{1,0:T(8,128)S(1)}) custom-call(bf16[320,768]{1,0:T(8,128)(2,1)S(1)} %pad_maximum_fusion.refs_0_, bf16[320,768]{1,0:T(8,128)(2,1)S(1)} %collective-permute-done.9.refs_1_.refs_0_, bf16[160,768]{1,0:T(8,128)(2,1)S(1)} %collective-permute-done.10.refs_2_, ...), custom_call_target="tpu_custom_call" | custom-call | flops 1258291200 | bytes 11796480 | tf_op jit(solution)/shard_map/attend/pallas_call | solution.py:27
  46.0 5.3 %collective-permute-done.15.refs_2_ = bf16[160,768]{1,0:T(8,128)(2,1)S(1)} collective-permute-done((bf16[160,768]{1,0:T(8,128)(2,1)S(1)}, bf16[160,768]{1,0:T(8,128)(2,1)S(1)}, u32[]{:S(2)}, u32[]{:S(2)}) %collective-permute-start.15) | collective-permute-done | bytes 245792 | tf_op jit(solution)/shard_map/ppermute | solution.py:260
  51.3 1.4 %attend.9 = bf16[320,896]{1,0:T(8,128)(2,1)S(1)} custom-call(bf16[320,768]{1,0:T(8,128)(2,1)S(1)} %collective-permute-done.9.refs_1_.refs_0_, bf16[160,768]{1,0:T(8,128)(2,1)S(1)} %collective-permute-done.12.refs_1_, bf16[160,768]{1,0:T(8,128)(2,1)S(1)} %collective-permute-done.15.refs_2_, f32[320,1920]{1,0:T(8,128)S(1)} %get-tuple-element.84.refs_3_), custom_call_target="tpu_custom_call" | custom-call | flops 314572800 | bytes 4014080 | tf_op jit(solution)/shard_map/attend/pallas_call | solution.py:27
  55.4 1.9 %collective-permute-start.18 = (bf16[160,896]{1,0:T(8,128)(2,1)S(1)}, bf16[160,896]{1,0:T(8,128)(2,1)S(1)}, u32[]{:S(2)}, u32[]{:S(2)}) collective-permute-start(bf16[160,896]{1,0:T(8,128)(2,1)S(1)} %join.3), channel_id=1, source_target_pairs={{0,128},{128,0},{1,129},{129,1},{2,130},{130,2},{3,131},{131,3},{4... | collective-permute-start | bytes 860168 | tf_op jit(solution)/shard_map/ppermute | solution.py:326
  57.9 8.1 %collective-permute-done.18.b_ref = bf16[160,896]{1,0:T(8,128)(2,1)S(1)} collective-permute-done((bf16[160,896]{1,0:T(8,128)(2,1)S(1)}, bf16[160,896]{1,0:T(8,128)(2,1)S(1)}, u32[]{:S(2)}, u32[]{:S(2)}) %collective-permute-start.18) | collective-permute-done | bytes 286752 | tf_op jit(solution)/shard_map/ppermute | solution.py:326
  66.8 7.1 %collective-permute-done.19.beside_ref = bf16[320,384]{1,0:T(8,128)(2,1)S(1)} collective-permute-done((bf16[320,384]{1,0:T(8,128)(2,1)S(1)}, bf16[320,384]{1,0:T(8,128)(2,1)S(1)}, u32[]{:S(2)}, u32[]{:S(2)}) %collective-permute-start.19) | collective-permute-done | bytes 245792 | tf_op jit(solution)/shard_map/ppermute | solution.py:329
  73.9 2.3 %project.1 = (bf16[320,384]{1,0:T(8,128)(2,1)S(1)}, bf16[320,384]{1,0:T(8,128)(2,1)S(1)}, bf16[320,384]{1,0:T(8,128)(2,1)S(1)}, bf16[320,384]{1,0:T(8,128)(2,1)S(1)}) custom-call(s32[3]{0:T(128)S(1)} %pad_add_fusion.at_ref, bf16[320,384]{1,0:T(8,128)(2,1)S(1)} %attended.1.own_ref, bf16[320,384]{1,0:T(8,128)(2,1)S(1)} %collective-permute-done.19.beside_ref, ...), custom_call_target="tpu_custom_call" | custom-call | tf_op jit(solution)/shard_map/project/pallas_call | solution.py:238
  76.2 3.3 %collective-permute-start.21 = (bf16[320,384]{1,0:T(8,128)(2,1)S(1)}, bf16[320,384]{1,0:T(8,128)(2,1)S(1)}, u32[]{:S(2)}, u32[]{:S(2)}) collective-permute-start(bf16[320,384]{1,0:T(8,128)(2,1)S(1)} %get-tuple-element.87), channel_id=1, source_target_pairs={{0,2},{1,3},{2,0},{3,1},{4,6},{5,7},{6,4},{7,5},{8,10},{9,11},{10,... | collective-permute-start | bytes 737288 | tf_op jit(solution)/shard_map/ppermute | solution.py:333
  80.2 2.6 %collective-permute-start.23 = (bf16[320,384]{1,0:T(8,128)(2,1)S(1)}, bf16[320,384]{1,0:T(8,128)(2,1)S(1)}, u32[]{:S(2)}, u32[]{:S(2)}) collective-permute-start(bf16[320,384]{1,0:T(8,128)(2,1)S(1)} %get-tuple-element.89), channel_id=1, source_target_pairs={{0,3},{1,0},{2,1},{3,2},{4,7},{5,4},{6,5},{7,6},{8,11},{9,8},{10,9... | collective-permute-start | bytes 737288 | tf_op jit(solution)/shard_map/ppermute | solution.py:333
  82.7 4.0 %collective-permute-done.21.refs_1_ = bf16[320,384]{1,0:T(8,128)(2,1)S(1)} collective-permute-done((bf16[320,384]{1,0:T(8,128)(2,1)S(1)}, bf16[320,384]{1,0:T(8,128)(2,1)S(1)}, u32[]{:S(2)}, u32[]{:S(2)}) %collective-permute-start.21) | collective-permute-done | bytes 245792 | tf_op jit(solution)/shard_map/ppermute | solution.py:333
  86.7 2.8 %collective-permute-done.22.refs_2_ = bf16[320,384]{1,0:T(8,128)(2,1)S(1)} collective-permute-done((bf16[320,384]{1,0:T(8,128)(2,1)S(1)}, bf16[320,384]{1,0:T(8,128)(2,1)S(1)}, u32[]{:S(2)}, u32[]{:S(2)}) %collective-permute-start.22) | collective-permute-done | bytes 245792 | tf_op jit(solution)/shard_map/ppermute | solution.py:333
  (42 shorter events, 15.8 us)
Async XLA Ops:
  1.6 13.3 %collective-permute-start.2 = (bf16[160,768]{1,0:T(8,128)(2,1)S(1)}, bf16[160,768]{1,0:T(8,128)(2,1)S(1)}, u32[]{:S(2)}, u32[]{:S(2)}) collective-permute-start(bf16[160,768]{1,0:T(8,128)(2,1)S(1)} %pad_maximum_fusion.2.refs_2_), channel_id=1, source_target_pairs={{0,16},{16,32},{32,48},{48,64},{64,80},{80,96},{96,112},{112,0},{1... | collective-permute-start | bytes 737288 | tf_op jit(solution)/shard_map/ppermute | solution.py:260
  4.8 13.2 %collective-permute-start.3 = (bf16[160,768]{1,0:T(8,128)(2,1)S(1)}, bf16[160,768]{1,0:T(8,128)(2,1)S(1)}, u32[]{:S(2)}, u32[]{:S(2)}) collective-permute-start(bf16[160,768]{1,0:T(8,128)(2,1)S(1)} %pad_maximum_fusion.2.refs_2_), channel_id=1, source_target_pairs={{0,112},{16,0},{32,16},{48,32},{64,48},{80,64},{96,80},{112,96},{1... | collective-permute-start | bytes 737288 | tf_op jit(solution)/shard_map/ppermute | solution.py:260
  5.8 9.0 %collective-permute-start.8 = (bf16[160,768]{1,0:T(8,128)(2,1)S(1)}, bf16[160,768]{1,0:T(8,128)(2,1)S(1)}, u32[]{:S(2)}, u32[]{:S(2)}) collective-permute-start(bf16[160,768]{1,0:T(8,128)(2,1)S(1)} %pad_maximum_fusion.1), channel_id=1, source_target_pairs={{0,128},{128,0},{1,129},{129,1},{2,130},{130,2},{3,131},{131,3},{4... | collective-permute-start | bytes 737288 | tf_op jit(solution)/shard_map/ppermute | solution.py:288
  9.0 9.0 %collective-permute-start = (bf16[160,768]{1,0:T(8,128)(2,1)S(1)}, bf16[160,768]{1,0:T(8,128)(2,1)S(1)}, u32[]{:S(2)}, u32[]{:S(2)}) collective-permute-start(bf16[160,768]{1,0:T(8,128)(2,1)S(1)} %pad_maximum_fusion.3.refs_3_), channel_id=1, source_target_pairs={{0,16},{16,32},{32,48},{48,64},{64,80},{80,96},{96,112},{112,0},{1... | collective-permute-start | bytes 737288 | tf_op jit(solution)/shard_map/ppermute | solution.py:260
  12.3 7.8 %collective-permute-start.1 = (bf16[160,768]{1,0:T(8,128)(2,1)S(1)}, bf16[160,768]{1,0:T(8,128)(2,1)S(1)}, u32[]{:S(2)}, u32[]{:S(2)}) collective-permute-start(bf16[160,768]{1,0:T(8,128)(2,1)S(1)} %pad_maximum_fusion.3.refs_3_), channel_id=1, source_target_pairs={{0,112},{16,0},{32,16},{48,32},{64,48},{80,64},{96,80},{112,96},{1... | collective-permute-start | bytes 737288 | tf_op jit(solution)/shard_map/ppermute | solution.py:260
  14.9 18.4 %collective-permute-start.9 = (bf16[320,768]{1,0:T(8,128)(2,1)S(1)}, bf16[320,768]{1,0:T(8,128)(2,1)S(1)}, u32[]{:S(2)}, u32[]{:S(2)}) collective-permute-start(bf16[320,768]{1,0:T(8,128)(2,1)S(1)} %pad_maximum_fusion.refs_0_), channel_id=1, source_target_pairs={{0,8},{8,0},{1,9},{9,1},{2,10},{10,2},{3,11},{11,3},{4,12},{12,4},... | collective-permute-start | bytes 1474568 | tf_op jit(solution)/shard_map/ppermute | solution.py:291
  15.0 9.3 %collective-permute-start.6 = (bf16[160,768]{1,0:T(8,128)(2,1)S(1)}, bf16[160,768]{1,0:T(8,128)(2,1)S(1)}, u32[]{:S(2)}, u32[]{:S(2)}) collective-permute-start(bf16[160,768]{1,0:T(8,128)(2,1)S(1)} %collective-permute-done.2.refs_4_), channel_id=1, source_target_pairs={{0,16},{16,32},{32,48},{48,64},{64,80},{80,96},{96,112},{112,0},{1... | collective-permute-start | bytes 737288 | tf_op jit(solution)/shard_map/ppermute | solution.py:260
  18.0 10.0 %collective-permute-start.7 = (bf16[160,768]{1,0:T(8,128)(2,1)S(1)}, bf16[160,768]{1,0:T(8,128)(2,1)S(1)}, u32[]{:S(2)}, u32[]{:S(2)}) collective-permute-start(bf16[160,768]{1,0:T(8,128)(2,1)S(1)} %collective-permute-done.3.refs_6_), channel_id=1, source_target_pairs={{0,112},{16,0},{32,16},{48,32},{64,48},{80,64},{96,80},{112,96},{1... | collective-permute-start | bytes 737288 | tf_op jit(solution)/shard_map/ppermute | solution.py:260
  20.1 9.9 %collective-permute-start.4 = (bf16[160,768]{1,0:T(8,128)(2,1)S(1)}, bf16[160,768]{1,0:T(8,128)(2,1)S(1)}, u32[]{:S(2)}, u32[]{:S(2)}) collective-permute-start(bf16[160,768]{1,0:T(8,128)(2,1)S(1)} %collective-permute-done.refs_5_), channel_id=1, source_target_pairs={{0,16},{16,32},{32,48},{48,64},{64,80},{80,96},{96,112},{112,0},{1... | collective-permute-start | bytes 737288 | tf_op jit(solution)/shard_map/ppermute | solution.py:260
  21.2 12.0 %collective-permute-start.5 = (bf16[160,768]{1,0:T(8,128)(2,1)S(1)}, bf16[160,768]{1,0:T(8,128)(2,1)S(1)}, u32[]{:S(2)}, u32[]{:S(2)}) collective-permute-start(bf16[160,768]{1,0:T(8,128)(2,1)S(1)} %collective-permute-done.1.refs_7_), channel_id=1, source_target_pairs={{0,112},{16,0},{32,16},{48,32},{64,48},{80,64},{96,80},{112,96},{1... | collective-permute-start | bytes 737288 | tf_op jit(solution)/shard_map/ppermute | solution.py:260
  28.0 10.0 %collective-permute-start.10 = (bf16[160,768]{1,0:T(8,128)(2,1)S(1)}, bf16[160,768]{1,0:T(8,128)(2,1)S(1)}, u32[]{:S(2)}, u32[]{:S(2)}) collective-permute-start(bf16[160,768]{1,0:T(8,128)(2,1)S(1)} %collective-permute-done.6.refs_2_), channel_id=1, source_target_pairs={{0,16},{16,32},{32,48},{48,64},{64,80},{80,96},{96,112},{112,0},{1... | collective-permute-start | bytes 737288 | tf_op jit(solution)/shard_map/ppermute | solution.py:260
  28.0 10.5 %collective-permute-start.11 = (bf16[160,768]{1,0:T(8,128)(2,1)S(1)}, bf16[160,768]{1,0:T(8,128)(2,1)S(1)}, u32[]{:S(2)}, u32[]{:S(2)}) collective-permute-start(bf16[160,768]{1,0:T(8,128)(2,1)S(1)} %collective-permute-done.7.refs_4_), channel_id=1, source_target_pairs={{0,112},{16,0},{32,16},{48,32},{64,48},{80,64},{96,80},{112,96},{1... | collective-permute-start | bytes 737288 | tf_op jit(solution)/shard_map/ppermute | solution.py:260
  30.0 16.0 %collective-permute-start.16 = (bf16[384,768]{1,0:T(8,128)(2,1)S(1)}, bf16[384,768]{1,0:T(8,128)(2,1)S(1)}, u32[]{:S(2)}, u32[]{:S(2)}) collective-permute-start(bf16[384,768]{1,0:T(8,128)(2,1)S(1)} %constant_dynamic-slice_fusion), channel_id=1, source_target_pairs={{0,4},{4,0},{1,5},{5,1},{2,6},{6,2},{3,7},{7,3},{8,12},{12,8},{9,1... | collective-permute-start | bytes 1769480 | tf_op jit(solution)/shard_map/ppermute | solution.py:302
  33.3 9.2 %collective-permute-start.13 = (bf16[160,768]{1,0:T(8,128)(2,1)S(1)}, bf16[160,768]{1,0:T(8,128)(2,1)S(1)}, u32[]{:S(2)}, u32[]{:S(2)}) collective-permute-start(bf16[160,768]{1,0:T(8,128)(2,1)S(1)} %collective-permute-done.4.refs_3_), channel_id=1, source_target_pairs={{0,16},{16,32},{32,48},{48,64},{64,80},{80,96},{96,112},{112,0},{1... | collective-permute-start | bytes 737288 | tf_op jit(solution)/shard_map/ppermute | solution.py:260
  33.8 9.2 %collective-permute-start.14 = (bf16[160,768]{1,0:T(8,128)(2,1)S(1)}, bf16[160,768]{1,0:T(8,128)(2,1)S(1)}, u32[]{:S(2)}, u32[]{:S(2)}) collective-permute-start(bf16[160,768]{1,0:T(8,128)(2,1)S(1)} %collective-permute-done.5.refs_5_), channel_id=1, source_target_pairs={{0,112},{16,0},{32,16},{48,32},{64,48},{80,64},{96,80},{112,96},{1... | collective-permute-start | bytes 737288 | tf_op jit(solution)/shard_map/ppermute | solution.py:260
  38.5 7.5 %collective-permute-start.12 = (bf16[160,768]{1,0:T(8,128)(2,1)S(1)}, bf16[160,768]{1,0:T(8,128)(2,1)S(1)}, u32[]{:S(2)}, u32[]{:S(2)}) collective-permute-start(bf16[160,768]{1,0:T(8,128)(2,1)S(1)} %collective-permute-done.10.refs_2_), channel_id=1, source_target_pairs={{0,16},{16,32},{32,48},{48,64},{64,80},{80,96},{96,112},{112,0},{1... | collective-permute-start | bytes 737288 | tf_op jit(solution)/shard_map/ppermute | solution.py:260
  43.0 8.3 %collective-permute-start.15 = (bf16[160,768]{1,0:T(8,128)(2,1)S(1)}, bf16[160,768]{1,0:T(8,128)(2,1)S(1)}, u32[]{:S(2)}, u32[]{:S(2)}) collective-permute-start(bf16[160,768]{1,0:T(8,128)(2,1)S(1)} %collective-permute-done.14.refs_5_), channel_id=1, source_target_pairs={{0,112},{16,0},{32,16},{48,32},{64,48},{80,64},{96,80},{112,96},{1... | collective-permute-start | bytes 737288 | tf_op jit(solution)/shard_map/ppermute | solution.py:260
  52.7 2.1 %collective-permute-start.17 = (bf16[320,896]{1,0:T(8,128)(2,1)S(1)}, bf16[320,896]{1,0:T(8,128)(2,1)S(1)}, u32[]{:S(2)}, u32[]{:S(2)}) collective-permute-start(bf16[320,896]{1,0:T(8,128)(2,1)S(1)} %attend.9), channel_id=1, source_target_pairs={{0,8},{8,0},{1,9},{9,1},{2,10},{10,2},{3,11},{11,3},{4,12},{12,4},... | collective-permute-start | bytes 1720328 | tf_op jit(solution)/shard_map/ppermute | solution.py:317
  52.8 14.0 %collective-permute-start.20 = (bf16[384,768]{1,0:T(8,128)(2,1)S(1)}, bf16[384,768]{1,0:T(8,128)(2,1)}, u32[]{:S(2)}, u32[]{:S(2)}) collective-permute-start(bf16[384,768]{1,0:T(8,128)(2,1)S(1)} %collective-permute-done.16.w_mine_ref), channel_id=1, source_target_pairs={{0,8},{8,0},{1,9},{9,1},{2,10},{10,2},{3,11},{11,3},{4,12},{12,4},... | collective-permute-start | bytes 1769480 | tf_op jit(solution)/shard_map/ppermute | solution.py:330
  55.4 10.6 %collective-permute-start.18 = (bf16[160,896]{1,0:T(8,128)(2,1)S(1)}, bf16[160,896]{1,0:T(8,128)(2,1)S(1)}, u32[]{:S(2)}, u32[]{:S(2)}) collective-permute-start(bf16[160,896]{1,0:T(8,128)(2,1)S(1)} %join.3), channel_id=1, source_target_pairs={{0,128},{128,0},{1,129},{129,1},{2,130},{130,2},{3,131},{131,3},{4... | collective-permute-start | bytes 860168 | tf_op jit(solution)/shard_map/ppermute | solution.py:326
  66.5 7.4 %collective-permute-start.19 = (bf16[320,384]{1,0:T(8,128)(2,1)S(1)}, bf16[320,384]{1,0:T(8,128)(2,1)S(1)}, u32[]{:S(2)}, u32[]{:S(2)}) collective-permute-start(bf16[320,384]{1,0:T(8,128)(2,1)S(1)} %attended.1.own_ref), channel_id=1, source_target_pairs={{0,4},{4,0},{1,5},{5,1},{2,6},{6,2},{3,7},{7,3},{8,12},{12,8},{9,1... | collective-permute-start | bytes 737288 | tf_op jit(solution)/shard_map/ppermute | solution.py:329
  76.2 10.5 %collective-permute-start.21 = (bf16[320,384]{1,0:T(8,128)(2,1)S(1)}, bf16[320,384]{1,0:T(8,128)(2,1)S(1)}, u32[]{:S(2)}, u32[]{:S(2)}) collective-permute-start(bf16[320,384]{1,0:T(8,128)(2,1)S(1)} %get-tuple-element.87), channel_id=1, source_target_pairs={{0,2},{1,3},{2,0},{3,1},{4,6},{5,7},{6,4},{7,5},{8,10},{9,11},{10,... | collective-permute-start | bytes 737288 | tf_op jit(solution)/shard_map/ppermute | solution.py:333
  79.5 10.0 %collective-permute-start.22 = (bf16[320,384]{1,0:T(8,128)(2,1)S(1)}, bf16[320,384]{1,0:T(8,128)(2,1)S(1)}, u32[]{:S(2)}, u32[]{:S(2)}) collective-permute-start(bf16[320,384]{1,0:T(8,128)(2,1)S(1)} %get-tuple-element.88), channel_id=1, source_target_pairs={{0,1},{1,2},{2,3},{3,0},{4,5},{5,6},{6,7},{7,4},{8,9},{9,10},{10,1... | collective-permute-start | bytes 737288 | tf_op jit(solution)/shard_map/ppermute | solution.py:333
  80.2 9.6 %collective-permute-start.23 = (bf16[320,384]{1,0:T(8,128)(2,1)S(1)}, bf16[320,384]{1,0:T(8,128)(2,1)S(1)}, u32[]{:S(2)}, u32[]{:S(2)}) collective-permute-start(bf16[320,384]{1,0:T(8,128)(2,1)S(1)} %get-tuple-element.89), channel_id=1, source_target_pairs={{0,3},{1,0},{2,1},{3,2},{4,7},{5,4},{6,5},{7,6},{8,11},{9,8},{10,9... | collective-permute-start | bytes 737288 | tf_op jit(solution)/shard_map/ppermute | solution.py:333
  (1 other events, 19.2 us)

commit v4 on v3

--- a/solution.py
+++ b/solution.py
@@ -217,32 +217,46 @@
             out[at * rows : (at + 1) * rows, head * DH : (head + 1) * DH] = each[at].astype(out.dtype)
 
 
-def project_kernel(at_ref, own_ref, beside_ref, w_ref, w_mine_ref, w_other_ref, *outs):
+def project_own_kernel(at_ref, own_ref, w_ref, w_mine_ref, w_other_ref, *refs):
     xl, y, core = at_ref[0], at_ref[1], at_ref[2]
-    columns = outs[0].shape[1]
-    both = jnp.concatenate([own_ref[...], beside_ref[...]], axis=1)
-    for step, out in enumerate(outs):
-        target = lax.rem(y + step, len(outs))
+    count = len(refs) // 2
+    columns = refs[0].shape[1]
+    for step, (out, w_out_ref) in enumerate(zip(refs[:count], refs[count:])):
+        target = lax.rem(y + step, count)
+        first = pl.multiple_of((xl * count + target) * columns, DH)
+        out[...] = jnp.dot(
+            own_ref[...], w_ref[:, pl.ds(first, columns)], preferred_element_type=jnp.float32
+        )
         fetched_by, place = lax.div(target, 2), lax.rem(target, 2)
-        first = pl.multiple_of((xl * len(outs) + target) * columns, DH)
-        first_beside = pl.ds(pl.multiple_of(place * columns, DH), columns)
-        w_beside = jnp.where(
-            fetched_by == core, w_mine_ref[:, first_beside], w_other_ref[:, first_beside]
+        half = pl.ds(pl.multiple_of(place * columns, DH), columns)
+        w_out_ref[...] = jnp.where(fetched_by == core, w_mine_ref[:, half], w_other_ref[:, half])
+
+
+def project_kernel(beside_ref, *refs):
+    count = len(refs) // 3
+    for own, w_beside, out in zip(refs[:count], refs[count : 2 * count], refs[2 * count :]):
+        total = own[...] + jnp.dot(
+            beside_ref[...], w_beside[...], preferred_element_type=jnp.float32
         )
-        w_both = jnp.concatenate([w_ref[:, pl.ds(first, columns)], w_beside], axis=0)
-        out[...] = jnp.dot(both, w_both, preferred_element_type=jnp.float32).astype(out.dtype)
-
-
-def project(place, own, beside, w_out, w_mine, w_other):
-    outs = [shape(*own.shape)] * 4
+        out[...] = total.astype(out.dtype)
+
+
+def project_own(where, own, w_out, w_mine, w_other):
+    rows, columns = own.shape
+    outs = [shape(rows, columns, jnp.float32)] * 4 + [shape(w_out.shape[0], columns)] * 4
     return pl.pallas_call(
-        project_kernel,
-        in_specs=[pl.BlockSpec(memory_space=pltpu.SMEM)] + [vmem()] * 5,
+        project_own_kernel,
+        in_specs=[pl.BlockSpec(memory_space=pltpu.SMEM)] + [vmem()] * 4,
         out_specs=[vmem()] * len(outs),
         out_shape=outs,
         compiler_params=PARAMS,
-        name="project",
-    )(jnp.stack(place).astype(jnp.int32), own, beside, w_out, w_mine, w_other)
+        cost_estimate=pl.CostEstimate(
+            flops=8 * rows * columns * columns,
+            bytes_accessed=16 * rows * columns,
+            transcendentals=0,
+        ),
+        name="project_own",
+    )(where, own, w_out, w_mine, w_other)
 
 
 def total_kernel(*refs):
@@ -272,6 +286,8 @@
 def on_device(queries, keys, values, tan_queries, tan_keys, tan_values, w_out):
     rows, width = queries.shape
     own = [beside(keys, tan_keys), beside(values, tan_values)]
+    own_q = beside(tan_queries, queries)
+    own_q, own[0] = lax.optimization_barrier((own_q, own[0]))
     def around(pair):
         return along_z(pair[0], 1), along_z(pair[1], -1)
 
@@ -279,7 +295,6 @@
     k_steps.append(around(k_steps[0]))
     v_steps.append(around(v_steps[0]))
 
-    own_q = beside(tan_queries, queries)
     place = [lax.axis_index(name) for name in ("xl", "y", "core")]
     quarter = w_out.shape[1] // 4
     wanted = lax.dynamic_slice_in_dim(
@@ -328,7 +343,16 @@
     attended = call(attended_kernel, "attended", [shape(2 * rows, width)], [near, from_far])[0]
     beside_attended = lax.ppermute(attended, "xl", SWAP)
     w_other = lax.ppermute(w_mine, "core", SWAP)
-    parts = list(project(place, attended, beside_attended, w_out, w_mine, w_other))
+    where = jnp.stack(place).astype(jnp.int32)
+    ready = project_own(where, attended, w_out, w_mine, w_other)
+    parts = call(
+        project_kernel,
+        "project",
+        [shape(*attended.shape)] * 4,
+        [beside_attended] + list(ready),
+        flops=8 * 2 * rows * width * width,
+    )
+    parts = list(parts)
     parts = parts[:1] + [
         lax.ppermute(part, "y", [(i, (i + step) % 4) for i in range(4)])
         for step, part in ((2, parts[2]), (1, parts[1]), (3, parts[3]))

time: 90.8 us -> 88.3 us (0.972)
  waiting for transfers between devices: 40.9 us -> 38.9 us
    ppermute x1, waiting for transfers between devices: 7.12 us -> 5.15 us  [on_device(): beside_attended = lax.ppermute(attended, 'xl', SWAP)]
    max x3 -> x2, other arithmetic: 2.95 us -> 2.1 us  [beside(): jnp.maximum(lax.pad(left, low, [(0, 0, 0), (0, width, 0)]), lax.pad(right...]
    pallas_call x9 -> x10, Pallas kernels: 13.2 us -> 14 us  [call(): pl.pallas_call(kernel, in_specs=[vmem()] * len(args), out_specs=[vmem()]...]
  transfers between devices with their start and end apart: 24 -> 24, of which waited for: 14 -> 14; matrix products, arithmetic and copies ran while one was open for 4% -> 2% of each run, Pallas kernels for 12% -> 15%
where the time goes in v4:
time: 88.3 us; the launch traced here: 88.1 us
  waiting for transfers between devices  38.9 us (44%)
  starting transfers between devices  29.2 us (33%)
  Pallas kernels  15.9 us (18%)
  other arithmetic  2.21 us (3%)
  local copies, waits for them, and re-layouts  1.11 us (1%)
    ppermute x14, starting transfers between devices, along_z(): return lax.ppermute(x, 'z', [(i, (i + step) % 8) for i in range(8)])  17.2 us
    ppermute x14, waiting for transfers between devices, along_z(): return lax.ppermute(x, 'z', [(i, (i + step) % 8) for i in range(8)])  17.1 us
    pallas_call x10, Pallas kernels, call(): pl.pallas_call(kernel, in_specs=[vmem()] * len(args), out_specs=[vmem()]...  14 us
    ppermute x1, waiting for transfers between devices, on_device(): from_far = lax.ppermute(join(rows), 'xh', SWAP)  8.08 us
    ppermute x3, waiting for transfers between devices, on_device(): lax.ppermute(part, 'y', [(i, (i + step) % 4) for i in range(4)])  7.07 us
    ppermute x3, starting transfers between devices, on_device(): lax.ppermute(part, 'y', [(i, (i + step) % 4) for i in range(4)])  6.52 us
    ppermute x1, waiting for transfers between devices, on_device(): beside_attended = lax.ppermute(attended, 'xl', SWAP)  5.15 us
    ppermute x1, starting transfers between devices, on_device(): far_q = lax.ppermute(own_q, 'xh', SWAP)  2.12 us
  transfers between devices with their start and end apart: 24, of which 14 were waited for; matrix products, arithmetic and copies ran while one was open for 2% of the time, Pallas kernels for 15%

profile of v4, /device:TPU:98, one launch (start us, length us, event | category | flops | bytes accessed | tf_op | source)
XLA Modules:
  0.0 88.1 jit_solution(8428975358847780723)
XLA Ops:
  1.8 3.2 %collective-permute-start.2 = (bf16[160,768]{1,0:T(8,128)(2,1)S(1)}, bf16[160,768]{1,0:T(8,128)(2,1)S(1)}, u32[]{:S(2)}, u32[]{:S(2)}) collective-permute-start(bf16[160,768]{1,0:T(8,128)(2,1)S(1)} %get-tuple-element.56.refs_2_), channel_id=1, source_target_pairs={{0,16},{16,32},{32,48},{48,64},{64,80},{80,96},{96,112},{112,0},{1... | collective-permute-start | bytes 737288 | tf_op jit(solution)/shard_map/ppermute | solution.py:274
  5.0 2.1 %collective-permute-start.8 = (bf16[160,768]{1,0:T(8,128)(2,1)S(1)}, bf16[160,768]{1,0:T(8,128)(2,1)S(1)}, u32[]{:S(2)}, u32[]{:S(2)}) collective-permute-start(bf16[160,768]{1,0:T(8,128)(2,1)S(1)} %get-tuple-element.61), channel_id=1, source_target_pairs={{0,128},{128,0},{1,129},{129,1},{2,130},{130,2},{3,131},{131,3},{4... | collective-permute-start | bytes 737288 | tf_op jit(solution)/shard_map/ppermute | solution.py:303
  8.1 3.3 %collective-permute-start = (bf16[160,768]{1,0:T(8,128)(2,1)S(1)}, bf16[160,768]{1,0:T(8,128)(2,1)S(1)}, u32[]{:S(2)}, u32[]{:S(2)}) collective-permute-start(bf16[160,768]{1,0:T(8,128)(2,1)S(1)} %pad_maximum_fusion.3.refs_3_), channel_id=1, source_target_pairs={{0,16},{16,32},{32,48},{48,64},{64,80},{80,96},{96,112},{112,0},{1... | collective-permute-start | bytes 737288 | tf_op jit(solution)/shard_map/ppermute | solution.py:274
  12.5 1.4 %collective-permute-done.8 = bf16[160,768]{1,0:T(8,128)(2,1)S(1)} collective-permute-done((bf16[160,768]{1,0:T(8,128)(2,1)S(1)}, bf16[160,768]{1,0:T(8,128)(2,1)S(1)}, u32[]{:S(2)}, u32[]{:S(2)}) %collective-permute-start.8) | collective-permute-done | bytes 245792 | tf_op jit(solution)/shard_map/ppermute | solution.py:303
  14.0 3.0 %collective-permute-start.6 = (bf16[160,768]{1,0:T(8,128)(2,1)S(1)}, bf16[160,768]{1,0:T(8,128)(2,1)S(1)}, u32[]{:S(2)}, u32[]{:S(2)}) collective-permute-start(bf16[160,768]{1,0:T(8,128)(2,1)S(1)} %collective-permute-done.2.refs_4_), channel_id=1, source_target_pairs={{0,16},{16,32},{32,48},{48,64},{64,80},{80,96},{96,112},{112,0},{1... | collective-permute-start | bytes 737288 | tf_op jit(solution)/shard_map/ppermute | solution.py:274
  17.1 2.1 %collective-permute-done.1.refs_7_ = bf16[160,768]{1,0:T(8,128)(2,1)S(1)} collective-permute-done((bf16[160,768]{1,0:T(8,128)(2,1)S(1)}, bf16[160,768]{1,0:T(8,128)(2,1)S(1)}, u32[]{:S(2)}, u32[]{:S(2)}) %collective-permute-start.1) | collective-permute-done | bytes 245792 | tf_op jit(solution)/shard_map/ppermute | solution.py:274
  21.2 2.1 %collective-permute-done.6.refs_2_ = bf16[160,768]{1,0:T(8,128)(2,1)S(1)} collective-permute-done((bf16[160,768]{1,0:T(8,128)(2,1)S(1)}, bf16[160,768]{1,0:T(8,128)(2,1)S(1)}, u32[]{:S(2)}, u32[]{:S(2)}) %collective-permute-start.6) | collective-permute-done | bytes 245792 | tf_op jit(solution)/shard_map/ppermute | solution.py:274
  23.3 3.7 %collective-permute-done.7.refs_4_ = bf16[160,768]{1,0:T(8,128)(2,1)S(1)} collective-permute-done((bf16[160,768]{1,0:T(8,128)(2,1)S(1)}, bf16[160,768]{1,0:T(8,128)(2,1)S(1)}, u32[]{:S(2)}, u32[]{:S(2)}) %collective-permute-start.7) | collective-permute-done | bytes 245792 | tf_op jit(solution)/shard_map/ppermute | solution.py:274
  27.1 2.0 %collective-permute-start.11 = (bf16[160,768]{1,0:T(8,128)(2,1)S(1)}, bf16[160,768]{1,0:T(8,128)(2,1)S(1)}, u32[]{:S(2)}, u32[]{:S(2)}) collective-permute-start(bf16[160,768]{1,0:T(8,128)(2,1)S(1)} %collective-permute-done.7.refs_4_), channel_id=1, source_target_pairs={{0,112},{16,0},{32,16},{48,32},{64,48},{80,64},{96,80},{112,96},{1... | collective-permute-start | bytes 737288 | tf_op jit(solution)/shard_map/ppermute | solution.py:274
  29.6 2.7 %collective-permute-done.5.refs_5_ = bf16[160,768]{1,0:T(8,128)(2,1)S(1)} collective-permute-done((bf16[160,768]{1,0:T(8,128)(2,1)S(1)}, bf16[160,768]{1,0:T(8,128)(2,1)S(1)}, u32[]{:S(2)}, u32[]{:S(2)}) %collective-permute-start.5) | collective-permute-done | bytes 245792 | tf_op jit(solution)/shard_map/ppermute | solution.py:274
  32.8 1.5 %collective-permute-start.14 = (bf16[160,768]{1,0:T(8,128)(2,1)S(1)}, bf16[160,768]{1,0:T(8,128)(2,1)S(1)}, u32[]{:S(2)}, u32[]{:S(2)}) collective-permute-start(bf16[160,768]{1,0:T(8,128)(2,1)S(1)} %collective-permute-done.5.refs_5_), channel_id=1, source_target_pairs={{0,112},{16,0},{32,16},{48,32},{64,48},{80,64},{96,80},{112,96},{1... | collective-permute-start | bytes 737288 | tf_op jit(solution)/shard_map/ppermute | solution.py:274
  34.4 2.7 %attend.5 = (f32[320,1920]{1,0:T(8,128)S(1)}, f32[320,1920]{1,0:T(8,128)S(1)}) custom-call(bf16[320,768]{1,0:T(8,128)(2,1)S(1)} %pad_maximum_fusion.refs_0_, bf16[320,768]{1,0:T(8,128)(2,1)S(1)} %collective-permute-done.9.refs_1_.refs_0_, bf16[160,768]{1,0:T(8,128)(2,1)S(1)} %get-tuple-element.56.refs_2_, bf16[160,768]{1,0:T(8,128)(2,1)S(1)} %pad_maximum_fusion.3.refs_3_, ...), custom_call_target="tpu_custom_call" | custom-call | flops 1887436800 | bytes 7372800 | tf_op jit(solution)/shard_map/attend/pallas_call | solution.py:27
  38.8 2.7 %attend.6 = (f32[320,1920]{1,0:T(8,128)S(1)}, f32[320,1920]{1,0:T(8,128)S(1)}) custom-call(bf16[320,768]{1,0:T(8,128)(2,1)S(1)} %pad_maximum_fusion.refs_0_, bf16[320,768]{1,0:T(8,128)(2,1)S(1)} %collective-permute-done.9.refs_1_.refs_0_, bf16[160,768]{1,0:T(8,128)(2,1)S(1)} %collective-permute-done.6.refs_2_, ...), custom_call_target="tpu_custom_call" | custom-call | flops 1258291200 | bytes 11796480 | tf_op jit(solution)/shard_map/attend/pallas_call | solution.py:27
  42.4 2.7 %attend.7 = (f32[320,1920]{1,0:T(8,128)S(1)}, f32[320,1920]{1,0:T(8,128)S(1)}) custom-call(bf16[320,768]{1,0:T(8,128)(2,1)S(1)} %pad_maximum_fusion.refs_0_, bf16[320,768]{1,0:T(8,128)(2,1)S(1)} %collective-permute-done.9.refs_1_.refs_0_, bf16[160,768]{1,0:T(8,128)(2,1)S(1)} %collective-permute-done.10.refs_2_, ...), custom_call_target="tpu_custom_call" | custom-call | flops 1258291200 | bytes 11796480 | tf_op jit(solution)/shard_map/attend/pallas_call | solution.py:27
  45.1 5.3 %collective-permute-done.15.refs_2_ = bf16[160,768]{1,0:T(8,128)(2,1)S(1)} collective-permute-done((bf16[160,768]{1,0:T(8,128)(2,1)S(1)}, bf16[160,768]{1,0:T(8,128)(2,1)S(1)}, u32[]{:S(2)}, u32[]{:S(2)}) %collective-permute-start.15) | collective-permute-done | bytes 245792 | tf_op jit(solution)/shard_map/ppermute | solution.py:274
  50.4 1.4 %attend.9 = bf16[320,896]{1,0:T(8,128)(2,1)S(1)} custom-call(bf16[320,768]{1,0:T(8,128)(2,1)S(1)} %collective-permute-done.9.refs_1_.refs_0_, bf16[160,768]{1,0:T(8,128)(2,1)S(1)} %collective-permute-done.12.refs_1_, bf16[160,768]{1,0:T(8,128)(2,1)S(1)} %collective-permute-done.15.refs_2_, f32[320,1920]{1,0:T(8,128)S(1)} %get-tuple-element.96.refs_3_), custom_call_target="tpu_custom_call" | custom-call | flops 314572800 | bytes 4014080 | tf_op jit(solution)/shard_map/attend/pallas_call | solution.py:27
  54.5 1.9 %collective-permute-start.18 = (bf16[160,896]{1,0:T(8,128)(2,1)S(1)}, bf16[160,896]{1,0:T(8,128)(2,1)S(1)}, u32[]{:S(2)}, u32[]{:S(2)}) collective-permute-start(bf16[160,896]{1,0:T(8,128)(2,1)S(1)} %join.3), channel_id=1, source_target_pairs={{0,128},{128,0},{1,129},{129,1},{2,130},{130,2},{3,131},{131,3},{4... | collective-permute-start | bytes 860168 | tf_op jit(solution)/shard_map/ppermute | solution.py:341
  57.0 8.1 %collective-permute-done.18.b_ref = bf16[160,896]{1,0:T(8,128)(2,1)S(1)} collective-permute-done((bf16[160,896]{1,0:T(8,128)(2,1)S(1)}, bf16[160,896]{1,0:T(8,128)(2,1)S(1)}, u32[]{:S(2)}, u32[]{:S(2)}) %collective-permute-start.18) | collective-permute-done | bytes 286752 | tf_op jit(solution)/shard_map/ppermute | solution.py:341
  65.9 2.0 %project_own.1 = (f32[320,384]{1,0:T(8,128)S(1)}, f32[320,384]{1,0:T(8,128)S(1)}, f32[320,384]{1,0:T(8,128)S(1)}, f32[320,384]{1,0:T(8,128)S(1)}, bf16[384,384]{...) custom-call(s32[3]{0:T(128)S(1)} %pad_add_fusion.at_ref, ...), custom_call_target="tpu_custom_call" | custom-call | flops 377487360 | bytes 1966080 | tf_op jit(solution)/shard_map/project_own/pallas_call | solution.py:247
  67.8 5.2 %collective-permute-done.19.beside_ref = bf16[320,384]{1,0:T(8,128)(2,1)S(1)} collective-permute-done((bf16[320,384]{1,0:T(8,128)(2,1)S(1)}, bf16[320,384]{1,0:T(8,128)(2,1)S(1)}, u32[]{:S(2)}, u32[]{:S(2)}) %collective-permute-start.19) | collective-permute-done | bytes 245792 | tf_op jit(solution)/shard_map/ppermute | solution.py:344
  73.8 3.3 %collective-permute-start.21 = (bf16[320,384]{1,0:T(8,128)(2,1)S(1)}, bf16[320,384]{1,0:T(8,128)(2,1)S(1)}, u32[]{:S(2)}, u32[]{:S(2)}) collective-permute-start(bf16[320,384]{1,0:T(8,128)(2,1)S(1)} %get-tuple-element.107), channel_id=1, source_target_pairs={{0,2},{1,3},{2,0},{3,1},{4,6},{5,7},{6,4},{7,5},{8,10},{9,11},{10,... | collective-permute-start | bytes 737288 | tf_op jit(solution)/shard_map/ppermute | solution.py:357
  77.7 2.6 %collective-permute-start.23 = (bf16[320,384]{1,0:T(8,128)(2,1)S(1)}, bf16[320,384]{1,0:T(8,128)(2,1)S(1)}, u32[]{:S(2)}, u32[]{:S(2)}) collective-permute-start(bf16[320,384]{1,0:T(8,128)(2,1)S(1)} %get-tuple-element.109), channel_id=1, source_target_pairs={{0,3},{1,0},{2,1},{3,2},{4,7},{5,4},{6,5},{7,6},{8,11},{9,8},{10,9... | collective-permute-start | bytes 737288 | tf_op jit(solution)/shard_map/ppermute | solution.py:357
  80.3 4.0 %collective-permute-done.21.refs_1_ = bf16[320,384]{1,0:T(8,128)(2,1)S(1)} collective-permute-done((bf16[320,384]{1,0:T(8,128)(2,1)S(1)}, bf16[320,384]{1,0:T(8,128)(2,1)S(1)}, u32[]{:S(2)}, u32[]{:S(2)}) %collective-permute-start.21) | collective-permute-done | bytes 245792 | tf_op jit(solution)/shard_map/ppermute | solution.py:357
  84.2 2.8 %collective-permute-done.22.refs_2_ = bf16[320,384]{1,0:T(8,128)(2,1)S(1)} collective-permute-done((bf16[320,384]{1,0:T(8,128)(2,1)S(1)}, bf16[320,384]{1,0:T(8,128)(2,1)S(1)}, u32[]{:S(2)}, u32[]{:S(2)}) %collective-permute-start.22) | collective-permute-done | bytes 245792 | tf_op jit(solution)/shard_map/ppermute | solution.py:357
  (42 shorter events, 15.7 us)
Async XLA Ops:
  1.8 12.3 %collective-permute-start.2 = (bf16[160,768]{1,0:T(8,128)(2,1)S(1)}, bf16[160,768]{1,0:T(8,128)(2,1)S(1)}, u32[]{:S(2)}, u32[]{:S(2)}) collective-permute-start(bf16[160,768]{1,0:T(8,128)(2,1)S(1)} %get-tuple-element.56.refs_2_), channel_id=1, source_target_pairs={{0,16},{16,32},{32,48},{48,64},{64,80},{80,96},{96,112},{112,0},{1... | collective-permute-start | bytes 737288 | tf_op jit(solution)/shard_map/ppermute | solution.py:274
  5.0 12.1 %collective-permute-start.3 = (bf16[160,768]{1,0:T(8,128)(2,1)S(1)}, bf16[160,768]{1,0:T(8,128)(2,1)S(1)}, u32[]{:S(2)}, u32[]{:S(2)}) collective-permute-start(bf16[160,768]{1,0:T(8,128)(2,1)S(1)} %get-tuple-element.56.refs_2_), channel_id=1, source_target_pairs={{0,112},{16,0},{32,16},{48,32},{64,48},{80,64},{96,80},{112,96},{1... | collective-permute-start | bytes 737288 | tf_op jit(solution)/shard_map/ppermute | solution.py:274
  5.0 8.9 %collective-permute-start.8 = (bf16[160,768]{1,0:T(8,128)(2,1)S(1)}, bf16[160,768]{1,0:T(8,128)(2,1)S(1)}, u32[]{:S(2)}, u32[]{:S(2)}) collective-permute-start(bf16[160,768]{1,0:T(8,128)(2,1)S(1)} %get-tuple-element.61), channel_id=1, source_target_pairs={{0,128},{128,0},{1,129},{129,1},{2,130},{130,2},{3,131},{131,3},{4... | collective-permute-start | bytes 737288 | tf_op jit(solution)/shard_map/ppermute | solution.py:303
  8.1 9.0 %collective-permute-start = (bf16[160,768]{1,0:T(8,128)(2,1)S(1)}, bf16[160,768]{1,0:T(8,128)(2,1)S(1)}, u32[]{:S(2)}, u32[]{:S(2)}) collective-permute-start(bf16[160,768]{1,0:T(8,128)(2,1)S(1)} %pad_maximum_fusion.3.refs_3_), channel_id=1, source_target_pairs={{0,16},{16,32},{32,48},{48,64},{64,80},{80,96},{96,112},{112,0},{1... | collective-permute-start | bytes 737288 | tf_op jit(solution)/shard_map/ppermute | solution.py:274
  11.4 7.8 %collective-permute-start.1 = (bf16[160,768]{1,0:T(8,128)(2,1)S(1)}, bf16[160,768]{1,0:T(8,128)(2,1)S(1)}, u32[]{:S(2)}, u32[]{:S(2)}) collective-permute-start(bf16[160,768]{1,0:T(8,128)(2,1)S(1)} %pad_maximum_fusion.3.refs_3_), channel_id=1, source_target_pairs={{0,112},{16,0},{32,16},{48,32},{64,48},{80,64},{96,80},{112,96},{1... | collective-permute-start | bytes 737288 | tf_op jit(solution)/shard_map/ppermute | solution.py:274
  13.9 18.4 %collective-permute-start.9 = (bf16[320,768]{1,0:T(8,128)(2,1)S(1)}, bf16[320,768]{1,0:T(8,128)(2,1)S(1)}, u32[]{:S(2)}, u32[]{:S(2)}) collective-permute-start(bf16[320,768]{1,0:T(8,128)(2,1)S(1)} %pad_maximum_fusion.refs_0_), channel_id=1, source_target_pairs={{0,8},{8,0},{1,9},{9,1},{2,10},{10,2},{3,11},{11,3},{4,12},{12,4},... | collective-permute-start | bytes 1474568 | tf_op jit(solution)/shard_map/ppermute | solution.py:306
  14.0 9.3 %collective-permute-start.6 = (bf16[160,768]{1,0:T(8,128)(2,1)S(1)}, bf16[160,768]{1,0:T(8,128)(2,1)S(1)}, u32[]{:S(2)}, u32[]{:S(2)}) collective-permute-start(bf16[160,768]{1,0:T(8,128)(2,1)S(1)} %collective-permute-done.2.refs_4_), channel_id=1, source_target_pairs={{0,16},{16,32},{32,48},{48,64},{64,80},{80,96},{96,112},{112,0},{1... | collective-permute-start | bytes 737288 | tf_op jit(solution)/shard_map/ppermute | solution.py:274
  17.1 10.0 %collective-permute-start.7 = (bf16[160,768]{1,0:T(8,128)(2,1)S(1)}, bf16[160,768]{1,0:T(8,128)(2,1)S(1)}, u32[]{:S(2)}, u32[]{:S(2)}) collective-permute-start(bf16[160,768]{1,0:T(8,128)(2,1)S(1)} %collective-permute-done.3.refs_6_), channel_id=1, source_target_pairs={{0,112},{16,0},{32,16},{48,32},{64,48},{80,64},{96,80},{112,96},{1... | collective-permute-start | bytes 737288 | tf_op jit(solution)/shard_map/ppermute | solution.py:274
  19.2 9.9 %collective-permute-start.4 = (bf16[160,768]{1,0:T(8,128)(2,1)S(1)}, bf16[160,768]{1,0:T(8,128)(2,1)S(1)}, u32[]{:S(2)}, u32[]{:S(2)}) collective-permute-start(bf16[160,768]{1,0:T(8,128)(2,1)S(1)} %collective-permute-done.refs_5_), channel_id=1, source_target_pairs={{0,16},{16,32},{32,48},{48,64},{64,80},{80,96},{96,112},{112,0},{1... | collective-permute-start | bytes 737288 | tf_op jit(solution)/shard_map/ppermute | solution.py:274
  20.3 12.0 %collective-permute-start.5 = (bf16[160,768]{1,0:T(8,128)(2,1)S(1)}, bf16[160,768]{1,0:T(8,128)(2,1)S(1)}, u32[]{:S(2)}, u32[]{:S(2)}) collective-permute-start(bf16[160,768]{1,0:T(8,128)(2,1)S(1)} %collective-permute-done.1.refs_7_), channel_id=1, source_target_pairs={{0,112},{16,0},{32,16},{48,32},{64,48},{80,64},{96,80},{112,96},{1... | collective-permute-start | bytes 737288 | tf_op jit(solution)/shard_map/ppermute | solution.py:274
  27.1 10.0 %collective-permute-start.10 = (bf16[160,768]{1,0:T(8,128)(2,1)S(1)}, bf16[160,768]{1,0:T(8,128)(2,1)S(1)}, u32[]{:S(2)}, u32[]{:S(2)}) collective-permute-start(bf16[160,768]{1,0:T(8,128)(2,1)S(1)} %collective-permute-done.6.refs_2_), channel_id=1, source_target_pairs={{0,16},{16,32},{32,48},{48,64},{64,80},{80,96},{96,112},{112,0},{1... | collective-permute-start | bytes 737288 | tf_op jit(solution)/shard_map/ppermute | solution.py:274
  27.1 10.5 %collective-permute-start.11 = (bf16[160,768]{1,0:T(8,128)(2,1)S(1)}, bf16[160,768]{1,0:T(8,128)(2,1)S(1)}, u32[]{:S(2)}, u32[]{:S(2)}) collective-permute-start(bf16[160,768]{1,0:T(8,128)(2,1)S(1)} %collective-permute-done.7.refs_4_), channel_id=1, source_target_pairs={{0,112},{16,0},{32,16},{48,32},{64,48},{80,64},{96,80},{112,96},{1... | collective-permute-start | bytes 737288 | tf_op jit(solution)/shard_map/ppermute | solution.py:274
  29.1 16.0 %collective-permute-start.16 = (bf16[384,768]{1,0:T(8,128)(2,1)S(1)}, bf16[384,768]{1,0:T(8,128)(2,1)S(1)}, u32[]{:S(2)}, u32[]{:S(2)}) collective-permute-start(bf16[384,768]{1,0:T(8,128)(2,1)S(1)} %constant_dynamic-slice_fusion), channel_id=1, source_target_pairs={{0,4},{4,0},{1,5},{5,1},{2,6},{6,2},{3,7},{7,3},{8,12},{12,8},{9,1... | collective-permute-start | bytes 1769480 | tf_op jit(solution)/shard_map/ppermute | solution.py:317
  32.3 9.2 %collective-permute-start.13 = (bf16[160,768]{1,0:T(8,128)(2,1)S(1)}, bf16[160,768]{1,0:T(8,128)(2,1)S(1)}, u32[]{:S(2)}, u32[]{:S(2)}) collective-permute-start(bf16[160,768]{1,0:T(8,128)(2,1)S(1)} %collective-permute-done.4.refs_3_), channel_id=1, source_target_pairs={{0,16},{16,32},{32,48},{48,64},{64,80},{80,96},{96,112},{112,0},{1... | collective-permute-start | bytes 737288 | tf_op jit(solution)/shard_map/ppermute | solution.py:274
  32.8 9.2 %collective-permute-start.14 = (bf16[160,768]{1,0:T(8,128)(2,1)S(1)}, bf16[160,768]{1,0:T(8,128)(2,1)S(1)}, u32[]{:S(2)}, u32[]{:S(2)}) collective-permute-start(bf16[160,768]{1,0:T(8,128)(2,1)S(1)} %collective-permute-done.5.refs_5_), channel_id=1, source_target_pairs={{0,112},{16,0},{32,16},{48,32},{64,48},{80,64},{96,80},{112,96},{1... | collective-permute-start | bytes 737288 | tf_op jit(solution)/shard_map/ppermute | solution.py:274
  37.6 7.5 %collective-permute-start.12 = (bf16[160,768]{1,0:T(8,128)(2,1)S(1)}, bf16[160,768]{1,0:T(8,128)(2,1)S(1)}, u32[]{:S(2)}, u32[]{:S(2)}) collective-permute-start(bf16[160,768]{1,0:T(8,128)(2,1)S(1)} %collective-permute-done.10.refs_2_), channel_id=1, source_target_pairs={{0,16},{16,32},{32,48},{48,64},{64,80},{80,96},{96,112},{112,0},{1... | collective-permute-start | bytes 737288 | tf_op jit(solution)/shard_map/ppermute | solution.py:274
  42.1 8.3 %collective-permute-start.15 = (bf16[160,768]{1,0:T(8,128)(2,1)S(1)}, bf16[160,768]{1,0:T(8,128)(2,1)S(1)}, u32[]{:S(2)}, u32[]{:S(2)}) collective-permute-start(bf16[160,768]{1,0:T(8,128)(2,1)S(1)} %collective-permute-done.14.refs_5_), channel_id=1, source_target_pairs={{0,112},{16,0},{32,16},{48,32},{64,48},{80,64},{96,80},{112,96},{1... | collective-permute-start | bytes 737288 | tf_op jit(solution)/shard_map/ppermute | solution.py:274
  51.8 2.1 %collective-permute-start.17 = (bf16[320,896]{1,0:T(8,128)(2,1)S(1)}, bf16[320,896]{1,0:T(8,128)(2,1)S(1)}, u32[]{:S(2)}, u32[]{:S(2)}) collective-permute-start(bf16[320,896]{1,0:T(8,128)(2,1)S(1)} %attend.9), channel_id=1, source_target_pairs={{0,8},{8,0},{1,9},{9,1},{2,10},{10,2},{3,11},{11,3},{4,12},{12,4},... | collective-permute-start | bytes 1720328 | tf_op jit(solution)/shard_map/ppermute | solution.py:332
  51.9 14.0 %collective-permute-start.20 = (bf16[384,768]{1,0:T(8,128)(2,1)S(1)}, bf16[384,768]{1,0:T(8,128)(2,1)}, u32[]{:S(2)}, u32[]{:S(2)}) collective-permute-start(bf16[384,768]{1,0:T(8,128)(2,1)S(1)} %collective-permute-done.16.w_mine_ref), channel_id=1, source_target_pairs={{0,8},{8,0},{1,9},{9,1},{2,10},{10,2},{3,11},{11,3},{4,12},{12,4},... | collective-permute-start | bytes 1769480 | tf_op jit(solution)/shard_map/ppermute | solution.py:345
  54.5 10.6 %collective-permute-start.18 = (bf16[160,896]{1,0:T(8,128)(2,1)S(1)}, bf16[160,896]{1,0:T(8,128)(2,1)S(1)}, u32[]{:S(2)}, u32[]{:S(2)}) collective-permute-start(bf16[160,896]{1,0:T(8,128)(2,1)S(1)} %join.3), channel_id=1, source_target_pairs={{0,128},{128,0},{1,129},{129,1},{2,130},{130,2},{3,131},{131,3},{4... | collective-permute-start | bytes 860168 | tf_op jit(solution)/shard_map/ppermute | solution.py:341
  65.6 7.4 %collective-permute-start.19 = (bf16[320,384]{1,0:T(8,128)(2,1)S(1)}, bf16[320,384]{1,0:T(8,128)(2,1)S(1)}, u32[]{:S(2)}, u32[]{:S(2)}) collective-permute-start(bf16[320,384]{1,0:T(8,128)(2,1)S(1)} %attended.1.own_ref), channel_id=1, source_target_pairs={{0,4},{4,0},{1,5},{5,1},{2,6},{6,2},{3,7},{7,3},{8,12},{12,8},{9,1... | collective-permute-start | bytes 737288 | tf_op jit(solution)/shard_map/ppermute | solution.py:344
  73.8 10.5 %collective-permute-start.21 = (bf16[320,384]{1,0:T(8,128)(2,1)S(1)}, bf16[320,384]{1,0:T(8,128)(2,1)S(1)}, u32[]{:S(2)}, u32[]{:S(2)}) collective-permute-start(bf16[320,384]{1,0:T(8,128)(2,1)S(1)} %get-tuple-element.107), channel_id=1, source_target_pairs={{0,2},{1,3},{2,0},{3,1},{4,6},{5,7},{6,4},{7,5},{8,10},{9,11},{10,... | collective-permute-start | bytes 737288 | tf_op jit(solution)/shard_map/ppermute | solution.py:357
  77.0 10.0 %collective-permute-start.22 = (bf16[320,384]{1,0:T(8,128)(2,1)S(1)}, bf16[320,384]{1,0:T(8,128)(2,1)S(1)}, u32[]{:S(2)}, u32[]{:S(2)}) collective-permute-start(bf16[320,384]{1,0:T(8,128)(2,1)S(1)} %get-tuple-element.108), channel_id=1, source_target_pairs={{0,1},{1,2},{2,3},{3,0},{4,5},{5,6},{6,7},{7,4},{8,9},{9,10},{10,1... | collective-permute-start | bytes 737288 | tf_op jit(solution)/shard_map/ppermute | solution.py:357
  77.7 9.6 %collective-permute-start.23 = (bf16[320,384]{1,0:T(8,128)(2,1)S(1)}, bf16[320,384]{1,0:T(8,128)(2,1)S(1)}, u32[]{:S(2)}, u32[]{:S(2)}) collective-permute-start(bf16[320,384]{1,0:T(8,128)(2,1)S(1)} %get-tuple-element.109), channel_id=1, source_target_pairs={{0,3},{1,0},{2,1},{3,2},{4,7},{5,4},{6,5},{7,6},{8,11},{9,8},{10,9... | collective-permute-start | bytes 737288 | tf_op jit(solution)/shard_map/ppermute | solution.py:357
  (1 other events, 12.1 us)

commit v5 on v4

--- a/solution.py
+++ b/solution.py
@@ -259,6 +259,10 @@
     )(where, own, w_out, w_mine, w_other)
 
 
+def early_kernel(a_ref, b_ref, out):
+    out[...] = a_ref[...].astype(jnp.float32) + b_ref[...].astype(jnp.float32)
+
+
 def total_kernel(*refs):
     parts, (value_ref, tangent_ref) = refs[:-2], refs[-2:]
     total = sum(part[...].astype(jnp.float32) for part in parts)
@@ -357,7 +361,8 @@
         lax.ppermute(part, "y", [(i, (i + step) % 4) for i in range(4)])
         for step, part in ((2, parts[2]), (1, parts[1]), (3, parts[3]))
     ]
-    return tuple(call(total_kernel, "total", [shape(rows, width)] * 2, parts))
+    early = call(early_kernel, "early", [shape(2 * rows, width, jnp.float32)], parts[:2])
+    return tuple(call(total_kernel, "total", [shape(rows, width)] * 2, list(early) + parts[2:]))
 
 
 def solution(mesh):

time: 88.3 us -> 88.3 us (level)
    pallas_call x10 -> x11, Pallas kernels: 14 us -> 14 us  [call(): pl.pallas_call(kernel, in_specs=[vmem()] * len(args), out_specs=[vmem()]...]
where the time goes in v5:
time: 88.3 us; the launch traced here: 88.1 us
  waiting for transfers between devices  38.8 us (44%)
  starting transfers between devices  29.2 us (33%)
  Pallas kernels  16 us (18%)
  other arithmetic  2.21 us (3%)
  local copies, waits for them, and re-layouts  1.11 us (1%)
    ppermute x14, starting transfers between devices, along_z(): return lax.ppermute(x, 'z', [(i, (i + step) % 8) for i in range(8)])  17.2 us
    ppermute x14, waiting for transfers between devices, along_z(): return lax.ppermute(x, 'z', [(i, (i + step) % 8) for i in range(8)])  17.1 us
    pallas_call x11, Pallas kernels, call(): pl.pallas_call(kernel, in_specs=[vmem()] * len(args), out_specs=[vmem()]...  14 us
    ppermute x1, waiting for transfers between devices, on_device(): from_far = lax.ppermute(join(rows), 'xh', SWAP)  8.08 us
    ppermute x3, waiting for transfers between devices, on_device(): lax.ppermute(part, 'y', [(i, (i + step) % 4) for i in range(4)])  7.01 us
    ppermute x3, starting transfers between devices, on_device(): lax.ppermute(part, 'y', [(i, (i + step) % 4) for i in range(4)])  6.52 us
    ppermute x1, waiting for transfers between devices, on_device(): beside_attended = lax.ppermute(attended, 'xl', SWAP)  5.15 us
    ppermute x1, starting transfers between devices, on_device(): far_q = lax.ppermute(own_q, 'xh', SWAP)  2.12 us
  transfers between devices with their start and end apart: 24, of which 14 were waited for; matrix products, arithmetic and copies ran while one was open for 2% of the time, Pallas kernels for 15%

profile of v5, /device:TPU:98, one launch (start us, length us, event | category | flops | bytes accessed | tf_op | source)
XLA Modules:
  0.0 88.1 jit_solution(11415348341078218512)
XLA Ops:
  1.8 3.2 %collective-permute-start.2 = (bf16[160,768]{1,0:T(8,128)(2,1)S(1)}, bf16[160,768]{1,0:T(8,128)(2,1)S(1)}, u32[]{:S(2)}, u32[]{:S(2)}) collective-permute-start(bf16[160,768]{1,0:T(8,128)(2,1)S(1)} %get-tuple-element.56.refs_2_), channel_id=1, source_target_pairs={{0,16},{16,32},{32,48},{48,64},{64,80},{80,96},{96,112},{112,0},{1... | collective-permute-start | bytes 737288 | tf_op jit(solution)/shard_map/ppermute | solution.py:278
  5.0 2.1 %collective-permute-start.8 = (bf16[160,768]{1,0:T(8,128)(2,1)S(1)}, bf16[160,768]{1,0:T(8,128)(2,1)S(1)}, u32[]{:S(2)}, u32[]{:S(2)}) collective-permute-start(bf16[160,768]{1,0:T(8,128)(2,1)S(1)} %get-tuple-element.61), channel_id=1, source_target_pairs={{0,128},{128,0},{1,129},{129,1},{2,130},{130,2},{3,131},{131,3},{4... | collective-permute-start | bytes 737288 | tf_op jit(solution)/shard_map/ppermute | solution.py:307
  8.1 3.3 %collective-permute-start = (bf16[160,768]{1,0:T(8,128)(2,1)S(1)}, bf16[160,768]{1,0:T(8,128)(2,1)S(1)}, u32[]{:S(2)}, u32[]{:S(2)}) collective-permute-start(bf16[160,768]{1,0:T(8,128)(2,1)S(1)} %pad_maximum_fusion.3.refs_3_), channel_id=1, source_target_pairs={{0,16},{16,32},{32,48},{48,64},{64,80},{80,96},{96,112},{112,0},{1... | collective-permute-start | bytes 737288 | tf_op jit(solution)/shard_map/ppermute | solution.py:278
  12.5 1.4 %collective-permute-done.8 = bf16[160,768]{1,0:T(8,128)(2,1)S(1)} collective-permute-done((bf16[160,768]{1,0:T(8,128)(2,1)S(1)}, bf16[160,768]{1,0:T(8,128)(2,1)S(1)}, u32[]{:S(2)}, u32[]{:S(2)}) %collective-permute-start.8) | collective-permute-done | bytes 245792 | tf_op jit(solution)/shard_map/ppermute | solution.py:307
  14.0 3.0 %collective-permute-start.6 = (bf16[160,768]{1,0:T(8,128)(2,1)S(1)}, bf16[160,768]{1,0:T(8,128)(2,1)S(1)}, u32[]{:S(2)}, u32[]{:S(2)}) collective-permute-start(bf16[160,768]{1,0:T(8,128)(2,1)S(1)} %collective-permute-done.2.refs_4_), channel_id=1, source_target_pairs={{0,16},{16,32},{32,48},{48,64},{64,80},{80,96},{96,112},{112,0},{1... | collective-permute-start | bytes 737288 | tf_op jit(solution)/shard_map/ppermute | solution.py:278
  17.1 2.1 %collective-permute-done.1.refs_7_ = bf16[160,768]{1,0:T(8,128)(2,1)S(1)} collective-permute-done((bf16[160,768]{1,0:T(8,128)(2,1)S(1)}, bf16[160,768]{1,0:T(8,128)(2,1)S(1)}, u32[]{:S(2)}, u32[]{:S(2)}) %collective-permute-start.1) | collective-permute-done | bytes 245792 | tf_op jit(solution)/shard_map/ppermute | solution.py:278
  21.2 2.1 %collective-permute-done.6.refs_2_ = bf16[160,768]{1,0:T(8,128)(2,1)S(1)} collective-permute-done((bf16[160,768]{1,0:T(8,128)(2,1)S(1)}, bf16[160,768]{1,0:T(8,128)(2,1)S(1)}, u32[]{:S(2)}, u32[]{:S(2)}) %collective-permute-start.6) | collective-permute-done | bytes 245792 | tf_op jit(solution)/shard_map/ppermute | solution.py:278
  23.3 3.7 %collective-permute-done.7.refs_4_ = bf16[160,768]{1,0:T(8,128)(2,1)S(1)} collective-permute-done((bf16[160,768]{1,0:T(8,128)(2,1)S(1)}, bf16[160,768]{1,0:T(8,128)(2,1)S(1)}, u32[]{:S(2)}, u32[]{:S(2)}) %collective-permute-start.7) | collective-permute-done | bytes 245792 | tf_op jit(solution)/shard_map/ppermute | solution.py:278
  27.1 2.0 %collective-permute-start.11 = (bf16[160,768]{1,0:T(8,128)(2,1)S(1)}, bf16[160,768]{1,0:T(8,128)(2,1)S(1)}, u32[]{:S(2)}, u32[]{:S(2)}) collective-permute-start(bf16[160,768]{1,0:T(8,128)(2,1)S(1)} %collective-permute-done.7.refs_4_), channel_id=1, source_target_pairs={{0,112},{16,0},{32,16},{48,32},{64,48},{80,64},{96,80},{112,96},{1... | collective-permute-start | bytes 737288 | tf_op jit(solution)/shard_map/ppermute | solution.py:278
  29.6 2.7 %collective-permute-done.5.refs_5_ = bf16[160,768]{1,0:T(8,128)(2,1)S(1)} collective-permute-done((bf16[160,768]{1,0:T(8,128)(2,1)S(1)}, bf16[160,768]{1,0:T(8,128)(2,1)S(1)}, u32[]{:S(2)}, u32[]{:S(2)}) %collective-permute-start.5) | collective-permute-done | bytes 245792 | tf_op jit(solution)/shard_map/ppermute | solution.py:278
  32.8 1.5 %collective-permute-start.14 = (bf16[160,768]{1,0:T(8,128)(2,1)S(1)}, bf16[160,768]{1,0:T(8,128)(2,1)S(1)}, u32[]{:S(2)}, u32[]{:S(2)}) collective-permute-start(bf16[160,768]{1,0:T(8,128)(2,1)S(1)} %collective-permute-done.5.refs_5_), channel_id=1, source_target_pairs={{0,112},{16,0},{32,16},{48,32},{64,48},{80,64},{96,80},{112,96},{1... | collective-permute-start | bytes 737288 | tf_op jit(solution)/shard_map/ppermute | solution.py:278
  34.4 2.7 %attend.5 = (f32[320,1920]{1,0:T(8,128)S(1)}, f32[320,1920]{1,0:T(8,128)S(1)}) custom-call(bf16[320,768]{1,0:T(8,128)(2,1)S(1)} %pad_maximum_fusion.refs_0_, bf16[320,768]{1,0:T(8,128)(2,1)S(1)} %collective-permute-done.9.refs_1_.refs_0_, bf16[160,768]{1,0:T(8,128)(2,1)S(1)} %get-tuple-element.56.refs_2_, bf16[160,768]{1,0:T(8,128)(2,1)S(1)} %pad_maximum_fusion.3.refs_3_, ...), custom_call_target="tpu_custom_call" | custom-call | flops 1887436800 | bytes 7372800 | tf_op jit(solution)/shard_map/attend/pallas_call | solution.py:27
  38.8 2.7 %attend.6 = (f32[320,1920]{1,0:T(8,128)S(1)}, f32[320,1920]{1,0:T(8,128)S(1)}) custom-call(bf16[320,768]{1,0:T(8,128)(2,1)S(1)} %pad_maximum_fusion.refs_0_, bf16[320,768]{1,0:T(8,128)(2,1)S(1)} %collective-permute-done.9.refs_1_.refs_0_, bf16[160,768]{1,0:T(8,128)(2,1)S(1)} %collective-permute-done.6.refs_2_, ...), custom_call_target="tpu_custom_call" | custom-call | flops 1258291200 | bytes 11796480 | tf_op jit(solution)/shard_map/attend/pallas_call | solution.py:27
  42.4 2.7 %attend.7 = (f32[320,1920]{1,0:T(8,128)S(1)}, f32[320,1920]{1,0:T(8,128)S(1)}) custom-call(bf16[320,768]{1,0:T(8,128)(2,1)S(1)} %pad_maximum_fusion.refs_0_, bf16[320,768]{1,0:T(8,128)(2,1)S(1)} %collective-permute-done.9.refs_1_.refs_0_, bf16[160,768]{1,0:T(8,128)(2,1)S(1)} %collective-permute-done.10.refs_2_, ...), custom_call_target="tpu_custom_call" | custom-call | flops 1258291200 | bytes 11796480 | tf_op jit(solution)/shard_map/attend/pallas_call | solution.py:27
  45.1 5.3 %collective-permute-done.15.refs_2_ = bf16[160,768]{1,0:T(8,128)(2,1)S(1)} collective-permute-done((bf16[160,768]{1,0:T(8,128)(2,1)S(1)}, bf16[160,768]{1,0:T(8,128)(2,1)S(1)}, u32[]{:S(2)}, u32[]{:S(2)}) %collective-permute-start.15) | collective-permute-done | bytes 245792 | tf_op jit(solution)/shard_map/ppermute | solution.py:278
  50.4 1.4 %attend.9 = bf16[320,896]{1,0:T(8,128)(2,1)S(1)} custom-call(bf16[320,768]{1,0:T(8,128)(2,1)S(1)} %collective-permute-done.9.refs_1_.refs_0_, bf16[160,768]{1,0:T(8,128)(2,1)S(1)} %collective-permute-done.12.refs_1_, bf16[160,768]{1,0:T(8,128)(2,1)S(1)} %collective-permute-done.15.refs_2_, f32[320,1920]{1,0:T(8,128)S(1)} %get-tuple-element.96.refs_3_), custom_call_target="tpu_custom_call" | custom-call | flops 314572800 | bytes 4014080 | tf_op jit(solution)/shard_map/attend/pallas_call | solution.py:27
  54.5 1.9 %collective-permute-start.18 = (bf16[160,896]{1,0:T(8,128)(2,1)S(1)}, bf16[160,896]{1,0:T(8,128)(2,1)S(1)}, u32[]{:S(2)}, u32[]{:S(2)}) collective-permute-start(bf16[160,896]{1,0:T(8,128)(2,1)S(1)} %join.3), channel_id=1, source_target_pairs={{0,128},{128,0},{1,129},{129,1},{2,130},{130,2},{3,131},{131,3},{4... | collective-permute-start | bytes 860168 | tf_op jit(solution)/shard_map/ppermute | solution.py:345
  57.0 8.1 %collective-permute-done.18.b_ref = bf16[160,896]{1,0:T(8,128)(2,1)S(1)} collective-permute-done((bf16[160,896]{1,0:T(8,128)(2,1)S(1)}, bf16[160,896]{1,0:T(8,128)(2,1)S(1)}, u32[]{:S(2)}, u32[]{:S(2)}) %collective-permute-start.18) | collective-permute-done | bytes 286752 | tf_op jit(solution)/shard_map/ppermute | solution.py:345
  65.9 2.0 %project_own.1 = (f32[320,384]{1,0:T(8,128)S(1)}, f32[320,384]{1,0:T(8,128)S(1)}, f32[320,384]{1,0:T(8,128)S(1)}, f32[320,384]{1,0:T(8,128)S(1)}, bf16[384,384]{...) custom-call(s32[3]{0:T(128)S(1)} %pad_add_fusion.at_ref, ...), custom_call_target="tpu_custom_call" | custom-call | flops 377487360 | bytes 1966080 | tf_op jit(solution)/shard_map/project_own/pallas_call | solution.py:247
  67.8 5.2 %collective-permute-done.19.beside_ref = bf16[320,384]{1,0:T(8,128)(2,1)S(1)} collective-permute-done((bf16[320,384]{1,0:T(8,128)(2,1)S(1)}, bf16[320,384]{1,0:T(8,128)(2,1)S(1)}, u32[]{:S(2)}, u32[]{:S(2)}) %collective-permute-start.19) | collective-permute-done | bytes 245792 | tf_op jit(solution)/shard_map/ppermute | solution.py:348
  73.8 3.3 %collective-permute-start.21 = (bf16[320,384]{1,0:T(8,128)(2,1)S(1)}, bf16[320,384]{1,0:T(8,128)(2,1)S(1)}, u32[]{:S(2)}, u32[]{:S(2)}) collective-permute-start(bf16[320,384]{1,0:T(8,128)(2,1)S(1)} %get-tuple-element.107), channel_id=1, source_target_pairs={{0,2},{1,3},{2,0},{3,1},{4,6},{5,7},{6,4},{7,5},{8,10},{9,11},{10,... | collective-permute-start | bytes 737288 | tf_op jit(solution)/shard_map/ppermute | solution.py:361
  77.7 2.6 %collective-permute-start.23 = (bf16[320,384]{1,0:T(8,128)(2,1)S(1)}, bf16[320,384]{1,0:T(8,128)(2,1)S(1)}, u32[]{:S(2)}, u32[]{:S(2)}) collective-permute-start(bf16[320,384]{1,0:T(8,128)(2,1)S(1)} %get-tuple-element.109), channel_id=1, source_target_pairs={{0,3},{1,0},{2,1},{3,2},{4,7},{5,4},{6,5},{7,6},{8,11},{9,8},{10,9... | collective-permute-start | bytes 737288 | tf_op jit(solution)/shard_map/ppermute | solution.py:361
  80.3 4.0 %collective-permute-done.21.b_ref = bf16[320,384]{1,0:T(8,128)(2,1)S(1)} collective-permute-done((bf16[320,384]{1,0:T(8,128)(2,1)S(1)}, bf16[320,384]{1,0:T(8,128)(2,1)S(1)}, u32[]{:S(2)}, u32[]{:S(2)}) %collective-permute-start.21) | collective-permute-done | bytes 245792 | tf_op jit(solution)/shard_map/ppermute | solution.py:361
  84.3 2.7 %collective-permute-done.22.refs_1_ = bf16[320,384]{1,0:T(8,128)(2,1)S(1)} collective-permute-done((bf16[320,384]{1,0:T(8,128)(2,1)S(1)}, bf16[320,384]{1,0:T(8,128)(2,1)S(1)}, u32[]{:S(2)}, u32[]{:S(2)}) %collective-permute-start.22) | collective-permute-done | bytes 245792 | tf_op jit(solution)/shard_map/ppermute | solution.py:361
  (43 shorter events, 15.7 us)
Async XLA Ops:
  1.8 12.3 %collective-permute-start.2 = (bf16[160,768]{1,0:T(8,128)(2,1)S(1)}, bf16[160,768]{1,0:T(8,128)(2,1)S(1)}, u32[]{:S(2)}, u32[]{:S(2)}) collective-permute-start(bf16[160,768]{1,0:T(8,128)(2,1)S(1)} %get-tuple-element.56.refs_2_), channel_id=1, source_target_pairs={{0,16},{16,32},{32,48},{48,64},{64,80},{80,96},{96,112},{112,0},{1... | collective-permute-start | bytes 737288 | tf_op jit(solution)/shard_map/ppermute | solution.py:278
  5.0 12.1 %collective-permute-start.3 = (bf16[160,768]{1,0:T(8,128)(2,1)S(1)}, bf16[160,768]{1,0:T(8,128)(2,1)S(1)}, u32[]{:S(2)}, u32[]{:S(2)}) collective-permute-start(bf16[160,768]{1,0:T(8,128)(2,1)S(1)} %get-tuple-element.56.refs_2_), channel_id=1, source_target_pairs={{0,112},{16,0},{32,16},{48,32},{64,48},{80,64},{96,80},{112,96},{1... | collective-permute-start | bytes 737288 | tf_op jit(solution)/shard_map/ppermute | solution.py:278
  5.0 8.9 %collective-permute-start.8 = (bf16[160,768]{1,0:T(8,128)(2,1)S(1)}, bf16[160,768]{1,0:T(8,128)(2,1)S(1)}, u32[]{:S(2)}, u32[]{:S(2)}) collective-permute-start(bf16[160,768]{1,0:T(8,128)(2,1)S(1)} %get-tuple-element.61), channel_id=1, source_target_pairs={{0,128},{128,0},{1,129},{129,1},{2,130},{130,2},{3,131},{131,3},{4... | collective-permute-start | bytes 737288 | tf_op jit(solution)/shard_map/ppermute | solution.py:307
  8.1 9.0 %collective-permute-start = (bf16[160,768]{1,0:T(8,128)(2,1)S(1)}, bf16[160,768]{1,0:T(8,128)(2,1)S(1)}, u32[]{:S(2)}, u32[]{:S(2)}) collective-permute-start(bf16[160,768]{1,0:T(8,128)(2,1)S(1)} %pad_maximum_fusion.3.refs_3_), channel_id=1, source_target_pairs={{0,16},{16,32},{32,48},{48,64},{64,80},{80,96},{96,112},{112,0},{1... | collective-permute-start | bytes 737288 | tf_op jit(solution)/shard_map/ppermute | solution.py:278
  11.4 7.8 %collective-permute-start.1 = (bf16[160,768]{1,0:T(8,128)(2,1)S(1)}, bf16[160,768]{1,0:T(8,128)(2,1)S(1)}, u32[]{:S(2)}, u32[]{:S(2)}) collective-permute-start(bf16[160,768]{1,0:T(8,128)(2,1)S(1)} %pad_maximum_fusion.3.refs_3_), channel_id=1, source_target_pairs={{0,112},{16,0},{32,16},{48,32},{64,48},{80,64},{96,80},{112,96},{1... | collective-permute-start | bytes 737288 | tf_op jit(solution)/shard_map/ppermute | solution.py:278
  13.9 18.4 %collective-permute-start.9 = (bf16[320,768]{1,0:T(8,128)(2,1)S(1)}, bf16[320,768]{1,0:T(8,128)(2,1)S(1)}, u32[]{:S(2)}, u32[]{:S(2)}) collective-permute-start(bf16[320,768]{1,0:T(8,128)(2,1)S(1)} %pad_maximum_fusion.refs_0_), channel_id=1, source_target_pairs={{0,8},{8,0},{1,9},{9,1},{2,10},{10,2},{3,11},{11,3},{4,12},{12,4},... | collective-permute-start | bytes 1474568 | tf_op jit(solution)/shard_map/ppermute | solution.py:310
  14.0 9.3 %collective-permute-start.6 = (bf16[160,768]{1,0:T(8,128)(2,1)S(1)}, bf16[160,768]{1,0:T(8,128)(2,1)S(1)}, u32[]{:S(2)}, u32[]{:S(2)}) collective-permute-start(bf16[160,768]{1,0:T(8,128)(2,1)S(1)} %collective-permute-done.2.refs_4_), channel_id=1, source_target_pairs={{0,16},{16,32},{32,48},{48,64},{64,80},{80,96},{96,112},{112,0},{1... | collective-permute-start | bytes 737288 | tf_op jit(solution)/shard_map/ppermute | solution.py:278
  17.1 10.0 %collective-permute-start.7 = (bf16[160,768]{1,0:T(8,128)(2,1)S(1)}, bf16[160,768]{1,0:T(8,128)(2,1)S(1)}, u32[]{:S(2)}, u32[]{:S(2)}) collective-permute-start(bf16[160,768]{1,0:T(8,128)(2,1)S(1)} %collective-permute-done.3.refs_6_), channel_id=1, source_target_pairs={{0,112},{16,0},{32,16},{48,32},{64,48},{80,64},{96,80},{112,96},{1... | collective-permute-start | bytes 737288 | tf_op jit(solution)/shard_map/ppermute | solution.py:278
  19.2 9.9 %collective-permute-start.4 = (bf16[160,768]{1,0:T(8,128)(2,1)S(1)}, bf16[160,768]{1,0:T(8,128)(2,1)S(1)}, u32[]{:S(2)}, u32[]{:S(2)}) collective-permute-start(bf16[160,768]{1,0:T(8,128)(2,1)S(1)} %collective-permute-done.refs_5_), channel_id=1, source_target_pairs={{0,16},{16,32},{32,48},{48,64},{64,80},{80,96},{96,112},{112,0},{1... | collective-permute-start | bytes 737288 | tf_op jit(solution)/shard_map/ppermute | solution.py:278
  20.3 12.0 %collective-permute-start.5 = (bf16[160,768]{1,0:T(8,128)(2,1)S(1)}, bf16[160,768]{1,0:T(8,128)(2,1)S(1)}, u32[]{:S(2)}, u32[]{:S(2)}) collective-permute-start(bf16[160,768]{1,0:T(8,128)(2,1)S(1)} %collective-permute-done.1.refs_7_), channel_id=1, source_target_pairs={{0,112},{16,0},{32,16},{48,32},{64,48},{80,64},{96,80},{112,96},{1... | collective-permute-start | bytes 737288 | tf_op jit(solution)/shard_map/ppermute | solution.py:278
  27.1 10.0 %collective-permute-start.10 = (bf16[160,768]{1,0:T(8,128)(2,1)S(1)}, bf16[160,768]{1,0:T(8,128)(2,1)S(1)}, u32[]{:S(2)}, u32[]{:S(2)}) collective-permute-start(bf16[160,768]{1,0:T(8,128)(2,1)S(1)} %collective-permute-done.6.refs_2_), channel_id=1, source_target_pairs={{0,16},{16,32},{32,48},{48,64},{64,80},{80,96},{96,112},{112,0},{1... | collective-permute-start | bytes 737288 | tf_op jit(solution)/shard_map/ppermute | solution.py:278
  27.1 10.5 %collective-permute-start.11 = (bf16[160,768]{1,0:T(8,128)(2,1)S(1)}, bf16[160,768]{1,0:T(8,128)(2,1)S(1)}, u32[]{:S(2)}, u32[]{:S(2)}) collective-permute-start(bf16[160,768]{1,0:T(8,128)(2,1)S(1)} %collective-permute-done.7.refs_4_), channel_id=1, source_target_pairs={{0,112},{16,0},{32,16},{48,32},{64,48},{80,64},{96,80},{112,96},{1... | collective-permute-start | bytes 737288 | tf_op jit(solution)/shard_map/ppermute | solution.py:278
  29.1 16.0 %collective-permute-start.16 = (bf16[384,768]{1,0:T(8,128)(2,1)S(1)}, bf16[384,768]{1,0:T(8,128)(2,1)S(1)}, u32[]{:S(2)}, u32[]{:S(2)}) collective-permute-start(bf16[384,768]{1,0:T(8,128)(2,1)S(1)} %constant_dynamic-slice_fusion), channel_id=1, source_target_pairs={{0,4},{4,0},{1,5},{5,1},{2,6},{6,2},{3,7},{7,3},{8,12},{12,8},{9,1... | collective-permute-start | bytes 1769480 | tf_op jit(solution)/shard_map/ppermute | solution.py:321
  32.3 9.2 %collective-permute-start.13 = (bf16[160,768]{1,0:T(8,128)(2,1)S(1)}, bf16[160,768]{1,0:T(8,128)(2,1)S(1)}, u32[]{:S(2)}, u32[]{:S(2)}) collective-permute-start(bf16[160,768]{1,0:T(8,128)(2,1)S(1)} %collective-permute-done.4.refs_3_), channel_id=1, source_target_pairs={{0,16},{16,32},{32,48},{48,64},{64,80},{80,96},{96,112},{112,0},{1... | collective-permute-start | bytes 737288 | tf_op jit(solution)/shard_map/ppermute | solution.py:278
  32.8 9.2 %collective-permute-start.14 = (bf16[160,768]{1,0:T(8,128)(2,1)S(1)}, bf16[160,768]{1,0:T(8,128)(2,1)S(1)}, u32[]{:S(2)}, u32[]{:S(2)}) collective-permute-start(bf16[160,768]{1,0:T(8,128)(2,1)S(1)} %collective-permute-done.5.refs_5_), channel_id=1, source_target_pairs={{0,112},{16,0},{32,16},{48,32},{64,48},{80,64},{96,80},{112,96},{1... | collective-permute-start | bytes 737288 | tf_op jit(solution)/shard_map/ppermute | solution.py:278
  37.6 7.5 %collective-permute-start.12 = (bf16[160,768]{1,0:T(8,128)(2,1)S(1)}, bf16[160,768]{1,0:T(8,128)(2,1)S(1)}, u32[]{:S(2)}, u32[]{:S(2)}) collective-permute-start(bf16[160,768]{1,0:T(8,128)(2,1)S(1)} %collective-permute-done.10.refs_2_), channel_id=1, source_target_pairs={{0,16},{16,32},{32,48},{48,64},{64,80},{80,96},{96,112},{112,0},{1... | collective-permute-start | bytes 737288 | tf_op jit(solution)/shard_map/ppermute | solution.py:278
  42.1 8.3 %collective-permute-start.15 = (bf16[160,768]{1,0:T(8,128)(2,1)S(1)}, bf16[160,768]{1,0:T(8,128)(2,1)S(1)}, u32[]{:S(2)}, u32[]{:S(2)}) collective-permute-start(bf16[160,768]{1,0:T(8,128)(2,1)S(1)} %collective-permute-done.14.refs_5_), channel_id=1, source_target_pairs={{0,112},{16,0},{32,16},{48,32},{64,48},{80,64},{96,80},{112,96},{1... | collective-permute-start | bytes 737288 | tf_op jit(solution)/shard_map/ppermute | solution.py:278
  51.8 2.1 %collective-permute-start.17 = (bf16[320,896]{1,0:T(8,128)(2,1)S(1)}, bf16[320,896]{1,0:T(8,128)(2,1)S(1)}, u32[]{:S(2)}, u32[]{:S(2)}) collective-permute-start(bf16[320,896]{1,0:T(8,128)(2,1)S(1)} %attend.9), channel_id=1, source_target_pairs={{0,8},{8,0},{1,9},{9,1},{2,10},{10,2},{3,11},{11,3},{4,12},{12,4},... | collective-permute-start | bytes 1720328 | tf_op jit(solution)/shard_map/ppermute | solution.py:336
  51.9 14.0 %collective-permute-start.20 = (bf16[384,768]{1,0:T(8,128)(2,1)S(1)}, bf16[384,768]{1,0:T(8,128)(2,1)}, u32[]{:S(2)}, u32[]{:S(2)}) collective-permute-start(bf16[384,768]{1,0:T(8,128)(2,1)S(1)} %collective-permute-done.16.w_mine_ref), channel_id=1, source_target_pairs={{0,8},{8,0},{1,9},{9,1},{2,10},{10,2},{3,11},{11,3},{4,12},{12,4},... | collective-permute-start | bytes 1769480 | tf_op jit(solution)/shard_map/ppermute | solution.py:349
  54.5 10.6 %collective-permute-start.18 = (bf16[160,896]{1,0:T(8,128)(2,1)S(1)}, bf16[160,896]{1,0:T(8,128)(2,1)S(1)}, u32[]{:S(2)}, u32[]{:S(2)}) collective-permute-start(bf16[160,896]{1,0:T(8,128)(2,1)S(1)} %join.3), channel_id=1, source_target_pairs={{0,128},{128,0},{1,129},{129,1},{2,130},{130,2},{3,131},{131,3},{4... | collective-permute-start | bytes 860168 | tf_op jit(solution)/shard_map/ppermute | solution.py:345
  65.6 7.4 %collective-permute-start.19 = (bf16[320,384]{1,0:T(8,128)(2,1)S(1)}, bf16[320,384]{1,0:T(8,128)(2,1)S(1)}, u32[]{:S(2)}, u32[]{:S(2)}) collective-permute-start(bf16[320,384]{1,0:T(8,128)(2,1)S(1)} %attended.1.own_ref), channel_id=1, source_target_pairs={{0,4},{4,0},{1,5},{5,1},{2,6},{6,2},{3,7},{7,3},{8,12},{12,8},{9,1... | collective-permute-start | bytes 737288 | tf_op jit(solution)/shard_map/ppermute | solution.py:348
  73.8 10.5 %collective-permute-start.21 = (bf16[320,384]{1,0:T(8,128)(2,1)S(1)}, bf16[320,384]{1,0:T(8,128)(2,1)S(1)}, u32[]{:S(2)}, u32[]{:S(2)}) collective-permute-start(bf16[320,384]{1,0:T(8,128)(2,1)S(1)} %get-tuple-element.107), channel_id=1, source_target_pairs={{0,2},{1,3},{2,0},{3,1},{4,6},{5,7},{6,4},{7,5},{8,10},{9,11},{10,... | collective-permute-start | bytes 737288 | tf_op jit(solution)/shard_map/ppermute | solution.py:361
  77.0 10.0 %collective-permute-start.22 = (bf16[320,384]{1,0:T(8,128)(2,1)S(1)}, bf16[320,384]{1,0:T(8,128)(2,1)S(1)}, u32[]{:S(2)}, u32[]{:S(2)}) collective-permute-start(bf16[320,384]{1,0:T(8,128)(2,1)S(1)} %get-tuple-element.108), channel_id=1, source_target_pairs={{0,1},{1,2},{2,3},{3,0},{4,5},{5,6},{6,7},{7,4},{8,9},{9,10},{10,1... | collective-permute-start | bytes 737288 | tf_op jit(solution)/shard_map/ppermute | solution.py:361
  77.7 9.6 %collective-permute-start.23 = (bf16[320,384]{1,0:T(8,128)(2,1)S(1)}, bf16[320,384]{1,0:T(8,128)(2,1)S(1)}, u32[]{:S(2)}, u32[]{:S(2)}) collective-permute-start(bf16[320,384]{1,0:T(8,128)(2,1)S(1)} %get-tuple-element.109), channel_id=1, source_target_pairs={{0,3},{1,0},{2,1},{3,2},{4,7},{5,4},{6,5},{7,6},{8,11},{9,8},{10,9... | collective-permute-start | bytes 737288 | tf_op jit(solution)/shard_map/ppermute | solution.py:361
  (1 other events, 12.1 us)
